TPU v7x, 128 devices: a whole 4x4x4 slice. The times are simulated.
128 devices in a mesh: row: 8 (over x, z_lo), col: 16 (over y, z_hi, core).
Axes of the slice: x: 4, y: 4, z: 4 (z_hi: 2, z_lo: 2; z = z_hi * 2 + z_lo), core: 2. Of those that a mesh axis runs over, the one named last changes fastest.
Arguments:
- attributes: bfloat16 [65536, 128], P(('row', 'col')), may hold values from -6 to 6
- adj_values: bfloat16 [8, 16, 384, 128, 128], P('row', 'col'), may hold values from 0 to 3, as said below
- adj_rows: int32 [8, 16, 384], P('row', 'col'), may hold values from 0 to 63
- adj_cols: int32 [8, 16, 384], P('row', 'col'), may hold values from 0 to 31
- adj_count: int32 [8, 16], P('row', 'col'), may hold values from 1 to 384, as said below
- pair_ids: int32 [512, 4], P(('row', 'col')), may hold values from 0 to 31
- struct_target: bfloat16 [65536, 4, 128], P(('row', 'col')), may hold values from 0 to 1
- w_first: bfloat16 [128, 512], replicated, may hold values from -0.5 to 0.5
- w_rest: bfloat16 [1, 256, 512], replicated, may hold values from -0.375 to 0.375
- layer_bias: float32 [1, 256], replicated, may hold values from -3 to 3
- w_attr: bfloat16 [256, 128], replicated, may hold values from -0.375 to 0.375
- attr_bias: float32 [128], replicated, may hold values from -3 to 3
Outputs:
- anomaly: float32 [65536], P(('row', 'col'))
Inputs may be any that keep to these rules, and one draw needn't show every extreme that they name: `adj_count`: every tile has at least one live slot, and some tile has all 384 live in every draw. `adj_values`: nonnegative entries; slots at or past a tile's count are ignored.
All inputs are finite; a program needn't handle non-finite values.
Results may differ from a plain program's by a relative error of at most 0.00075.
Values may be sent and summed in bfloat16 or wider, within the bound.
No kernel may reach another device: no remote copies, remote signals or barrier semaphores. Data moves between devices by JAX's collectives and lax.ppermute only.
A program may use at most 128 MiB of HBM per device.

v0:
```python
import math

import jax
import jax.numpy as jnp
from jax import lax
from jax.sharding import PartitionSpec as P

epsilon = 1e-06
mix_alpha = 0.8


def run_blocks(partial_sum, panel_blocks, block_vals, row_ids, col_ids, low_slot, high_slot):
    capacity = block_vals.shape[0]
    group_size = math.gcd(capacity, 32)

    def add_group(group_index, carried):
        start = group_index * group_size
        vals_now = lax.dynamic_slice_in_dim(block_vals, start, group_size, 0)
        rows_now = lax.dynamic_slice_in_dim(row_ids, start, group_size, 0)
        cols_now = lax.dynamic_slice_in_dim(col_ids, start, group_size, 0)
        slot_ids = start + jnp.arange(group_size, dtype=jnp.int32)
        live_mask = ((slot_ids >= low_slot) & (slot_ids < high_slot)).astype(jnp.float32)
        picked = jnp.take(panel_blocks, cols_now, axis=0)
        products = jnp.einsum("gij,gjf->gif", vals_now, picked, preferred_element_type=jnp.float32)
        return carried.at[rows_now].add(products * live_mask[:, None, None])

    first_group = low_slot // group_size
    last_group = (high_slot + group_size - 1) // group_size
    return lax.fori_loop(first_group, last_group, add_group, partial_sum)


def column_panel(features):
    gathered = lax.all_gather(features, "row", axis=0, tiled=True)
    return gathered


def per_device(
    attributes,
    adj_values,
    adj_rows,
    adj_cols,
    adj_count,
    pair_ids,
    struct_target,
    w_first,
    w_rest,
    layer_bias,
    w_attr,
    attr_bias,
):
    block_vals = adj_values[0, 0]
    row_ids = adj_rows[0, 0]
    col_ids = adj_cols[0, 0]
    live_count = adj_count[0, 0]
    capacity = block_vals.shape[0]
    block_size = block_vals.shape[1]
    nodes_dev = attributes.shape[0]
    hidden_size = w_rest.shape[1]
    pair_count = pair_ids.shape[1]
    row_blocks = lax.axis_size("col") * nodes_dev // block_size
    slot_ids = jnp.arange(capacity, dtype=jnp.int32)
    live_mask = (slot_ids < live_count).astype(jnp.float32)
    row_mass = jnp.sum(block_vals, axis=2, dtype=jnp.float32) * live_mask[:, None]
    degree_terms = jnp.zeros((row_blocks, block_size), jnp.float32).at[row_ids].add(row_mass)
    degree = 1.0 + lax.psum_scatter(
        degree_terms.reshape(-1).astype(jnp.bfloat16), "col", scatter_dimension=0, tiled=True
    ).astype(jnp.float32)
    row_scale = lax.rsqrt(degree)[:, None]
    hidden_state = attributes
    for layer_index in range(w_rest.shape[0] + 1):
        weight = w_first if layer_index == 0 else w_rest[layer_index - 1]
        projected = jnp.dot(hidden_state, weight, preferred_element_type=jnp.float32)
        features = projected[:, :hidden_size].astype(jnp.bfloat16)
        panel_rows = column_panel(features)
        panel_blocks = panel_rows.reshape(-1, block_size, hidden_size)
        partial_sum = jnp.zeros((row_blocks, block_size, hidden_size), jnp.float32)
        partial_sum = run_blocks(
            partial_sum, panel_blocks, block_vals, row_ids, col_ids, jnp.int32(0), live_count
        )
        flattened = partial_sum.reshape(-1, hidden_size)
        summed = lax.psum_scatter(
            flattened.astype(jnp.bfloat16), "col", scatter_dimension=0, tiled=True
        ).astype(jnp.float32)
        before = row_scale * summed + projected[:, hidden_size:]
        if layer_index > 0:
            before = before + layer_bias[layer_index - 1]
        hidden_state = jnp.tanh(before).astype(jnp.bfloat16)
    rebuilt = jnp.dot(hidden_state, w_attr, preferred_element_type=jnp.float32) + attr_bias
    attr_error = jnp.sqrt(
        jnp.mean((rebuilt - attributes.astype(jnp.float32)) ** 2, axis=1) + epsilon
    )
    group_blocks = column_panel(hidden_state).reshape(-1, block_size, hidden_size)
    own_blocks = hidden_state.reshape(-1, block_size, hidden_size)
    partners = jnp.take(group_blocks, pair_ids, axis=0)
    logits = jnp.einsum(
        "bif,bpjf->bipj", own_blocks, partners, preferred_element_type=jnp.float32
    ) * hidden_size ** (-0.5)
    probability = jax.nn.sigmoid(logits).reshape(nodes_dev, pair_count, block_size)
    struct_error = jnp.sqrt(
        jnp.mean((probability - struct_target.astype(jnp.float32)) ** 2, axis=(1, 2)) + epsilon
    )
    return mix_alpha * attr_error + (1.0 - mix_alpha) * struct_error


def solution(mesh):
    return jax.shard_map(
        per_device,
        mesh=mesh,
        in_specs=(
            P(("row", "col"), None),
            P("row", "col", None, None, None),
            P("row", "col", None),
            P("row", "col", None),
            P("row", "col"),
            P(("row", "col"), None),
            P(("row", "col"), None, None),
            P(),
            P(),
            P(),
            P(),
            P(),
        ),
        out_specs=P(("row", "col")),
        check_vma=False,
    )
```

profile of v0, /device:TPU:0, one launch (start us, length us, event | category | flops | bytes accessed | tf_op | source)
XLA Modules:
  0.0 770.7 jit_solution(15295695291408610806)
XLA Ops:
  10.7 52.0 %all-gather.4.cloned.1.call-done = bf16[4096,256]{1,0:T(8,128)(2,1)} async-done(((bf16[512,256]{1,0:T(8,128)(2,1)}), bf16[4096,256]{1,0:T(8,128)(2,1)}) %all-gather.4.cloned.1.call-update) | async-done | bytes 2097168 | tf_op jit(solution)/shard_map/all_gather | solution.py:33
  67.0 204.9 %while.20 = (s32[]{:T(128)}, f32[64,128,256]{2,1,0:T(8,128)}, s32[]{:T(128)}, s32[384]{0:T(512)S(1)}, bf16[384,128,128]{2,1,0:T(8,128)(2,1)}, /*index=5*/s32[384...) while((s32[]{:T(128)}, f32[64,128,256]{2,1,0:T(8,128)}, ...), condition=%wide.region_5.7_spmd, body=%wide.region_3.6_spmd.sunk | while | flops 271582656 | bytes 24122744 | solution.py:29
  74.1 10.0 %scatter_fusion = f32[64,128,256]{2,1,0:T(8,128)} fusion(f32[64,128,256]{2,1,0:T(8,128)} %get-tuple-element.257, s32[32]{0:T(128)S(1)} %compare_select_fusion.10, f32[32,128,256]{2,1,0:T(8,128)} %convolution_multiply_fusion.5), kind=kCustom, calls=%fused_computation.3.clone.1 | custom fusion | flops 1048576 | bytes 12583040 | tf_op jit(solution)/shard_map/while/body/scatter-add | solution.py:25
  91.1 10.0 %scatter_fusion = f32[64,128,256]{2,1,0:T(8,128)} fusion(f32[64,128,256]{2,1,0:T(8,128)} %get-tuple-element.257, s32[32]{0:T(128)S(1)} %compare_select_fusion.10, f32[32,128,256]{2,1,0:T(8,128)} %convolution_multiply_fusion.5), kind=kCustom, calls=%fused_computation.3.clone.1 | custom fusion | flops 1048576 | bytes 12583040 | tf_op jit(solution)/shard_map/while/body/scatter-add | solution.py:25
  125.2 10.0 %scatter_fusion = f32[64,128,256]{2,1,0:T(8,128)} fusion(f32[64,128,256]{2,1,0:T(8,128)} %get-tuple-element.257, s32[32]{0:T(128)S(1)} %compare_select_fusion.10, f32[32,128,256]{2,1,0:T(8,128)} %convolution_multiply_fusion.5), kind=kCustom, calls=%fused_computation.3.clone.1 | custom fusion | flops 1048576 | bytes 12583040 | tf_op jit(solution)/shard_map/while/body/scatter-add | solution.py:25
  142.2 10.1 %scatter_fusion = f32[64,128,256]{2,1,0:T(8,128)} fusion(f32[64,128,256]{2,1,0:T(8,128)} %get-tuple-element.257, s32[32]{0:T(128)S(1)} %compare_select_fusion.10, f32[32,128,256]{2,1,0:T(8,128)} %convolution_multiply_fusion.5), kind=kCustom, calls=%fused_computation.3.clone.1 | custom fusion | flops 1048576 | bytes 12583040 | tf_op jit(solution)/shard_map/while/body/scatter-add | solution.py:25
  159.4 10.0 %scatter_fusion = f32[64,128,256]{2,1,0:T(8,128)} fusion(f32[64,128,256]{2,1,0:T(8,128)} %get-tuple-element.257, s32[32]{0:T(128)S(1)} %compare_select_fusion.10, f32[32,128,256]{2,1,0:T(8,128)} %convolution_multiply_fusion.5), kind=kCustom, calls=%fused_computation.3.clone.1 | custom fusion | flops 1048576 | bytes 12583040 | tf_op jit(solution)/shard_map/while/body/scatter-add | solution.py:25
  176.5 10.0 %scatter_fusion = f32[64,128,256]{2,1,0:T(8,128)} fusion(f32[64,128,256]{2,1,0:T(8,128)} %get-tuple-element.257, s32[32]{0:T(128)S(1)} %compare_select_fusion.10, f32[32,128,256]{2,1,0:T(8,128)} %convolution_multiply_fusion.5), kind=kCustom, calls=%fused_computation.3.clone.1 | custom fusion | flops 1048576 | bytes 12583040 | tf_op jit(solution)/shard_map/while/body/scatter-add | solution.py:25
  227.4 10.1 %scatter_fusion = f32[64,128,256]{2,1,0:T(8,128)} fusion(f32[64,128,256]{2,1,0:T(8,128)} %get-tuple-element.257, s32[32]{0:T(128)S(1)} %compare_select_fusion.10, f32[32,128,256]{2,1,0:T(8,128)} %convolution_multiply_fusion.5), kind=kCustom, calls=%fused_computation.3.clone.1 | custom fusion | flops 1048576 | bytes 12583040 | tf_op jit(solution)/shard_map/while/body/scatter-add | solution.py:25
  244.7 10.1 %scatter_fusion = f32[64,128,256]{2,1,0:T(8,128)} fusion(f32[64,128,256]{2,1,0:T(8,128)} %get-tuple-element.257, s32[32]{0:T(128)S(1)} %compare_select_fusion.10, f32[32,128,256]{2,1,0:T(8,128)} %convolution_multiply_fusion.5), kind=kCustom, calls=%fused_computation.3.clone.1 | custom fusion | flops 1048576 | bytes 12583040 | tf_op jit(solution)/shard_map/while/body/scatter-add | solution.py:25
  261.9 10.1 %scatter_fusion = f32[64,128,256]{2,1,0:T(8,128)} fusion(f32[64,128,256]{2,1,0:T(8,128)} %get-tuple-element.257, s32[32]{0:T(128)S(1)} %compare_select_fusion.10, f32[32,128,256]{2,1,0:T(8,128)} %convolution_multiply_fusion.5), kind=kCustom, calls=%fused_computation.3.clone.1 | custom fusion | flops 1048576 | bytes 12583040 | tf_op jit(solution)/shard_map/while/body/scatter-add | solution.py:25
  289.6 65.5 %all-reduce = bf16[8192]{0:T(1024)(128)(2,1)S(1)} all-reduce(bf16[8192]{0:T(1024)(128)(2,1)S(1)} %convert_bitcast_fusion), channel_id=2, replica_groups=mesh['row'=8,'col'=16] {'col'}, use_global_device_ids=true, to_apply=%region_2.0.clone | all-reduce | flops 8192 | bytes 32768
  362.0 49.8 %all-gather.6.cloned.1.call-done = bf16[4096,256]{1,0:T(8,128)(2,1)} async-done(((bf16[512,256]{1,0:T(8,128)(2,1)}), bf16[4096,256]{1,0:T(8,128)(2,1)}) %all-gather.6.cloned.1.call-update) | async-done | bytes 2097168 | tf_op jit(solution)/shard_map/all_gather | solution.py:33
  416.1 204.9 %while.21 = (s32[]{:T(128)}, f32[64,128,256]{2,1,0:T(8,128)}, s32[]{:T(128)}, s32[384]{0:T(512)S(1)}, bf16[384,128,128]{2,1,0:T(8,128)(2,1)}, /*index=5*/s32[384...) while((s32[]{:T(128)}, f32[64,128,256]{2,1,0:T(8,128)}, ...), condition=%wide.region_9.11_spmd, body=%wide.region_7.10_spmd.sunk | while | flops 271582656 | bytes 24122744 | solution.py:29
  423.1 10.0 %scatter_fusion.1 = f32[64,128,256]{2,1,0:T(8,128)} fusion(f32[64,128,256]{2,1,0:T(8,128)} %get-tuple-element.293, s32[32]{0:T(128)S(1)} %compare_select_fusion.11, f32[32,128,256]{2,1,0:T(8,128)} %convolution_multiply_fusion.6), kind=kCustom, calls=%fused_computation.4.clone.1 | custom fusion | flops 1048576 | bytes 12583040 | tf_op jit(solution)/shard_map/while/body/scatter-add | solution.py:25
  440.2 10.0 %scatter_fusion.1 = f32[64,128,256]{2,1,0:T(8,128)} fusion(f32[64,128,256]{2,1,0:T(8,128)} %get-tuple-element.293, s32[32]{0:T(128)S(1)} %compare_select_fusion.11, f32[32,128,256]{2,1,0:T(8,128)} %convolution_multiply_fusion.6), kind=kCustom, calls=%fused_computation.4.clone.1 | custom fusion | flops 1048576 | bytes 12583040 | tf_op jit(solution)/shard_map/while/body/scatter-add | solution.py:25
  491.3 10.1 %scatter_fusion.1 = f32[64,128,256]{2,1,0:T(8,128)} fusion(f32[64,128,256]{2,1,0:T(8,128)} %get-tuple-element.293, s32[32]{0:T(128)S(1)} %compare_select_fusion.11, f32[32,128,256]{2,1,0:T(8,128)} %convolution_multiply_fusion.6), kind=kCustom, calls=%fused_computation.4.clone.1 | custom fusion | flops 1048576 | bytes 12583040 | tf_op jit(solution)/shard_map/while/body/scatter-add | solution.py:25
  508.5 10.0 %scatter_fusion.1 = f32[64,128,256]{2,1,0:T(8,128)} fusion(f32[64,128,256]{2,1,0:T(8,128)} %get-tuple-element.293, s32[32]{0:T(128)S(1)} %compare_select_fusion.11, f32[32,128,256]{2,1,0:T(8,128)} %convolution_multiply_fusion.6), kind=kCustom, calls=%fused_computation.4.clone.1 | custom fusion | flops 1048576 | bytes 12583040 | tf_op jit(solution)/shard_map/while/body/scatter-add | solution.py:25
  525.5 10.0 %scatter_fusion.1 = f32[64,128,256]{2,1,0:T(8,128)} fusion(f32[64,128,256]{2,1,0:T(8,128)} %get-tuple-element.293, s32[32]{0:T(128)S(1)} %compare_select_fusion.11, f32[32,128,256]{2,1,0:T(8,128)} %convolution_multiply_fusion.6), kind=kCustom, calls=%fused_computation.4.clone.1 | custom fusion | flops 1048576 | bytes 12583040 | tf_op jit(solution)/shard_map/while/body/scatter-add | solution.py:25
  576.5 10.1 %scatter_fusion.1 = f32[64,128,256]{2,1,0:T(8,128)} fusion(f32[64,128,256]{2,1,0:T(8,128)} %get-tuple-element.293, s32[32]{0:T(128)S(1)} %compare_select_fusion.11, f32[32,128,256]{2,1,0:T(8,128)} %convolution_multiply_fusion.6), kind=kCustom, calls=%fused_computation.4.clone.1 | custom fusion | flops 1048576 | bytes 12583040 | tf_op jit(solution)/shard_map/while/body/scatter-add | solution.py:25
  593.7 10.1 %scatter_fusion.1 = f32[64,128,256]{2,1,0:T(8,128)} fusion(f32[64,128,256]{2,1,0:T(8,128)} %get-tuple-element.293, s32[32]{0:T(128)S(1)} %compare_select_fusion.11, f32[32,128,256]{2,1,0:T(8,128)} %convolution_multiply_fusion.6), kind=kCustom, calls=%fused_computation.4.clone.1 | custom fusion | flops 1048576 | bytes 12583040 | tf_op jit(solution)/shard_map/while/body/scatter-add | solution.py:25
  610.9 10.1 %scatter_fusion.1 = f32[64,128,256]{2,1,0:T(8,128)} fusion(f32[64,128,256]{2,1,0:T(8,128)} %get-tuple-element.293, s32[32]{0:T(128)S(1)} %compare_select_fusion.11, f32[32,128,256]{2,1,0:T(8,128)} %convolution_multiply_fusion.6), kind=kCustom, calls=%fused_computation.4.clone.1 | custom fusion | flops 1048576 | bytes 12583040 | tf_op jit(solution)/shard_map/while/body/scatter-add | solution.py:25
  627.1 80.6 %reduce-scatter.5.cloned.1.call-done = bf16[512,256]{1,0:T(8,128)(2,1)} async-done(((bf16[8192,256]{1,0:T(8,128)(2,1)}), bf16[512,256]{1,0:T(8,128)(2,1)}) %reduce-scatter.5.cloned.1.call-update) | async-done | bytes 262160 | tf_op jit(solution)/shard_map/reduce_scatter | solution.py:81
  711.1 48.3 %all-gather.8.cloned.1.call-done = bf16[4096,256]{1,0:T(8,128)(2,1)} async-done(((bf16[512,256]{1,0:T(8,128)(2,1)}), bf16[4096,256]{1,0:T(8,128)(2,1)}) %all-gather.8.cloned.1.call-update) | async-done | bytes 2097168 | tf_op jit(solution)/shard_map/all_gather | solution.py:33
  (189 shorter events, 288.7 us)
Async XLA Ops:
  6.5 352.4 %copy-start = (bf16[1,256,512]{2,1,0:T(8,128)(2,1)S(1)}, bf16[1,256,512]{2,1,0:T(8,128)(2,1)}, u32[]{:S(2)}) copy-start(bf16[1,256,512]{2,1,0:T(8,128)(2,1)} %param.26) | copy-start | bytes 786436
  6.5 56.2 %all-gather.4.cloned.1.call-start = ((), (), s32[]{:S(2)}) async-start(), calls=%async_computation.2 | async-start | bytes 2359296 | tf_op jit(solution)/shard_map/all_gather | solution.py:33
  8.6 350.4 %reduce-scatter.3.cloned.1.call-start = ((), (), s32[]{:S(2)}) async-start(), calls=%async_computation.3 | async-start | bytes 4456448 | tf_op jit(solution)/shard_map/reduce_scatter | solution.py:81
  277.9 0.7 copy-start.10
  277.9 1.9 copy-start.6
  277.9 133.9 %all-gather.6.cloned.1.call-start = ((), (), s32[]{:S(2)}) async-start(), calls=%async_computation.4 | async-start | bytes 2359296 | tf_op jit(solution)/shard_map/all_gather | solution.py:33
  360.3 1.0 copy-start.1
  362.0 345.7 %reduce-scatter.5.cloned.1.call-start = ((), (), s32[]{:S(2)}) async-start(), calls=%async_computation.5 | async-start | bytes 4456448 | tf_op jit(solution)/shard_map/reduce_scatter | solution.py:81
  627.0 80.7 %copy-start.2 = (f32[512,512]{1,0:T(8,128)S(1)}, f32[512,512]{1,0:T(8,128)}, u32[]{:S(2)}) copy-start(f32[512,512]{1,0:T(8,128)} %copy-done.1) | copy-start | bytes 3145732
  627.0 80.7 %copy-start.7 = (f32[1,256]{1,0:T(1,128)S(1)}, f32[1,256]{1,0:T(1,128)}, u32[]{:S(2)}) copy-start(f32[1,256]{1,0:T(1,128)} %param.27) | copy-start | bytes 3076
  627.0 82.6 %copy-start.3 = (bf16[512,128]{1,0:T(8,128)(2,1)S(1)}, bf16[512,128]{1,0:T(8,128)(2,1)}, u32[]{:S(2)}) copy-start(bf16[512,128]{1,0:T(8,128)(2,1)} %param.18) | copy-start | bytes 393220
  627.0 82.7 %copy-start.5 = (s32[4,4]{1,0:T(4,128)S(1)}, s32[4,4]{1,0:T(4,128)}, u32[]{:S(2)}) copy-start(s32[4,4]{1,0:T(4,128)} %param.23) | copy-start | bytes 196
  627.0 82.9 %copy-start.8 = (bf16[256,128]{1,0:T(8,128)(2,1)S(1)}, bf16[256,128]{1,0:T(8,128)(2,1)}, u32[]{:S(2)}) copy-start(bf16[256,128]{1,0:T(8,128)(2,1)} %param.28) | copy-start | bytes 196612
  627.0 82.9 %copy-start.9 = (f32[128]{0:T(128)S(1)}, f32[128]{0:T(128)}, u32[]{:S(2)}) copy-start(f32[128]{0:T(128)} %param.29) | copy-start | bytes 1540
  627.0 132.4 %all-gather.8.cloned.1.call-start = ((), (), s32[]{:S(2)}) async-start(), calls=%async_computation.6 | async-start | bytes 2359296 | tf_op jit(solution)/shard_map/all_gather | solution.py:33
  761.6 1.7 copy-start.4
Sparse Core Ops, SparseCore 0:
  9.0 53.6 all-gather.3
  278.1 80.8 reduce-scatter.2
  362.1 49.6 all-gather.5
  627.2 80.5 reduce-scatter.4
  709.7 49.6 all-gather.7
where the time goes:
time: 774 us; the launch traced here: 771 us
  other arithmetic  285 us (37%)
  waiting for transfers between devices  235 us (30%)
  matrix products  101 us (13%)
  local copies, waits for them, and re-layouts  69.1 us (9%)
  blocking collectives  65.5 us (8%)
  between operations  14.6 us (2%)
    scatter-add x24, other arithmetic, add_group(): return carried.at[rows_now].add(products * live_mask[:, None, None])  240 us
    all_gather x3, waiting for transfers between devices, column_panel(): gathered = lax.all_gather(features, 'row', axis=0, tiled=True)  150 us
    dot_general x24, matrix products, add_group(): jnp.einsum('gij,gjf->gif', vals_now, picked, preferred_element_type=jnp.f...  95.6 us
    reduce_scatter x2, waiting for transfers between devices, per_device(): lax.psum_scatter(flattened.astype(jnp.bfloat16), 'col', scatter_dimension...  84.5 us
    unnamed x1, blocking collectives  65.5 us
    gather x24, local copies, waits for them, and re-layouts, add_group(): picked = jnp.take(panel_blocks, cols_now, axis=0)  54.5 us
    and x24, other arithmetic, add_group(): picked = jnp.take(panel_blocks, cols_now, axis=0)  17.4 us
  transfers between devices with their start and end apart: 5, of which 5 were waited for; matrix products, arithmetic and copies ran while one was open for 2% of the time, Pallas kernels for 0%

commit v1 on v0

v1 whole, which is shorter than its diff:
```python
import functools

import jax
import jax.numpy as jnp
from jax import lax
from jax.experimental import pallas as pl
from jax.experimental.pallas import tpu as pltpu
from jax.sharding import PartitionSpec as P

epsilon = 1e-06
mix_alpha = 0.8

BLK = 128
N_X, N_Y = 4, 4
N_ROW, N_COL = 8, 16
DEV_BLOCKS = 4
HALF_BLOCKS = 32
RING = 64
UNROLL = 4


def row_of(x, z_lo):
    return (x % N_X) * 2 + z_lo


def col_of(y, z_hi, core):
    return ((y % N_Y) * 2 + z_hi) * 2 + core


def shift_row(value, dx, dz):
    perm = [(row_of(x, z), row_of(x + dx, z ^ dz)) for x in range(N_X) for z in range(2)]
    return lax.ppermute(value, "row", perm)


def shift_col(value, dy, dz, dc):
    perm = [
        (col_of(y, z, c), col_of(y + dy, z ^ dz, c ^ dc))
        for y in range(N_Y)
        for z in range(2)
        for c in range(2)
    ]
    return lax.ppermute(value, "col", perm)


def gather_row(own):
    half = own.shape[0] // 2
    from_z = shift_row(own, 0, 1)
    from_left = shift_row(own, 1, 0)
    from_right = shift_row(own, -1, 0)
    far = shift_row(from_right, -1, 0)
    left_z = shift_row(from_z, 1, 0)
    right_z = shift_row(from_right, 0, 1)
    far_z_top = shift_row(left_z[:half], 1, 0)
    far_z_bottom = shift_row(right_z[half:], -1, 0)
    return [own, from_z, from_right, right_z, far, (far_z_top, far_z_bottom), from_left, left_z]


def add(*values):
    total = values[0].astype(jnp.float32)
    for value in values[1:]:
        total = total + value.astype(jnp.float32)
    return total


def scatter_col(send, keep):
    got = shift_col(send, 0, 0, 1)

    def pair(dy, dz, *more):
        at = dy * 2 + dz
        return add(keep[at], got[at], *more)

    low = jnp.bfloat16
    far_up = shift_col(pair(2, 0).astype(low), 1, 0, 0)
    far_down = shift_col(pair(2, 1).astype(low), -1, 0, 0)
    direct_up = shift_col(pair(1, 1).astype(low), 1, 0, 0)
    direct_down = shift_col(pair(3, 0).astype(low), -1, 0, 0)
    relay_up = shift_col(pair(1, 0, far_up).astype(low), 1, 0, 0)
    relay_down = shift_col(pair(3, 1, far_down).astype(low), -1, 0, 0)
    other = pair(0, 1, relay_down, direct_up).astype(low)
    from_other = shift_col(other, 0, 1, 0)
    return pair(0, 0, relay_up, direct_down, from_other)


def spmm_kernel(with_degree, half, count_ref, first_ref, second_ref, *refs):
    pieces = refs[:9]
    vals_ref = refs[9]
    out_ref = refs[10]
    panel, total, ring, ring_sem, panel_sem = refs[11:16]
    width = pieces[0].shape[-1]
    rows_half = pieces[5].shape[0]

    groups = (count_ref[half] + UNROLL - 1) // UNROLL
    pairs = groups * UNROLL

    def copies(pair, slot):
        a = first_ref[half, pair] & 511
        b = second_ref[half, pair] & 511
        return (
            pltpu.make_async_copy(vals_ref.at[a], ring.at[slot, 0], ring_sem.at[slot, 0]),
            pltpu.make_async_copy(vals_ref.at[b], ring.at[slot, 1], ring_sem.at[slot, 1]),
        )

    def start(pair, slot):
        for copy in copies(pair, slot):
            copy.start()

    panel_copies = []
    at = 0
    for index, piece in enumerate(pieces):
        blocks = piece.shape[0]
        panel_copies.append(
            pltpu.make_async_copy(
                piece,
                panel.at[pl.ds(at, blocks), :, pl.ds(0, width)],
                panel_sem.at[index],
            )
        )
        at += blocks
    for copy in panel_copies:
        copy.start()

    @pl.loop(0, jnp.minimum(pairs, RING))
    def _(pair):
        start(pair, pair)

    panel[N_ROW * DEV_BLOCKS] = jnp.zeros(panel.shape[1:], panel.dtype)
    if with_degree:

        @pl.loop(0, N_ROW * DEV_BLOCKS)
        def _(block):
            panel[block, :, width:] = jnp.ones((BLK, panel.shape[2] - width), panel.dtype)

    @pl.loop(0, HALF_BLOCKS)
    def _(block):
        total[block] = jnp.zeros(total.shape[1:], jnp.float32)

    for copy in panel_copies:
        copy.wait()

    @pl.loop(0, groups)
    def _(group):
        base = (group % (RING // UNROLL)) * UNROLL
        for u in range(UNROLL):
            pair = group * UNROLL + u
            slot = base + u
            for copy in copies(pair, slot):
                copy.wait()
        for u in range(UNROLL):
            pair = group * UNROLL + u
            slot = base + u
            first = first_ref[half, pair]
            second = second_ref[half, pair]
            row = lax.shift_right_logical(first, 15)
            col_a = lax.shift_right_logical(first, 9) & 63
            col_b = lax.shift_right_logical(second, 9) & 63
            left = jnp.concatenate([ring[slot, 0], ring[slot, 1]], axis=1)
            right = jnp.concatenate([panel[col_a], panel[col_b]], axis=0)
            total[row] += jnp.dot(left, right, preferred_element_type=jnp.float32)
        for u in range(UNROLL):
            pair = group * UNROLL + u
            slot = base + u

            @pl.when(pair + RING < pairs)
            def _():
                start(pair + RING, slot)

    if with_degree:
        degree = refs[16]
        degree[...] = jnp.zeros(degree.shape, jnp.float32)
        eye = lax.broadcasted_iota(jnp.int32, (BLK, BLK), 0) == lax.broadcasted_iota(
            jnp.int32, (BLK, BLK), 1
        )

    @pl.loop(0, HALF_BLOCKS // DEV_BLOCKS)
    def _(dest):
        for j in range(DEV_BLOCKS):
            block = dest * DEV_BLOCKS + j
            out_ref[dest, pl.ds(j * BLK, BLK), :] = total[block, :, :width].astype(out_ref.dtype)
            if with_degree:
                spread = jnp.where(eye, total[block, :, width:], 0.0)
                degree[j : j + 1, :] = jnp.sum(spread, axis=0, keepdims=True)
        if with_degree:
            out_ref[dest, pl.ds(DEV_BLOCKS * BLK, 16), :] = degree[...].astype(out_ref.dtype)


def spmm(pieces, vals, plan, half, with_degree):
    count, first, second = plan
    flat = []
    for piece in pieces:
        for part in piece if isinstance(piece, tuple) else (piece,):
            flat.append(part.reshape(-1, BLK, part.shape[-1]))
    width = flat[0].shape[-1]
    rows = DEV_BLOCKS * BLK + (16 if with_degree else 0)
    wide = width + (BLK if with_degree else 0)
    scratch = [
        pltpu.VMEM((N_ROW * DEV_BLOCKS + 1, BLK, wide), jnp.bfloat16),
        pltpu.VMEM((HALF_BLOCKS, BLK, wide), jnp.float32),
        pltpu.VMEM((RING, 2, BLK, BLK), jnp.bfloat16),
        pltpu.SemaphoreType.DMA((RING, 2)),
        pltpu.SemaphoreType.DMA((len(flat),)),
    ]
    if with_degree:
        scratch.append(pltpu.VMEM((16, BLK), jnp.float32))
    any_spec = pl.BlockSpec(memory_space=pl.ANY)
    smem = pl.BlockSpec(memory_space=pltpu.SMEM)
    return pl.pallas_call(
        functools.partial(spmm_kernel, with_degree, half),
        out_shape=jax.ShapeDtypeStruct((HALF_BLOCKS // DEV_BLOCKS, rows, width), jnp.bfloat16),
        in_specs=[smem] * 3 + [any_spec] * (len(flat) + 1),
        out_specs=pl.BlockSpec(memory_space=pltpu.VMEM),
        scratch_shapes=scratch,
        compiler_params=pltpu.CompilerParams(vmem_limit_bytes=24 * 1024 * 1024),
        cost_estimate=pl.CostEstimate(
            flops=2 * 208 * BLK * 256 * 256, bytes_accessed=8 * 1024 * 1024, transcendentals=0
        ),
        name="spmm_keep" if half else "spmm_send",
    )(count, first, second, *flat, vals)


def make_plan(row_ids, col_ids, live_count, row_at, col_at):
    capacity = row_ids.shape[0]
    slots = jnp.arange(capacity, dtype=jnp.int32)
    live = slots < live_count
    x, z_lo = row_at // 2, row_at % 2
    y, z_hi, core = col_at // 4, (col_at // 2) % 2, col_at % 2
    dest, j = row_ids // DEV_BLOCKS, row_ids % DEV_BLOCKS
    dy = (dest // 4 - y) % N_Y
    dz = (dest // 2 + z_hi) % 2
    dc = (dest + core) % 2
    row = (1 - dc) * HALF_BLOCKS + (dy * 2 + dz) * DEV_BLOCKS + j
    col = relative_block(col_ids, x, z_lo)
    row_key = jnp.where(live, row, 2 * HALF_BLOCKS)
    same = (row_key[:, None] == row_key[None, :]) & live[None, :]
    within = jnp.sum((same & (slots[None, :] < slots[:, None])).astype(jnp.int32), axis=1)
    opens = live & (within % 2 == 0)
    same_half = (row_key[:, None] // HALF_BLOCKS) == (row_key[None, :] // HALF_BLOCKS)
    ahead = (row_key[None, :] < row_key[:, None]) & same_half & opens[None, :]
    pair = jnp.sum(ahead.astype(jnp.int32), axis=1) + within // 2
    half = row_key // HALF_BLOCKS
    longest = (capacity + HALF_BLOCKS) // 2 + UNROLL
    places = jnp.arange(longest, dtype=jnp.int32)
    word = slots + col * 512 + (row % HALF_BLOCKS) * (512 * 64) - N_ROW * DEV_BLOCKS * 512

    def lay(side):
        out = []
        for h in range(2):
            here = (within % 2 == side) & (half == h)
            hit = (pair[None, :] == places[:, None]) & here[None, :]
            out.append(
                N_ROW * DEV_BLOCKS * 512 + jnp.sum(jnp.where(hit, word[None, :], 0), axis=1)
            )
        return jnp.stack(out).astype(jnp.int32)

    count = jnp.stack(
        [jnp.sum((opens & (half == h)).astype(jnp.int32)) for h in range(2)]
    ).astype(jnp.int32)
    return count, lay(0), lay(1)


def relative_block(ids, x, z_lo):
    owner, j = ids // DEV_BLOCKS, ids % DEV_BLOCKS
    return (((owner // 2 - x) % N_X) * 2 + (owner + z_lo) % 2) * DEV_BLOCKS + j


def per_device(
    attributes,
    adj_values,
    adj_rows,
    adj_cols,
    adj_count,
    pair_ids,
    struct_target,
    w_first,
    w_rest,
    layer_bias,
    w_attr,
    attr_bias,
):
    vals = adj_values[0, 0]
    nodes_dev = attributes.shape[0]
    hidden_size = w_rest.shape[1]
    pair_count = pair_ids.shape[1]
    row_at = lax.axis_index("row")
    col_at = lax.axis_index("col")
    plan = make_plan(adj_rows[0, 0], adj_cols[0, 0], adj_count[0, 0], row_at, col_at)

    pieces = gather_row(attributes)
    send = spmm(pieces, vals, plan, 0, True)
    keep = spmm(pieces, vals, plan, 1, True)
    summed = scatter_col(send, keep)
    degree = 1.0 + summed[nodes_dev : nodes_dev + DEV_BLOCKS].reshape(-1)
    row_scale = lax.rsqrt(degree)[:, None]
    aggregate = summed[:nodes_dev]
    coarse = lax.reduce_precision(aggregate, 8, 7)
    fine = (aggregate - coarse).astype(jnp.bfloat16)
    coarse = coarse.astype(jnp.bfloat16)
    w_near, w_self = w_first[:, :hidden_size], w_first[:, hidden_size:]
    own_part = jnp.dot(attributes, w_self, preferred_element_type=jnp.float32)
    mixed = jnp.dot(coarse, w_near, preferred_element_type=jnp.float32) + jnp.dot(
        fine, w_near, preferred_element_type=jnp.float32
    )
    hidden_state = jnp.tanh(row_scale * mixed + own_part).astype(jnp.bfloat16)

    features = jnp.dot(
        hidden_state, w_rest[0][:, :hidden_size], preferred_element_type=jnp.float32
    ).astype(jnp.bfloat16)
    pieces = gather_row(features)
    own_part = (
        jnp.dot(hidden_state, w_rest[0][:, hidden_size:], preferred_element_type=jnp.float32)
        + layer_bias[0]
    )
    send = spmm(pieces, vals, plan, 0, False)
    keep = spmm(pieces, vals, plan, 1, False)
    summed = scatter_col(send, keep)
    hidden_state = jnp.tanh(row_scale * summed + own_part).astype(jnp.bfloat16)

    pieces = gather_row(hidden_state)
    rebuilt = jnp.dot(hidden_state, w_attr, preferred_element_type=jnp.float32) + attr_bias
    attr_error = jnp.sqrt(
        jnp.mean((rebuilt - attributes.astype(jnp.float32)) ** 2, axis=1) + epsilon
    )
    whole = jnp.concatenate(
        [part for piece in pieces for part in (piece if isinstance(piece, tuple) else (piece,))]
    ).reshape(-1, BLK, hidden_size)
    own_blocks = hidden_state.reshape(-1, BLK, hidden_size)
    partners = jnp.take(whole, relative_block(pair_ids, row_at // 2, row_at % 2), axis=0)
    logits = jnp.einsum(
        "bif,bpjf->bipj", own_blocks, partners, preferred_element_type=jnp.float32
    ) * hidden_size ** (-0.5)
    probability = jax.nn.sigmoid(logits).reshape(nodes_dev, pair_count, BLK)
    struct_error = jnp.sqrt(
        jnp.mean((probability - struct_target.astype(jnp.float32)) ** 2, axis=(1, 2)) + epsilon
    )
    return mix_alpha * attr_error + (1.0 - mix_alpha) * struct_error


def solution(mesh):
    return jax.shard_map(
        per_device,
        mesh=mesh,
        in_specs=(
            P(("row", "col"), None),
            P("row", "col", None, None, None),
            P("row", "col", None),
            P("row", "col", None),
            P("row", "col"),
            P(("row", "col"), None),
            P(("row", "col"), None, None),
            P(),
            P(),
            P(),
            P(),
            P(),
        ),
        out_specs=P(("row", "col")),
        check_vma=False,
    )
```

time: 774 us -> 215 us (0.28)
  other arithmetic: 285 us -> 8.97 us
  waiting for transfers between devices: 235 us -> 50.6 us
  matrix products: 101 us -> 1.97 us
  Pallas kernels: 0 us -> 73.9 us
  blocking collectives: 65.5 us -> 0 us
  starting transfers between devices: 0.17 us -> 62.8 us
  local copies, waits for them, and re-layouts: 69.1 us -> 14.7 us
  between operations: 14.6 us -> 1.2 us
    scatter-add x25 -> x0, other arithmetic: 242 us -> none  [the longest x24 240 us: add_group(): return carried.at[rows_now].add(products * live_mask[:, None, None])]
    all_gather x3 -> x0, waiting for transfers between devices: 150 us -> none  [column_panel(): gathered = lax.all_gather(features, 'row', axis=0, tiled=True)]
    dot_general x26 -> x5, matrix products: 98.2 us -> 1.11 us  [the longest x1 0.23 us: per_device(): jnp.dot(hidden_state, w_rest[0][:, :hidden_size], preferred_element_type=...]
    reduce_scatter x2 -> x0, waiting for transfers between devices: 84.5 us -> none  [per_device(): lax.psum_scatter(flattened.astype(jnp.bfloat16), 'col', scatter_dimension...]
    pallas_call x0 -> x4, Pallas kernels: none -> 73.9 us  [spmm(): pl.pallas_call(functools.partial(spmm_kernel, with_degree, half), out_sha...]
    unnamed x1 -> x0, blocking collectives: 65.5 us -> none
    ppermute x0 -> x40, starting transfers between devices: none -> 62.8 us  [the longest x24 35.7 us: shift_row(): return lax.ppermute(value, 'row', perm)]
    gather x25 -> x1, local copies, waits for them, and re-layouts: 56.7 us -> 2.2 us  [per_device(): jnp.take(whole, relative_block(pair_ids, row_at // 2, row_at % 2), axis=0)]
  transfers between devices with their start and end apart: 5 -> 40, of which waited for: 5 -> 18; matrix products, arithmetic and copies ran while one was open for 2% -> 5% of each run, Pallas kernels for 0% -> 18%
where the time goes in v1:
time: 215 us; the launch traced here: 214 us
  Pallas kernels  73.9 us (34%)
  starting transfers between devices  62.8 us (29%)
  waiting for transfers between devices  50.6 us (24%)
  local copies, waits for them, and re-layouts  14.7 us (7%)
  other arithmetic  8.97 us (4%)
    pallas_call x4, Pallas kernels, spmm(): pl.pallas_call(functools.partial(spmm_kernel, with_degree, half), out_sha...  73.9 us
    ppermute x24, starting transfers between devices, shift_row(): return lax.ppermute(value, 'row', perm)  35.7 us
    ppermute x16, waiting for transfers between devices, shift_col(): return lax.ppermute(value, 'col', perm)  27.5 us
    ppermute x16, starting transfers between devices, shift_col(): return lax.ppermute(value, 'col', perm)  27.1 us
    ppermute x24, waiting for transfers between devices, shift_row(): return lax.ppermute(value, 'row', perm)  23.2 us
    unnamed x36, local copies, waits for them, and re-layouts  11.6 us
  transfers between devices with their start and end apart: 40, of which 18 were waited for; matrix products, arithmetic and copies ran while one was open for 5% of the time, Pallas kernels for 18%

profile of v1, /device:TPU:0, one launch (start us, length us, event | category | flops | bytes accessed | tf_op | source)
XLA Modules:
  0.0 214.2 jit_solution(9475594388365441192)
XLA Ops:
  0.0 2.8 %collective-permute-start.1 = (bf16[512,128]{1,0:T(8,128)(2,1)}, bf16[512,128]{1,0:T(8,128)(2,1)S(1)}, u32[]{:S(2)}, u32[]{:S(2)}) collective-permute-start(bf16[512,128]{1,0:T(8,128)(2,1)} %param.12), channel_id=1, source_target_pairs={{0,96},{16,112},{32,0},{48,16},{64,32},{80,48},{96,64},{112,80},{1... | collective-permute-start | bytes 393224 | tf_op jit(solution)/shard_map/ppermute | solution.py:32
  13.6 3.2 %collective-permute-start.6 = (bf16[256,128]{1,0:T(8,128)(2,1)S(1)}, bf16[256,128]{1,0:T(8,128)(2,1)S(1)}, u32[]{:S(2)}, u32[]{:S(2)}) collective-permute-start(bf16[256,128]{1,0:T(8,128)(2,1)S(1)} %slice.179), channel_id=1, source_target_pairs={{0,96},{16,112},{32,0},{48,16},{64,32},{80,48},{96,64},{112,80},{1... | collective-permute-start | bytes 196616 | tf_op jit(solution)/shard_map/ppermute | solution.py:32
  18.7 3.7 %collective-permute-done.5 = bf16[256,128]{1,0:T(8,128)(2,1)S(1)} collective-permute-done((bf16[256,128]{1,0:T(8,128)(2,1)S(1)}, bf16[256,128]{1,0:T(8,128)(2,1)S(1)}, u32[]{:S(2)}, u32[]{:S(2)}) %collective-permute-start.5) | collective-permute-done | bytes 65568 | tf_op jit(solution)/shard_map/ppermute | solution.py:32
  22.4 4.6 %copy-done.1 = bf16[1,1,384,128,128]{4,3,2,1,0:T(8,128)(2,1)S(1)} copy-done((bf16[1,1,384,128,128]{4,3,2,1,0:T(8,128)(2,1)S(1)}, bf16[1,1,384,128,128]{4,3,2,1,0:T(8,128)(2,1)}, u32[]{:S(2)}) %copy-start.1) | copy-done | bytes 12582936
  27.8 17.5 %spmm_send.2 = bf16[8,528,128]{2,1,0:T(8,128)(2,1)S(1)} custom-call(s32[2]{0:T(128)S(1)} %pad_add_fusion.2.count_ref, s32[2,212]{1,0:T(2,128)S(1)} %pad_add_fusion.first_ref, s32[2,212]{1,0:T(2,128)S(1)} %pad_add_fusion.1.second_ref, bf16[4,128,128]{2,1,0:T(8,128)(2,1)S(1)} %bitcast.126, bf16[4,128,128]{2,1,0:T(8,128)(2,1)S(1)} %bitcast.146, ...), custom_call_target="tpu_custom_call" | custom-call | flops 3489660928 | bytes 8388608 | tf_op jit(solution)/shard_map/spmm_send/pallas_call | solution.py:206
  45.5 19.5 %spmm_keep.2 = bf16[8,528,128]{2,1,0:T(8,128)(2,1)S(1)} custom-call(s32[2]{0:T(128)S(1)} %pad_add_fusion.2.count_ref, s32[2,212]{1,0:T(2,128)S(1)} %pad_add_fusion.first_ref, s32[2,212]{1,0:T(2,128)S(1)} %pad_add_fusion.1.second_ref, bf16[4,128,128]{2,1,0:T(8,128)(2,1)S(1)} %bitcast.127, bf16[4,128,128]{2,1,0:T(8,128)(2,1)S(1)} %bitcast.147, ...), custom_call_target="tpu_custom_call" | custom-call | flops 3489660928 | bytes 8388608 | tf_op jit(solution)/shard_map/spmm_keep/pallas_call | solution.py:206
  67.3 3.0 %collective-permute-done.12 = bf16[528,128]{1,0:T(8,128)(2,1)S(1)} collective-permute-done((bf16[528,128]{1,0:T(8,128)(2,1)S(1)}, bf16[528,128]{1,0:T(8,128)(2,1)S(1)}, u32[]{:S(2)}, u32[]{:S(2)}) %collective-permute-start.12) | collective-permute-done | bytes 135200 | tf_op jit(solution)/shard_map/ppermute | solution.py:42
  76.8 9.1 %collective-permute-start.15 = (bf16[528,128]{1,0:T(8,128)(2,1)S(1)}, bf16[528,128]{1,0:T(8,128)(2,1)S(1)}, u32[]{:S(2)}, u32[]{:S(2)}) collective-permute-start(bf16[528,128]{1,0:T(8,128)(2,1)S(1)} %fusion.32), channel_id=1, source_target_pairs={{0,2},{1,3},{2,0},{3,1},{4,6},{5,7},{6,4},{7,5},{8,10},{9,11},{10,... | collective-permute-start | bytes 405512 | tf_op jit(solution)/shard_map/ppermute | solution.py:42
  86.0 3.7 %collective-permute-done.15 = bf16[528,128]{1,0:T(8,128)(2,1)S(1)} collective-permute-done((bf16[528,128]{1,0:T(8,128)(2,1)S(1)}, bf16[528,128]{1,0:T(8,128)(2,1)S(1)}, u32[]{:S(2)}, u32[]{:S(2)}) %collective-permute-start.15) | collective-permute-done | bytes 135200 | tf_op jit(solution)/shard_map/ppermute | solution.py:42
  90.8 3.3 %collective-permute-start.17 = (bf16[512,256]{1,0:T(8,128)(2,1)S(1)}, bf16[512,256]{1,0:T(8,128)(2,1)S(1)}, u32[]{:S(2)}, u32[]{:S(2)}) collective-permute-start(bf16[512,256]{1,0:T(8,128)(2,1)S(1)} %convolution_convert_fusion), channel_id=1, source_target_pairs={{0,96},{16,112},{32,0},{48,16},{64,32},{80,48},{96,64},{112,80},{1... | collective-permute-start | bytes 786440 | tf_op jit(solution)/shard_map/ppermute | solution.py:32
  94.1 3.8 %collective-permute-done.16 = bf16[512,256]{1,0:T(8,128)(2,1)S(1)} collective-permute-done((bf16[512,256]{1,0:T(8,128)(2,1)S(1)}, bf16[512,256]{1,0:T(8,128)(2,1)S(1)}, u32[]{:S(2)}, u32[]{:S(2)}) %collective-permute-start.16) | collective-permute-done | bytes 262176 | tf_op jit(solution)/shard_map/ppermute | solution.py:32
  109.6 2.7 %collective-permute-done.21 = bf16[256,256]{1,0:T(8,128)(2,1)S(1)} collective-permute-done((bf16[256,256]{1,0:T(8,128)(2,1)S(1)}, bf16[256,256]{1,0:T(8,128)(2,1)S(1)}, u32[]{:S(2)}, u32[]{:S(2)}) %collective-permute-start.21) | collective-permute-done | bytes 131104 | tf_op jit(solution)/shard_map/ppermute | solution.py:32
  112.3 17.4 %spmm_send.3 = bf16[8,512,256]{2,1,0:T(8,128)(2,1)S(1)} custom-call(s32[2]{0:T(128)S(1)} %pad_add_fusion.2.count_ref, s32[2,212]{1,0:T(2,128)S(1)} %pad_add_fusion.first_ref, s32[2,212]{1,0:T(2,128)S(1)} %pad_add_fusion.1.second_ref, bf16[4,128,256]{2,1,0:T(8,128)(2,1)S(1)} %bitcast.124, bf16[4,128,256]{2,1,0:T(8,128)(2,1)S(1)} %bitcast.132, ...), custom_call_target="tpu_custom_call" | custom-call | flops 3489660928 | bytes 8388608 | tf_op jit(solution)/shard_map/spmm_send/pallas_call | solution.py:206
  129.8 19.5 %spmm_keep.3 = bf16[8,512,256]{2,1,0:T(8,128)(2,1)S(1)} custom-call(s32[2]{0:T(128)S(1)} %pad_add_fusion.2.count_ref, s32[2,212]{1,0:T(2,128)S(1)} %pad_add_fusion.first_ref, s32[2,212]{1,0:T(2,128)S(1)} %pad_add_fusion.1.second_ref, bf16[4,128,256]{2,1,0:T(8,128)(2,1)S(1)} %bitcast.125, bf16[4,128,256]{2,1,0:T(8,128)(2,1)S(1)} %bitcast.133, ...), custom_call_target="tpu_custom_call" | custom-call | flops 3489660928 | bytes 8388608 | tf_op jit(solution)/shard_map/spmm_keep/pallas_call | solution.py:206
  149.7 3.2 %collective-permute-start.28 = (bf16[512,256]{1,0:T(8,128)(2,1)S(1)}, bf16[512,256]{1,0:T(8,128)(2,1)S(1)}, u32[]{:S(2)}, u32[]{:S(2)}) collective-permute-start(bf16[512,256]{1,0:T(8,128)(2,1)S(1)} %get-tuple-element.29), channel_id=1, source_target_pairs={{0,12},{1,13},{2,14},{3,15},{4,0},{5,1},{6,2},{7,3},{8,4},{9,5},{1... | collective-permute-start | bytes 786440 | tf_op jit(solution)/shard_map/ppermute | solution.py:42
  152.9 7.2 %collective-permute-done.25 = bf16[512,256]{1,0:T(8,128)(2,1)S(1)} collective-permute-done((bf16[512,256]{1,0:T(8,128)(2,1)S(1)}, bf16[512,256]{1,0:T(8,128)(2,1)S(1)}, u32[]{:S(2)}, u32[]{:S(2)}) %collective-permute-start.25) | collective-permute-done | bytes 262176 | tf_op jit(solution)/shard_map/ppermute | solution.py:42
  163.8 3.6 %collective-permute-done.29 = bf16[512,256]{1,0:T(8,128)(2,1)S(1)} collective-permute-done((bf16[512,256]{1,0:T(8,128)(2,1)S(1)}, bf16[512,256]{1,0:T(8,128)(2,1)S(1)}, u32[]{:S(2)}, u32[]{:S(2)}) %collective-permute-start.29) | collective-permute-done | bytes 262176 | tf_op jit(solution)/shard_map/ppermute | solution.py:42
  167.6 7.7 %collective-permute-start.31 = (bf16[512,256]{1,0:T(8,128)(2,1)S(1)}, bf16[512,256]{1,0:T(8,128)(2,1)}, u32[]{:S(2)}, u32[]{:S(2)}) collective-permute-start(bf16[512,256]{1,0:T(8,128)(2,1)S(1)} %fusion.17), channel_id=1, source_target_pairs={{0,2},{1,3},{2,0},{3,1},{4,6},{5,7},{6,4},{7,5},{8,10},{9,11},{10,... | collective-permute-start | bytes 786440 | tf_op jit(solution)/shard_map/ppermute | solution.py:42
  175.7 5.5 %collective-permute-done.31 = bf16[512,256]{1,0:T(8,128)(2,1)} collective-permute-done((bf16[512,256]{1,0:T(8,128)(2,1)S(1)}, bf16[512,256]{1,0:T(8,128)(2,1)}, u32[]{:S(2)}, u32[]{:S(2)}) %collective-permute-start.31) | collective-permute-done | bytes 262176 | tf_op jit(solution)/shard_map/ppermute | solution.py:42
  183.4 3.7 %collective-permute-start.33 = (bf16[512,256]{1,0:T(8,128)(2,1)S(1)}, bf16[512,256]{1,0:T(8,128)(2,1)S(1)}, u32[]{:S(2)}, u32[]{:S(2)}) collective-permute-start(bf16[512,256]{1,0:T(8,128)(2,1)S(1)} %get-tuple-element.14), channel_id=1, source_target_pairs={{0,96},{16,112},{32,0},{48,16},{64,32},{80,48},{96,64},{112,80},{1... | collective-permute-start | bytes 786440 | tf_op jit(solution)/shard_map/ppermute | solution.py:32
  187.3 3.7 %collective-permute-done.33 = bf16[512,256]{1,0:T(8,128)(2,1)S(1)} collective-permute-done((bf16[512,256]{1,0:T(8,128)(2,1)S(1)}, bf16[512,256]{1,0:T(8,128)(2,1)S(1)}, u32[]{:S(2)}, u32[]{:S(2)}) %collective-permute-start.33) | collective-permute-done | bytes 262176 | tf_op jit(solution)/shard_map/ppermute | solution.py:32
  192.2 3.1 %collective-permute-start.35 = (bf16[512,256]{1,0:T(8,128)(2,1)S(1)}, bf16[512,256]{1,0:T(8,128)(2,1)S(1)}, u32[]{:S(2)}, u32[]{:S(2)}) collective-permute-start(bf16[512,256]{1,0:T(8,128)(2,1)S(1)} %collective-permute-done.33), channel_id=1, source_target_pairs={{0,96},{16,112},{32,0},{48,16},{64,32},{80,48},{96,64},{112,80},{1... | collective-permute-start | bytes 786440 | tf_op jit(solution)/shard_map/ppermute | solution.py:32
  196.8 3.6 %collective-permute-done.36 = bf16[512,256]{1,0:T(8,128)(2,1)S(1)} collective-permute-done((bf16[512,256]{1,0:T(8,128)(2,1)S(1)}, bf16[512,256]{1,0:T(8,128)(2,1)S(1)}, u32[]{:S(2)}, u32[]{:S(2)}) %collective-permute-start.36) | collective-permute-done | bytes 262176 | tf_op jit(solution)/shard_map/ppermute | solution.py:32
  200.6 3.3 %collective-permute-start.38 = (bf16[256,256]{1,0:T(8,128)(2,1)S(1)}, bf16[256,256]{1,0:T(8,128)(2,1)S(1)}, u32[]{:S(2)}, u32[]{:S(2)}) collective-permute-start(bf16[256,256]{1,0:T(8,128)(2,1)S(1)} %slice.219), channel_id=1, source_target_pairs={{0,96},{16,112},{32,0},{48,16},{64,32},{80,48},{96,64},{112,80},{1... | collective-permute-start | bytes 393224 | tf_op jit(solution)/shard_map/ppermute | solution.py:32
  (146 shorter events, 54.5 us)
Async XLA Ops:
  0.0 8.5 %collective-permute-start.1 = (bf16[512,128]{1,0:T(8,128)(2,1)}, bf16[512,128]{1,0:T(8,128)(2,1)S(1)}, u32[]{:S(2)}, u32[]{:S(2)}) collective-permute-start(bf16[512,128]{1,0:T(8,128)(2,1)} %param.12), channel_id=1, source_target_pairs={{0,96},{16,112},{32,0},{48,16},{64,32},{80,48},{96,64},{112,80},{1... | collective-permute-start | bytes 393224 | tf_op jit(solution)/shard_map/ppermute | solution.py:32
  4.8 13.4 %collective-permute-start.7 = (bf16[512,128]{1,0:T(8,128)(2,1)}, bf16[512,128]{1,0:T(8,128)(2,1)S(1)}, u32[]{:S(2)}, u32[]{:S(2)}) collective-permute-start(bf16[512,128]{1,0:T(8,128)(2,1)} %param.12), channel_id=1, source_target_pairs={{0,32},{16,48},{32,64},{48,80},{64,96},{80,112},{96,0},{112,16},{1... | collective-permute-start | bytes 393224 | tf_op jit(solution)/shard_map/ppermute | solution.py:32
  8.7 8.1 %collective-permute-start.4 = (bf16[512,128]{1,0:T(8,128)(2,1)S(1)}, bf16[512,128]{1,0:T(8,128)(2,1)S(1)}, u32[]{:S(2)}, u32[]{:S(2)}) collective-permute-start(bf16[512,128]{1,0:T(8,128)(2,1)S(1)} %collective-permute-done), channel_id=1, source_target_pairs={{0,32},{16,48},{32,64},{48,80},{64,96},{80,112},{96,0},{112,16},{1... | collective-permute-start | bytes 393224 | tf_op jit(solution)/shard_map/ppermute | solution.py:32
  9.5 8.7 %collective-permute-start.3 = (bf16[512,128]{1,0:T(8,128)(2,1)S(1)}, bf16[512,128]{1,0:T(8,128)(2,1)S(1)}, u32[]{:S(2)}, u32[]{:S(2)}) collective-permute-start(bf16[512,128]{1,0:T(8,128)(2,1)S(1)} %collective-permute-done.1), channel_id=1, source_target_pairs={{0,96},{16,112},{32,0},{48,16},{64,32},{80,48},{96,64},{112,80},{1... | collective-permute-start | bytes 393224 | tf_op jit(solution)/shard_map/ppermute | solution.py:32
  45.3 19.7 %collective-permute-start.8 = (bf16[8,528,128]{2,1,0:T(8,128)(2,1)S(1)}, bf16[8,528,128]{2,1,0:T(8,128)(2,1)S(1)}, u32[]{:S(2)}, u32[]{:S(2)}) collective-permute-start(bf16[8,528,128]{2,1,0:T(8,128)(2,1)S(1)} %spmm_send.2), channel_id=1, source_target_pairs={{0,1},{1,0},{2,3},{3,2},{4,5},{5,4},{6,7},{7,6},{8,9},{9,8},{10,11... | collective-permute-start | bytes 3244040 | tf_op jit(solution)/shard_map/ppermute | solution.py:42
  67.3 7.7 %collective-permute-start.14 = (bf16[528,128]{1,0:T(8,128)(2,1)S(1)}, bf16[528,128]{1,0:T(8,128)(2,1)S(1)}, u32[]{:S(2)}, u32[]{:S(2)}) collective-permute-start(bf16[528,128]{1,0:T(8,128)(2,1)S(1)} %get-tuple-element.34), channel_id=1, source_target_pairs={{0,4},{1,5},{2,6},{3,7},{4,8},{5,9},{6,10},{7,11},{8,12},{9,13},{1... | collective-permute-start | bytes 405512 | tf_op jit(solution)/shard_map/ppermute | solution.py:42
  71.7 14.2 %collective-permute-start.11 = (bf16[528,128]{1,0:T(8,128)(2,1)S(1)}, bf16[528,128]{1,0:T(8,128)(2,1)S(1)}, u32[]{:S(2)}, u32[]{:S(2)}) collective-permute-start(bf16[528,128]{1,0:T(8,128)(2,1)S(1)} %get-tuple-element.36), channel_id=1, source_target_pairs={{0,12},{1,13},{2,14},{3,15},{4,0},{5,1},{6,2},{7,3},{8,4},{9,5},{1... | collective-permute-start | bytes 405512 | tf_op jit(solution)/shard_map/ppermute | solution.py:42
  73.1 12.9 %collective-permute-start.10 = (bf16[528,128]{1,0:T(8,128)(2,1)S(1)}, bf16[528,128]{1,0:T(8,128)(2,1)S(1)}, u32[]{:S(2)}, u32[]{:S(2)}) collective-permute-start(bf16[528,128]{1,0:T(8,128)(2,1)S(1)} %get-tuple-element.31), channel_id=1, source_target_pairs={{0,4},{1,5},{2,6},{3,7},{4,8},{5,9},{6,10},{7,11},{8,12},{9,13},{1... | collective-permute-start | bytes 405512 | tf_op jit(solution)/shard_map/ppermute | solution.py:42
  76.8 12.8 %collective-permute-start.15 = (bf16[528,128]{1,0:T(8,128)(2,1)S(1)}, bf16[528,128]{1,0:T(8,128)(2,1)S(1)}, u32[]{:S(2)}, u32[]{:S(2)}) collective-permute-start(bf16[528,128]{1,0:T(8,128)(2,1)S(1)} %fusion.32), channel_id=1, source_target_pairs={{0,2},{1,3},{2,0},{3,1},{4,6},{5,7},{6,4},{7,5},{8,10},{9,11},{10,... | collective-permute-start | bytes 405512 | tf_op jit(solution)/shard_map/ppermute | solution.py:42
  90.8 9.8 %collective-permute-start.17 = (bf16[512,256]{1,0:T(8,128)(2,1)S(1)}, bf16[512,256]{1,0:T(8,128)(2,1)S(1)}, u32[]{:S(2)}, u32[]{:S(2)}) collective-permute-start(bf16[512,256]{1,0:T(8,128)(2,1)S(1)} %convolution_convert_fusion), channel_id=1, source_target_pairs={{0,96},{16,112},{32,0},{48,16},{64,32},{80,48},{96,64},{112,80},{1... | collective-permute-start | bytes 786440 | tf_op jit(solution)/shard_map/ppermute | solution.py:32
  97.9 8.1 %collective-permute-start.20 = (bf16[512,256]{1,0:T(8,128)(2,1)S(1)}, bf16[512,256]{1,0:T(8,128)(2,1)S(1)}, u32[]{:S(2)}, u32[]{:S(2)}) collective-permute-start(bf16[512,256]{1,0:T(8,128)(2,1)S(1)} %collective-permute-done.16), channel_id=1, source_target_pairs={{0,32},{16,48},{32,64},{48,80},{64,96},{80,112},{96,0},{112,16},{1... | collective-permute-start | bytes 786440 | tf_op jit(solution)/shard_map/ppermute | solution.py:32
  100.6 9.0 %collective-permute-start.23 = (bf16[512,256]{1,0:T(8,128)(2,1)S(1)}, bf16[512,256]{1,0:T(8,128)(2,1)S(1)}, u32[]{:S(2)}, u32[]{:S(2)}) collective-permute-start(bf16[512,256]{1,0:T(8,128)(2,1)S(1)} %convolution_convert_fusion), channel_id=1, source_target_pairs={{0,32},{16,48},{32,64},{48,80},{64,96},{80,112},{96,0},{112,16},{1... | collective-permute-start | bytes 786440 | tf_op jit(solution)/shard_map/ppermute | solution.py:32
  129.7 19.6 %collective-permute-start.24 = (bf16[8,512,256]{2,1,0:T(8,128)(2,1)S(1)}, bf16[8,512,256]{2,1,0:T(8,128)(2,1)S(1)}, u32[]{:S(2)}, u32[]{:S(2)}) collective-permute-start(bf16[8,512,256]{2,1,0:T(8,128)(2,1)S(1)} %spmm_send.3), channel_id=1, source_target_pairs={{0,1},{1,0},{2,3},{3,2},{4,5},{5,4},{6,7},{7,6},{8,9},{9,8},{10,11... | collective-permute-start | bytes 6291464 | tf_op jit(solution)/shard_map/ppermute | solution.py:42
  149.6 10.5 %collective-permute-start.25 = (bf16[512,256]{1,0:T(8,128)(2,1)S(1)}, bf16[512,256]{1,0:T(8,128)(2,1)S(1)}, u32[]{:S(2)}, u32[]{:S(2)}) collective-permute-start(bf16[512,256]{1,0:T(8,128)(2,1)S(1)} %get-tuple-element.27), channel_id=1, source_target_pairs={{0,4},{1,5},{2,6},{3,7},{4,8},{5,9},{6,10},{7,11},{8,12},{9,13},{1... | collective-permute-start | bytes 786440 | tf_op jit(solution)/shard_map/ppermute | solution.py:42
  149.7 10.4 %collective-permute-start.28 = (bf16[512,256]{1,0:T(8,128)(2,1)S(1)}, bf16[512,256]{1,0:T(8,128)(2,1)S(1)}, u32[]{:S(2)}, u32[]{:S(2)}) collective-permute-start(bf16[512,256]{1,0:T(8,128)(2,1)S(1)} %get-tuple-element.29), channel_id=1, source_target_pairs={{0,12},{1,13},{2,14},{3,15},{4,0},{5,1},{6,2},{7,3},{8,4},{9,5},{1... | collective-permute-start | bytes 786440 | tf_op jit(solution)/shard_map/ppermute | solution.py:42
  152.9 10.9 %collective-permute-start.30 = (bf16[512,256]{1,0:T(8,128)(2,1)S(1)}, bf16[512,256]{1,0:T(8,128)(2,1)S(1)}, u32[]{:S(2)}, u32[]{:S(2)}) collective-permute-start(bf16[512,256]{1,0:T(8,128)(2,1)S(1)} %get-tuple-element.28), channel_id=1, source_target_pairs={{0,4},{1,5},{2,6},{3,7},{4,8},{5,9},{6,10},{7,11},{8,12},{9,13},{1... | collective-permute-start | bytes 786440 | tf_op jit(solution)/shard_map/ppermute | solution.py:42
  161.5 14.1 %collective-permute-start.27 = (bf16[512,256]{1,0:T(8,128)(2,1)S(1)}, bf16[512,256]{1,0:T(8,128)(2,1)}, u32[]{:S(2)}, u32[]{:S(2)}) collective-permute-start(bf16[512,256]{1,0:T(8,128)(2,1)S(1)} %get-tuple-element.30), channel_id=1, source_target_pairs={{0,12},{1,13},{2,14},{3,15},{4,0},{5,1},{6,2},{7,3},{8,4},{9,5},{1... | collective-permute-start | bytes 786440 | tf_op jit(solution)/shard_map/ppermute | solution.py:42
  161.6 14.1 %collective-permute-start.26 = (bf16[512,256]{1,0:T(8,128)(2,1)}, bf16[512,256]{1,0:T(8,128)(2,1)}, u32[]{:S(2)}, u32[]{:S(2)}) collective-permute-start(bf16[512,256]{1,0:T(8,128)(2,1)} %get-tuple-element.25), channel_id=1, source_target_pairs={{0,4},{1,5},{2,6},{3,7},{4,8},{5,9},{6,10},{7,11},{8,12},{9,13},{1... | collective-permute-start | bytes 786440 | tf_op jit(solution)/shard_map/ppermute | solution.py:42
  167.6 13.6 %collective-permute-start.31 = (bf16[512,256]{1,0:T(8,128)(2,1)S(1)}, bf16[512,256]{1,0:T(8,128)(2,1)}, u32[]{:S(2)}, u32[]{:S(2)}) collective-permute-start(bf16[512,256]{1,0:T(8,128)(2,1)S(1)} %fusion.17), channel_id=1, source_target_pairs={{0,2},{1,3},{2,0},{3,1},{4,6},{5,7},{6,4},{7,5},{8,10},{9,11},{10,... | collective-permute-start | bytes 786440 | tf_op jit(solution)/shard_map/ppermute | solution.py:42
  183.4 8.4 %collective-permute-start.32 = (bf16[512,256]{1,0:T(8,128)(2,1)S(1)}, bf16[512,256]{1,0:T(8,128)(2,1)S(1)}, u32[]{:S(2)}, u32[]{:S(2)}) collective-permute-start(bf16[512,256]{1,0:T(8,128)(2,1)S(1)} %get-tuple-element.14), channel_id=1, source_target_pairs={{0,16},{16,0},{32,48},{48,32},{64,80},{80,64},{96,112},{112,96},{1... | collective-permute-start | bytes 786440 | tf_op jit(solution)/shard_map/ppermute | solution.py:32
  187.2 20.8 %collective-permute-start.39 = (bf16[512,256]{1,0:T(8,128)(2,1)S(1)}, bf16[512,256]{1,0:T(8,128)(2,1)S(1)}, u32[]{:S(2)}, u32[]{:S(2)}) collective-permute-start(bf16[512,256]{1,0:T(8,128)(2,1)S(1)} %get-tuple-element.14), channel_id=1, source_target_pairs={{0,32},{16,48},{32,64},{48,80},{64,96},{80,112},{96,0},{112,16},{1... | collective-permute-start | bytes 786440 | tf_op jit(solution)/shard_map/ppermute | solution.py:32
  191.0 9.6 %collective-permute-start.34 = (bf16[512,256]{1,0:T(8,128)(2,1)S(1)}, bf16[512,256]{1,0:T(8,128)(2,1)S(1)}, u32[]{:S(2)}, u32[]{:S(2)}) collective-permute-start(bf16[512,256]{1,0:T(8,128)(2,1)S(1)} %collective-permute-done.33), channel_id=1, source_target_pairs={{0,16},{16,0},{32,48},{48,32},{64,80},{80,64},{96,112},{112,96},{1... | collective-permute-start | bytes 786440 | tf_op jit(solution)/shard_map/ppermute | solution.py:32
  191.8 8.7 %collective-permute-start.36 = (bf16[512,256]{1,0:T(8,128)(2,1)S(1)}, bf16[512,256]{1,0:T(8,128)(2,1)S(1)}, u32[]{:S(2)}, u32[]{:S(2)}) collective-permute-start(bf16[512,256]{1,0:T(8,128)(2,1)S(1)} %collective-permute-done.32), channel_id=1, source_target_pairs={{0,32},{16,48},{32,64},{48,80},{64,96},{80,112},{96,0},{112,16},{1... | collective-permute-start | bytes 786440 | tf_op jit(solution)/shard_map/ppermute | solution.py:32
  192.2 12.3 %collective-permute-start.35 = (bf16[512,256]{1,0:T(8,128)(2,1)S(1)}, bf16[512,256]{1,0:T(8,128)(2,1)S(1)}, u32[]{:S(2)}, u32[]{:S(2)}) collective-permute-start(bf16[512,256]{1,0:T(8,128)(2,1)S(1)} %collective-permute-done.33), channel_id=1, source_target_pairs={{0,96},{16,112},{32,0},{48,16},{64,32},{80,48},{96,64},{112,80},{1... | collective-permute-start | bytes 786440 | tf_op jit(solution)/shard_map/ppermute | solution.py:32
  (30 other events, 629.3 us)

commit v2 on v1

v2 whole, which is shorter than its diff:
```python
import functools

import jax
import jax.numpy as jnp
from jax import lax
from jax.experimental import pallas as pl
from jax.experimental.pallas import tpu as pltpu
from jax.sharding import PartitionSpec as P

epsilon = 1e-06
mix_alpha = 0.8

BLK = 128
N_X, N_Y = 4, 4
N_ROW, N_COL = 8, 16
DEV_BLOCKS = 4
PANEL_BLOCKS = N_ROW * DEV_BLOCKS
DEST = 8
CHUNKS = 1
CHUNK_BLOCKS = DEV_BLOCKS // CHUNKS
PART_BLOCKS = DEST * CHUNK_BLOCKS
UNROLL = 8


def row_of(x, z_lo):
    return (x % N_X) * 2 + z_lo


def col_of(y, z_hi, core):
    return ((y % N_Y) * 2 + z_hi) * 2 + core


def shift_row(value, dx, dz):
    perm = [(row_of(x, z), row_of(x + dx, z ^ dz)) for x in range(N_X) for z in range(2)]
    return lax.ppermute(value, "row", perm)


def shift_col(value, dy, dz, dc):
    perm = [
        (col_of(y, z, c), col_of(y + dy, z ^ dz, c ^ dc))
        for y in range(N_Y)
        for z in range(2)
        for c in range(2)
    ]
    return lax.ppermute(value, "col", perm)


def gather_row(own, first_block=0):
    half = own.shape[0] // 2
    from_z = shift_row(own, 0, 1)
    from_left = shift_row(own, 1, 0)
    from_right = shift_row(own, -1, 0)
    far = shift_row(from_right, -1, 0)
    left_z = shift_row(from_z, 1, 0)
    right_z = shift_row(from_right, 0, 1)
    far_z_top = shift_row(left_z[:half], 1, 0)
    far_z_bottom = shift_row(right_z[half:], -1, 0)
    placed = [
        (0, own),
        (1, from_z),
        (2, from_right),
        (3, right_z),
        (4, far),
        (5, far_z_top),
        (6, from_left),
        (7, left_z),
    ]
    out = [(at * DEV_BLOCKS + first_block, piece) for at, piece in placed]
    out.append((5 * DEV_BLOCKS + first_block + half // BLK, far_z_bottom))
    return out


def add(*values):
    total = values[0].astype(jnp.float32)
    for value in values[1:]:
        total = total + value.astype(jnp.float32)
    return total


def scatter_col(send, keep):
    got = shift_col(send, 0, 0, 1)

    def pair(dy, dz, *more):
        at = dy * 2 + dz
        return add(keep[at], got[at], *more)

    low = jnp.bfloat16
    far_up = shift_col(pair(2, 0).astype(low), 1, 0, 0)
    far_down = shift_col(pair(2, 1).astype(low), -1, 0, 0)
    direct_up = shift_col(pair(1, 1).astype(low), 1, 0, 0)
    direct_down = shift_col(pair(3, 0).astype(low), -1, 0, 0)
    relay_up = shift_col(pair(1, 0, far_up).astype(low), 1, 0, 0)
    relay_down = shift_col(pair(3, 1, far_down).astype(low), -1, 0, 0)
    other = pair(0, 1, relay_down, direct_up).astype(low)
    from_other = shift_col(other, 0, 1, 0)
    return pair(0, 0, relay_up, direct_down, from_other)


def params(mib):
    return pltpu.CompilerParams(vmem_limit_bytes=mib * 1024 * 1024)


any_spec = pl.BlockSpec(memory_space=pl.ANY)
smem_spec = pl.BlockSpec(memory_space=pltpu.SMEM)
vmem_spec = pl.BlockSpec(memory_space=pltpu.VMEM)


def preload_kernel(source, target, sem):
    copy = pltpu.make_async_copy(source, target, sem)
    copy.start()
    copy.wait()


def preload(vals):
    return pl.pallas_call(
        preload_kernel,
        out_shape=pltpu.VMEM(vals.shape, vals.dtype),
        in_specs=[pl.BlockSpec(memory_space=pltpu.HBM)],
        out_specs=vmem_spec,
        scratch_shapes=[pltpu.SemaphoreType.DMA(())],
        compiler_params=params(16),
        cost_estimate=pl.CostEstimate(flops=0, bytes_accessed=2 * vals.size, transcendentals=0),
        name="load_blocks",
    )(vals)


def start_panel(pieces, starts, panel, sems):
    copies = []
    for index, (piece, start) in enumerate(zip(pieces, starts)):
        where = panel.at[pl.ds(start, piece.shape[0]), :, pl.ds(0, piece.shape[2])]
        copies.append(pltpu.make_async_copy(piece, where, sems.at[index]))
    for copy in copies:
        copy.start()
    return copies


def panel_kernel(starts, fill, *refs):
    pieces = refs[: len(starts)]
    panel, sems = refs[len(starts) :]
    copies = start_panel(pieces, starts, panel, sems)
    panel[PANEL_BLOCKS] = jnp.zeros(panel.shape[1:], panel.dtype)
    width = pieces[0].shape[2]
    if fill:

        @pl.loop(0, PANEL_BLOCKS)
        def _(block):
            panel[block, :, width:] = jnp.ones((BLK, panel.shape[2] - width), panel.dtype)

    for copy in copies:
        copy.wait()


def make_panel(placed, fill):
    starts = [start for start, _ in placed]
    pieces = [piece.reshape(-1, BLK, piece.shape[-1]) for _, piece in placed]
    width = pieces[0].shape[-1] + (BLK if fill else 0)
    return pl.pallas_call(
        functools.partial(panel_kernel, starts, fill),
        out_shape=pltpu.VMEM((PANEL_BLOCKS + 1, BLK, width), jnp.bfloat16),
        in_specs=[any_spec] * len(pieces),
        out_specs=vmem_spec,
        scratch_shapes=[pltpu.SemaphoreType.DMA((len(pieces),))],
        compiler_params=params(16),
        name="panel",
    )(*pieces)


def spmm_kernel(with_degree, part, count_ref, first_ref, second_ref, panel, vals, out_ref, *refs):
    total = refs[0]
    width = out_ref.shape[-1]

    @pl.loop(0, PART_BLOCKS)
    def _(block):
        total[block] = jnp.zeros(total.shape[1:], jnp.float32)

    @pl.loop(0, (count_ref[part] + UNROLL - 1) // UNROLL)
    def _(group):
        for u in range(UNROLL):
            first = first_ref[part, group * UNROLL + u]
            second = second_ref[part, group * UNROLL + u]
            row = lax.shift_right_logical(first, 15)
            col_a = lax.shift_right_logical(first, 9) & 63
            col_b = lax.shift_right_logical(second, 9) & 63
            left = jnp.concatenate([vals[first & 511], vals[second & 511]], axis=1)
            right = jnp.concatenate([panel[col_a], panel[col_b]], axis=0)
            total[row] += jnp.dot(left, right, preferred_element_type=jnp.float32)

    if with_degree:
        degree = refs[1]
        degree[...] = jnp.zeros(degree.shape, jnp.float32)
        eye = lax.broadcasted_iota(jnp.int32, (BLK, BLK), 0) == lax.broadcasted_iota(
            jnp.int32, (BLK, BLK), 1
        )

    @pl.loop(0, DEST)
    def _(dest):
        for j in range(CHUNK_BLOCKS):
            block = dest * CHUNK_BLOCKS + j
            out_ref[dest, pl.ds(j * BLK, BLK), :] = total[block, :, :width].astype(out_ref.dtype)
            if with_degree:
                spread = jnp.where(eye, total[block, :, width:], 0.0)
                degree[j : j + 1, :] = jnp.sum(spread, axis=0, keepdims=True)
        if with_degree:
            out_ref[dest, pl.ds(CHUNK_BLOCKS * BLK, 16), :] = degree[...].astype(out_ref.dtype)


def spmm(panel, vals, plan, part, with_degree):
    wide = panel.shape[2]
    width = wide - BLK if with_degree else wide
    rows = CHUNK_BLOCKS * BLK + (16 if with_degree else 0)
    scratch = [pltpu.VMEM((PART_BLOCKS, BLK, wide), jnp.float32)]
    if with_degree:
        scratch.append(pltpu.VMEM((16, BLK), jnp.float32))
    return pl.pallas_call(
        functools.partial(spmm_kernel, with_degree, part),
        out_shape=jax.ShapeDtypeStruct((DEST, rows, width), jnp.bfloat16),
        in_specs=[smem_spec] * 3 + [vmem_spec] * 2,
        out_specs=vmem_spec,
        scratch_shapes=scratch,
        compiler_params=params(16),
        cost_estimate=pl.CostEstimate(
            flops=2 * 208 * BLK * 256 * 256 // CHUNKS,
            bytes_accessed=4 * 1024 * 1024 // CHUNKS,
            transcendentals=0,
        ),
        name="product_keep" if part % 2 else "product_send",
    )(*plan, panel, vals)


def score_kernel(starts, pair_ref, own, target, attributes, w_attr, attr_bias, *refs):
    pieces = refs[: len(starts)]
    out_ref, panel, sems = refs[len(starts) :]
    copies = start_panel(pieces, starts, panel, sems)
    scale = own.shape[1] ** (-0.5)
    n_pair = pair_ref.shape[1]

    def row_mean(squares, count):
        return jnp.sum(squares.T, axis=0, keepdims=True) / count

    errors = []
    for block in range(DEV_BLOCKS):
        rows = pl.ds(block * BLK, BLK)
        rebuilt = jnp.dot(own[rows, :], w_attr[...], preferred_element_type=jnp.float32)
        gap = rebuilt + attr_bias[...] - attributes[rows, :].astype(jnp.float32)
        errors.append(jnp.sqrt(row_mean(gap * gap, gap.shape[1]) + epsilon))
    for copy in copies:
        copy.wait()
    for block in range(DEV_BLOCKS):
        rows = pl.ds(block * BLK, BLK)
        squares = jnp.zeros((BLK, BLK), jnp.float32)
        for pair in range(n_pair):
            logits = lax.dot_general(
                own[rows, :],
                panel[pair_ref[block, pair]],
                (((1,), (1,)), ((), ())),
                preferred_element_type=jnp.float32,
            )
            gap = jax.nn.sigmoid(logits * scale) - target[rows, pl.ds(pair * BLK, BLK)].astype(
                jnp.float32
            )
            squares = squares + gap * gap
        struct = jnp.sqrt(row_mean(squares, n_pair * BLK) + epsilon)
        out_ref[block : block + 1, :] = mix_alpha * errors[block] + (1.0 - mix_alpha) * struct


def score(placed, pairs, own, target, attributes, w_attr, attr_bias):
    starts = [start for start, _ in placed]
    pieces = [piece.reshape(-1, BLK, piece.shape[-1]) for _, piece in placed]
    out = pl.pallas_call(
        functools.partial(score_kernel, starts),
        out_shape=jax.ShapeDtypeStruct((DEV_BLOCKS, BLK), jnp.float32),
        in_specs=[smem_spec] + [vmem_spec] * 5 + [any_spec] * len(pieces),
        out_specs=vmem_spec,
        scratch_shapes=[
            pltpu.VMEM((PANEL_BLOCKS, BLK, own.shape[1]), jnp.bfloat16),
            pltpu.SemaphoreType.DMA((len(pieces),)),
        ],
        compiler_params=params(16),
        name="score",
    )(pairs, own, target, attributes, w_attr, attr_bias, *pieces)
    return out.reshape(-1)


def make_plan(row_ids, col_ids, live_count, row_at, col_at):
    capacity = row_ids.shape[0]
    parts = 2 * CHUNKS
    slots = jnp.arange(capacity, dtype=jnp.int32)
    live = slots < live_count
    y, z_hi, core = col_at // 4, (col_at // 2) % 2, col_at % 2
    dest, j = row_ids // DEV_BLOCKS, row_ids % DEV_BLOCKS
    dy = (dest // 4 - y) % N_Y
    dz = (dest // 2 + z_hi) % 2
    dc = (dest + core) % 2
    part = (j // CHUNK_BLOCKS) * 2 + 1 - dc
    row = (dy * 2 + dz) * CHUNK_BLOCKS + j % CHUNK_BLOCKS
    key = part * PART_BLOCKS + row
    col = relative_block(col_ids, row_at)
    same = (key[:, None] == key[None, :]) & live[None, :]
    within = jnp.sum((same & (slots[None, :] < slots[:, None])).astype(jnp.int32), axis=1)
    opens = live & (within % 2 == 0)
    ahead = (key[None, :] < key[:, None]) & (part[None, :] == part[:, None]) & opens[None, :]
    pair = jnp.sum(ahead.astype(jnp.int32), axis=1) + within // 2
    longest = -(-((capacity + PART_BLOCKS) // 2) // UNROLL) * UNROLL
    place = jnp.where(live, (part * longest + pair) * 2 + within % 2, -1)
    places = jnp.arange(parts * longest, dtype=jnp.int32)
    empty = PANEL_BLOCKS * 512
    word = slots + col * 512 + row * (512 * 64) - empty

    def lay(side):
        hit = place[None, :] == (places * 2 + side)[:, None]
        return (empty + jnp.sum(jnp.where(hit, word[None, :], 0), axis=1)).reshape(parts, longest)

    count = jnp.sum(
        (opens[None, :] & (part[None, :] == jnp.arange(parts)[:, None])).astype(jnp.int32), axis=1
    )
    return count, lay(0), lay(1)


def relative_block(ids, row_at):
    owner, j = ids // DEV_BLOCKS, ids % DEV_BLOCKS
    dx = (owner // 2 - row_at // 2) % N_X
    return (dx * 2 + (owner + row_at) % 2) * DEV_BLOCKS + j


def per_device(
    attributes,
    adj_values,
    adj_rows,
    adj_cols,
    adj_count,
    pair_ids,
    struct_target,
    w_first,
    w_rest,
    layer_bias,
    w_attr,
    attr_bias,
):
    vals = preload(adj_values[0, 0])
    hidden_size = w_rest.shape[1]
    row_at = lax.axis_index("row")
    col_at = lax.axis_index("col")
    plan = make_plan(adj_rows[0, 0], adj_cols[0, 0], adj_count[0, 0], row_at, col_at)
    chunk = CHUNK_BLOCKS * BLK
    w_near, w_self = w_first[:, :hidden_size], w_first[:, hidden_size:]
    own_part = jnp.dot(attributes, w_self, preferred_element_type=jnp.float32)

    panel = make_panel(gather_row(attributes), True)
    placed, scales, own_second = [], [], []
    products = [spmm(panel, vals, plan, part, True) for part in range(2 * CHUNKS)]
    for c in range(CHUNKS):
        summed = scatter_col(products[2 * c], products[2 * c + 1])
        degree = 1.0 + summed[chunk : chunk + CHUNK_BLOCKS].reshape(-1)
        row_scale = lax.rsqrt(degree)[:, None]
        aggregate = summed[:chunk]
        coarse = lax.reduce_precision(aggregate, 8, 7)
        fine = (aggregate - coarse).astype(jnp.bfloat16)
        coarse = coarse.astype(jnp.bfloat16)
        mixed = jnp.dot(coarse, w_near, preferred_element_type=jnp.float32) + jnp.dot(
            fine, w_near, preferred_element_type=jnp.float32
        )
        before = row_scale * mixed + own_part[c * chunk : (c + 1) * chunk]
        hidden = jnp.tanh(before).astype(jnp.bfloat16)
        features = jnp.dot(
            hidden, w_rest[0][:, :hidden_size], preferred_element_type=jnp.float32
        ).astype(jnp.bfloat16)
        placed += gather_row(features, c * CHUNK_BLOCKS)
        scales.append(row_scale)
        own_second.append(
            jnp.dot(hidden, w_rest[0][:, hidden_size:], preferred_element_type=jnp.float32)
            + layer_bias[0]
        )

    panel = make_panel(placed, False)
    placed, embedding = [], []
    products = [spmm(panel, vals, plan, part, False) for part in range(2 * CHUNKS)]
    for c in range(CHUNKS):
        summed = scatter_col(products[2 * c], products[2 * c + 1])
        hidden = jnp.tanh(scales[c] * summed + own_second[c]).astype(jnp.bfloat16)
        embedding.append(hidden)
        placed += gather_row(hidden, c * CHUNK_BLOCKS)

    return score(
        placed,
        relative_block(pair_ids, row_at),
        jnp.concatenate(embedding),
        struct_target.reshape(struct_target.shape[0], -1),
        attributes,
        w_attr,
        attr_bias[None, :],
    )


def solution(mesh):
    return jax.shard_map(
        per_device,
        mesh=mesh,
        in_specs=(
            P(("row", "col"), None),
            P("row", "col", None, None, None),
            P("row", "col", None),
            P("row", "col", None),
            P("row", "col"),
            P(("row", "col"), None),
            P(("row", "col"), None, None),
            P(),
            P(),
            P(),
            P(),
            P(),
        ),
        out_specs=P(("row", "col")),
        check_vma=False,
    )
```

time: 215 us -> 154 us (0.72)
  Pallas kernels: 73.9 us -> 26 us
  local copies, waits for them, and re-layouts: 14.7 us -> 4.91 us
  waiting for transfers between devices: 50.6 us -> 58.1 us
  starting transfers between devices: 62.8 us -> 57 us
  other arithmetic: 8.97 us -> 3.84 us
    pallas_call x4 -> x8, Pallas kernels: 73.9 us -> 26 us  [the longest x4 21.6 us: spmm(): pl.pallas_call(functools.partial(spmm_kernel, with_degree, part), out_sha...]
    unnamed x36 -> x19, local copies, waits for them, and re-layouts: 11.6 us -> 4.7 us
    ppermute x24, waiting for transfers between devices: 23.2 us -> 29.9 us  [shift_row(): return lax.ppermute(value, 'row', perm)]
    ppermute x16, starting transfers between devices: 27.1 us -> 23.3 us  [shift_col(): return lax.ppermute(value, 'col', perm)]
    gather x1 -> x0, local copies, waits for them, and re-layouts: 2.2 us -> none  [per_device(): jnp.take(whole, relative_block(pair_ids, row_at // 2, row_at % 2), axis=0)]
  transfers between devices with their start and end apart: 40 -> 40, of which waited for: 18 -> 19; matrix products, arithmetic and copies ran while one was open for 5% -> 2% of each run, Pallas kernels for 18% -> 8%
where the time goes in v2:
time: 154 us; the launch traced here: 152 us
  waiting for transfers between devices  58.1 us (38%)
  starting transfers between devices  57 us (37%)
  Pallas kernels  26 us (17%)
  local copies, waits for them, and re-layouts  4.91 us (3%)
  other arithmetic  3.84 us (2%)
    ppermute x24, starting transfers between devices, shift_row(): return lax.ppermute(value, 'row', perm)  33.7 us
    ppermute x24, waiting for transfers between devices, shift_row(): return lax.ppermute(value, 'row', perm)  29.9 us
    ppermute x16, waiting for transfers between devices, shift_col(): return lax.ppermute(value, 'col', perm)  28.2 us
    ppermute x16, starting transfers between devices, shift_col(): return lax.ppermute(value, 'col', perm)  23.3 us
    pallas_call x4, Pallas kernels, spmm(): pl.pallas_call(functools.partial(spmm_kernel, with_degree, part), out_sha...  21.6 us
    unnamed x19, local copies, waits for them, and re-layouts  4.7 us
  transfers between devices with their start and end apart: 40, of which 19 were waited for; matrix products, arithmetic and copies ran while one was open for 2% of the time, Pallas kernels for 8%

profile of v2, /device:TPU:0, one launch (start us, length us, event | category | flops | bytes accessed | tf_op | source)
XLA Modules:
  0.0 152.2 jit_solution(17980158484287282401)
XLA Ops:
  0.0 2.8 %collective-permute-start.1 = (bf16[512,128]{1,0:T(8,128)(2,1)}, bf16[512,128]{1,0:T(8,128)(2,1)S(1)}, u32[]{:S(2)}, u32[]{:S(2)}) collective-permute-start(bf16[512,128]{1,0:T(8,128)(2,1)} %attributes.1), channel_id=1, source_target_pairs={{0,96},{16,112},{32,0},{48,16},{64,32},{80,48},{96,64},{112,80},{1... | collective-permute-start | bytes 393224 | tf_op jit(solution)/shard_map/ppermute | solution.py:35
  8.1 3.4 %collective-permute-start.3 = (bf16[512,128]{1,0:T(8,128)(2,1)S(1)}, bf16[512,128]{1,0:T(8,128)(2,1)S(1)}, u32[]{:S(2)}, u32[]{:S(2)}) collective-permute-start(bf16[512,128]{1,0:T(8,128)(2,1)S(1)} %collective-permute-done.1), channel_id=1, source_target_pairs={{0,96},{16,112},{32,0},{48,16},{64,32},{80,48},{96,64},{112,80},{1... | collective-permute-start | bytes 393224 | tf_op jit(solution)/shard_map/ppermute | solution.py:35
  11.6 4.6 %copy-done = bf16[1,1,384,128,128]{4,3,2,1,0:T(8,128)(2,1)S(1)} copy-done((bf16[1,1,384,128,128]{4,3,2,1,0:T(8,128)(2,1)S(1)}, bf16[1,1,384,128,128]{4,3,2,1,0:T(8,128)(2,1)}, u32[]{:S(2)}) %copy-start) | copy-done | bytes 12582936
  17.1 3.3 %collective-permute-start.7 = (bf16[256,128]{1,0:T(8,128)(2,1)S(1)}, bf16[256,128]{1,0:T(8,128)(2,1)S(1)}, u32[]{:S(2)}, u32[]{:S(2)}) collective-permute-start(bf16[256,128]{1,0:T(8,128)(2,1)S(1)} %slice.177), channel_id=1, source_target_pairs={{0,96},{16,112},{32,0},{48,16},{64,32},{80,48},{96,64},{112,80},{1... | collective-permute-start | bytes 196616 | tf_op jit(solution)/shard_map/ppermute | solution.py:35
  22.3 3.7 %collective-permute-done.5 = bf16[256,128]{1,0:T(8,128)(2,1)S(1)} collective-permute-done((bf16[256,128]{1,0:T(8,128)(2,1)S(1)}, bf16[256,128]{1,0:T(8,128)(2,1)S(1)}, u32[]{:S(2)}, u32[]{:S(2)}) %collective-permute-start.5) | collective-permute-done | bytes 65568 | tf_op jit(solution)/shard_map/ppermute | solution.py:35
  26.4 5.3 %product_send.2 = bf16[8,528,128]{2,1,0:T(8,128)(2,1)S(1)} custom-call(s32[2]{0:T(128)S(1)} %fusion.36.count_ref, s32[2,208]{1,0:T(2,128)S(1)} %add.621.first_ref, s32[2,208]{1,0:T(2,128)S(1)} %add.625.second_ref, bf16[33,128,256]{2,1,0:T(8,128)(2,1)S(1)} %panel.2, bf16[384,128,128]{2,1,0:T(8,128)(2,1)S(1)} %load_blocks.1.vals), custom_call_target="tpu_custom_call" | custom-call | flops 3489660928 | bytes 4194304 | tf_op jit(solution)/shard_map/product_send/pallas_call | solution.py:214
  31.7 5.6 %product_keep.2 = bf16[8,528,128]{2,1,0:T(8,128)(2,1)S(1)} custom-call(s32[2]{0:T(128)S(1)} %fusion.36.count_ref, s32[2,208]{1,0:T(2,128)S(1)} %add.621.first_ref, s32[2,208]{1,0:T(2,128)S(1)} %add.625.second_ref, bf16[33,128,256]{2,1,0:T(8,128)(2,1)S(1)} %panel.2, bf16[384,128,128]{2,1,0:T(8,128)(2,1)S(1)} %load_blocks.1.vals), custom_call_target="tpu_custom_call" | custom-call | flops 3489660928 | bytes 4194304 | tf_op jit(solution)/shard_map/product_keep/pallas_call | solution.py:214
  48.7 3.0 %collective-permute-done.13 = bf16[528,128]{1,0:T(8,128)(2,1)S(1)} collective-permute-done((bf16[528,128]{1,0:T(8,128)(2,1)S(1)}, bf16[528,128]{1,0:T(8,128)(2,1)S(1)}, u32[]{:S(2)}, u32[]{:S(2)}) %collective-permute-start.13) | collective-permute-done | bytes 135200 | tf_op jit(solution)/shard_map/ppermute | solution.py:45
  51.8 4.2 %collective-permute-start.15 = (bf16[528,128]{1,0:T(8,128)(2,1)S(1)}, bf16[528,128]{1,0:T(8,128)(2,1)S(1)}, u32[]{:S(2)}, u32[]{:S(2)}) collective-permute-start(bf16[528,128]{1,0:T(8,128)(2,1)S(1)} %fusion.16), channel_id=1, source_target_pairs={{0,2},{1,3},{2,0},{3,1},{4,6},{5,7},{6,4},{7,5},{8,10},{9,11},{10,... | collective-permute-start | bytes 405512 | tf_op jit(solution)/shard_map/ppermute | solution.py:45
  56.1 4.0 %collective-permute-done.15 = bf16[528,128]{1,0:T(8,128)(2,1)S(1)} collective-permute-done((bf16[528,128]{1,0:T(8,128)(2,1)S(1)}, bf16[528,128]{1,0:T(8,128)(2,1)S(1)}, u32[]{:S(2)}, u32[]{:S(2)}) %collective-permute-start.15) | collective-permute-done | bytes 135200 | tf_op jit(solution)/shard_map/ppermute | solution.py:45
  61.9 8.2 %collective-permute-done.16 = bf16[512,256]{1,0:T(8,128)(2,1)S(1)} collective-permute-done((bf16[512,256]{1,0:T(8,128)(2,1)S(1)}, bf16[512,256]{1,0:T(8,128)(2,1)S(1)}, u32[]{:S(2)}, u32[]{:S(2)}) %collective-permute-start.16) | collective-permute-done | bytes 262176 | tf_op jit(solution)/shard_map/ppermute | solution.py:35
  71.9 3.2 %collective-permute-start.19 = (bf16[512,256]{1,0:T(8,128)(2,1)S(1)}, bf16[512,256]{1,0:T(8,128)(2,1)S(1)}, u32[]{:S(2)}, u32[]{:S(2)}) collective-permute-start(bf16[512,256]{1,0:T(8,128)(2,1)S(1)} %collective-permute-done.17), channel_id=1, source_target_pairs={{0,96},{16,112},{32,0},{48,16},{64,32},{80,48},{96,64},{112,80},{1... | collective-permute-start | bytes 786440 | tf_op jit(solution)/shard_map/ppermute | solution.py:35
  77.8 3.3 %collective-permute-start.23 = (bf16[256,256]{1,0:T(8,128)(2,1)S(1)}, bf16[256,256]{1,0:T(8,128)(2,1)S(1)}, u32[]{:S(2)}, u32[]{:S(2)}) collective-permute-start(bf16[256,256]{1,0:T(8,128)(2,1)S(1)} %slice.198), channel_id=1, source_target_pairs={{0,96},{16,112},{32,0},{48,16},{64,32},{80,48},{96,64},{112,80},{1... | collective-permute-start | bytes 393224 | tf_op jit(solution)/shard_map/ppermute | solution.py:35
  81.1 2.8 %collective-permute-done.21 = bf16[256,256]{1,0:T(8,128)(2,1)S(1)} collective-permute-done((bf16[256,256]{1,0:T(8,128)(2,1)S(1)}, bf16[256,256]{1,0:T(8,128)(2,1)S(1)}, u32[]{:S(2)}, u32[]{:S(2)}) %collective-permute-start.21) | collective-permute-done | bytes 131104 | tf_op jit(solution)/shard_map/ppermute | solution.py:35
  84.5 5.3 %product_send.3 = bf16[8,512,256]{2,1,0:T(8,128)(2,1)S(1)} custom-call(s32[2]{0:T(128)S(1)} %fusion.36.count_ref, s32[2,208]{1,0:T(2,128)S(1)} %add.621.first_ref, s32[2,208]{1,0:T(2,128)S(1)} %add.625.second_ref, bf16[33,128,256]{2,1,0:T(8,128)(2,1)S(1)} %panel.3, bf16[384,128,128]{2,1,0:T(8,128)(2,1)S(1)} %load_blocks.1.vals), custom_call_target="tpu_custom_call" | custom-call | flops 3489660928 | bytes 4194304 | tf_op jit(solution)/shard_map/product_send/pallas_call | solution.py:214
  89.9 5.4 %product_keep.3 = bf16[8,512,256]{2,1,0:T(8,128)(2,1)S(1)} custom-call(s32[2]{0:T(128)S(1)} %fusion.36.count_ref, s32[2,208]{1,0:T(2,128)S(1)} %add.621.first_ref, s32[2,208]{1,0:T(2,128)S(1)} %add.625.second_ref, bf16[33,128,256]{2,1,0:T(8,128)(2,1)S(1)} %panel.3, bf16[384,128,128]{2,1,0:T(8,128)(2,1)S(1)} %load_blocks.1.vals), custom_call_target="tpu_custom_call" | custom-call | flops 3489660928 | bytes 4194304 | tf_op jit(solution)/shard_map/product_keep/pallas_call | solution.py:214
  99.0 7.1 %collective-permute-done.25 = bf16[512,256]{1,0:T(8,128)(2,1)S(1)} collective-permute-done((bf16[512,256]{1,0:T(8,128)(2,1)S(1)}, bf16[512,256]{1,0:T(8,128)(2,1)S(1)}, u32[]{:S(2)}, u32[]{:S(2)}) %collective-permute-start.25) | collective-permute-done | bytes 262176 | tf_op jit(solution)/shard_map/ppermute | solution.py:45
  111.3 4.4 %collective-permute-done.29 = bf16[512,256]{1,0:T(8,128)(2,1)S(1)} collective-permute-done((bf16[512,256]{1,0:T(8,128)(2,1)S(1)}, bf16[512,256]{1,0:T(8,128)(2,1)S(1)}, u32[]{:S(2)}, u32[]{:S(2)}) %collective-permute-start.29) | collective-permute-done | bytes 262176 | tf_op jit(solution)/shard_map/ppermute | solution.py:45
  115.8 3.6 %collective-permute-start.31 = (bf16[512,256]{1,0:T(8,128)(2,1)S(1)}, bf16[512,256]{1,0:T(8,128)(2,1)S(1)}, u32[]{:S(2)}, u32[]{:S(2)}) collective-permute-start(bf16[512,256]{1,0:T(8,128)(2,1)S(1)} %fusion.6), channel_id=1, source_target_pairs={{0,2},{1,3},{2,0},{3,1},{4,6},{5,7},{6,4},{7,5},{8,10},{9,11},{10,... | collective-permute-start | bytes 786440 | tf_op jit(solution)/shard_map/ppermute | solution.py:45
  119.7 5.7 %collective-permute-done.31 = bf16[512,256]{1,0:T(8,128)(2,1)S(1)} collective-permute-done((bf16[512,256]{1,0:T(8,128)(2,1)S(1)}, bf16[512,256]{1,0:T(8,128)(2,1)S(1)}, u32[]{:S(2)}, u32[]{:S(2)}) %collective-permute-start.31) | collective-permute-done | bytes 262176 | tf_op jit(solution)/shard_map/ppermute | solution.py:45
  125.7 4.6 %collective-permute-start.33 = (bf16[512,256]{1,0:T(8,128)(2,1)S(1)}, bf16[512,256]{1,0:T(8,128)(2,1)S(1)}, u32[]{:S(2)}, u32[]{:S(2)}) collective-permute-start(bf16[512,256]{1,0:T(8,128)(2,1)S(1)} %fusion.13.own), channel_id=1, source_target_pairs={{0,96},{16,112},{32,0},{48,16},{64,32},{80,48},{96,64},{112,80},{1... | collective-permute-start | bytes 786440 | tf_op jit(solution)/shard_map/ppermute | solution.py:35
  130.2 4.6 %collective-permute-done.32 = bf16[512,256]{1,0:T(8,128)(2,1)S(1)} collective-permute-done((bf16[512,256]{1,0:T(8,128)(2,1)S(1)}, bf16[512,256]{1,0:T(8,128)(2,1)S(1)}, u32[]{:S(2)}, u32[]{:S(2)}) %collective-permute-start.32) | collective-permute-done | bytes 262176 | tf_op jit(solution)/shard_map/ppermute | solution.py:35
  137.4 3.7 %collective-permute-start.35 = (bf16[512,256]{1,0:T(8,128)(2,1)S(1)}, bf16[512,256]{1,0:T(8,128)(2,1)S(1)}, u32[]{:S(2)}, u32[]{:S(2)}) collective-permute-start(bf16[512,256]{1,0:T(8,128)(2,1)S(1)} %collective-permute-done.33), channel_id=1, source_target_pairs={{0,96},{16,112},{32,0},{48,16},{64,32},{80,48},{96,64},{112,80},{1... | collective-permute-start | bytes 786440 | tf_op jit(solution)/shard_map/ppermute | solution.py:35
  143.2 3.8 %collective-permute-start.39 = (bf16[256,256]{1,0:T(8,128)(2,1)S(1)}, bf16[256,256]{1,0:T(8,128)(2,1)S(1)}, u32[]{:S(2)}, u32[]{:S(2)}) collective-permute-start(bf16[256,256]{1,0:T(8,128)(2,1)S(1)} %slice.217), channel_id=1, source_target_pairs={{0,96},{16,112},{32,0},{48,16},{64,32},{80,48},{96,64},{112,80},{1... | collective-permute-start | bytes 393224 | tf_op jit(solution)/shard_map/ppermute | solution.py:35
  (120 shorter events, 45.5 us)
Async XLA Ops:
  2.8 8.6 %collective-permute-start = (bf16[512,128]{1,0:T(8,128)(2,1)}, bf16[512,128]{1,0:T(8,128)(2,1)S(1)}, u32[]{:S(2)}, u32[]{:S(2)}) collective-permute-start(bf16[512,128]{1,0:T(8,128)(2,1)} %attributes.1), channel_id=1, source_target_pairs={{0,16},{16,0},{32,48},{48,32},{64,80},{80,64},{96,112},{112,96},{1... | collective-permute-start | bytes 393224 | tf_op jit(solution)/shard_map/ppermute | solution.py:35
  4.8 15.8 %collective-permute-start.6 = (bf16[512,128]{1,0:T(8,128)(2,1)}, bf16[512,128]{1,0:T(8,128)(2,1)S(1)}, u32[]{:S(2)}, u32[]{:S(2)}) collective-permute-start(bf16[512,128]{1,0:T(8,128)(2,1)} %attributes.1), channel_id=1, source_target_pairs={{0,32},{16,48},{32,64},{48,80},{64,96},{80,112},{96,0},{112,16},{1... | collective-permute-start | bytes 393224 | tf_op jit(solution)/shard_map/ppermute | solution.py:35
  7.9 9.2 %collective-permute-start.2 = (bf16[512,128]{1,0:T(8,128)(2,1)S(1)}, bf16[512,128]{1,0:T(8,128)(2,1)S(1)}, u32[]{:S(2)}, u32[]{:S(2)}) collective-permute-start(bf16[512,128]{1,0:T(8,128)(2,1)S(1)} %collective-permute-done.1), channel_id=1, source_target_pairs={{0,16},{16,0},{32,48},{48,32},{64,80},{80,64},{96,112},{112,96},{1... | collective-permute-start | bytes 393224 | tf_op jit(solution)/shard_map/ppermute | solution.py:35
  8.1 12.5 %collective-permute-start.3 = (bf16[512,128]{1,0:T(8,128)(2,1)S(1)}, bf16[512,128]{1,0:T(8,128)(2,1)S(1)}, u32[]{:S(2)}, u32[]{:S(2)}) collective-permute-start(bf16[512,128]{1,0:T(8,128)(2,1)S(1)} %collective-permute-done.1), channel_id=1, source_target_pairs={{0,96},{16,112},{32,0},{48,16},{64,32},{80,48},{96,64},{112,80},{1... | collective-permute-start | bytes 393224 | tf_op jit(solution)/shard_map/ppermute | solution.py:35
  11.4 8.9 %collective-permute-start.4 = (bf16[512,128]{1,0:T(8,128)(2,1)S(1)}, bf16[512,128]{1,0:T(8,128)(2,1)S(1)}, u32[]{:S(2)}, u32[]{:S(2)}) collective-permute-start(bf16[512,128]{1,0:T(8,128)(2,1)S(1)} %collective-permute-done), channel_id=1, source_target_pairs={{0,32},{16,48},{32,64},{48,80},{64,96},{80,112},{96,0},{112,16},{1... | collective-permute-start | bytes 393224 | tf_op jit(solution)/shard_map/ppermute | solution.py:35
  39.6 9.1 %collective-permute-start.14 = (bf16[528,128]{1,0:T(8,128)(2,1)S(1)}, bf16[528,128]{1,0:T(8,128)(2,1)S(1)}, u32[]{:S(2)}, u32[]{:S(2)}) collective-permute-start(bf16[528,128]{1,0:T(8,128)(2,1)S(1)} %get-tuple-element.20), channel_id=1, source_target_pairs={{0,4},{1,5},{2,6},{3,7},{4,8},{5,9},{6,10},{7,11},{8,12},{9,13},{1... | collective-permute-start | bytes 405512 | tf_op jit(solution)/shard_map/ppermute | solution.py:45
  46.7 9.4 %collective-permute-start.11 = (bf16[528,128]{1,0:T(8,128)(2,1)S(1)}, bf16[528,128]{1,0:T(8,128)(2,1)S(1)}, u32[]{:S(2)}, u32[]{:S(2)}) collective-permute-start(bf16[528,128]{1,0:T(8,128)(2,1)S(1)} %get-tuple-element.22), channel_id=1, source_target_pairs={{0,12},{1,13},{2,14},{3,15},{4,0},{5,1},{6,2},{7,3},{8,4},{9,5},{1... | collective-permute-start | bytes 405512 | tf_op jit(solution)/shard_map/ppermute | solution.py:45
  47.9 8.2 %collective-permute-start.10 = (bf16[528,128]{1,0:T(8,128)(2,1)S(1)}, bf16[528,128]{1,0:T(8,128)(2,1)S(1)}, u32[]{:S(2)}, u32[]{:S(2)}) collective-permute-start(bf16[528,128]{1,0:T(8,128)(2,1)S(1)} %get-tuple-element.17), channel_id=1, source_target_pairs={{0,4},{1,5},{2,6},{3,7},{4,8},{5,9},{6,10},{7,11},{8,12},{9,13},{1... | collective-permute-start | bytes 405512 | tf_op jit(solution)/shard_map/ppermute | solution.py:45
  51.8 8.2 %collective-permute-start.15 = (bf16[528,128]{1,0:T(8,128)(2,1)S(1)}, bf16[528,128]{1,0:T(8,128)(2,1)S(1)}, u32[]{:S(2)}, u32[]{:S(2)}) collective-permute-start(bf16[528,128]{1,0:T(8,128)(2,1)S(1)} %fusion.16), channel_id=1, source_target_pairs={{0,2},{1,3},{2,0},{3,1},{4,6},{5,7},{6,4},{7,5},{8,10},{9,11},{10,... | collective-permute-start | bytes 405512 | tf_op jit(solution)/shard_map/ppermute | solution.py:45
  61.0 9.0 %collective-permute-start.16 = (bf16[512,256]{1,0:T(8,128)(2,1)S(1)}, bf16[512,256]{1,0:T(8,128)(2,1)S(1)}, u32[]{:S(2)}, u32[]{:S(2)}) collective-permute-start(bf16[512,256]{1,0:T(8,128)(2,1)S(1)} %convolution_convert_fusion), channel_id=1, source_target_pairs={{0,16},{16,0},{32,48},{48,32},{64,80},{80,64},{96,112},{112,96},{1... | collective-permute-start | bytes 786440 | tf_op jit(solution)/shard_map/ppermute | solution.py:35
  61.1 9.0 %collective-permute-start.17 = (bf16[512,256]{1,0:T(8,128)(2,1)S(1)}, bf16[512,256]{1,0:T(8,128)(2,1)S(1)}, u32[]{:S(2)}, u32[]{:S(2)}) collective-permute-start(bf16[512,256]{1,0:T(8,128)(2,1)S(1)} %convolution_convert_fusion), channel_id=1, source_target_pairs={{0,96},{16,112},{32,0},{48,16},{64,32},{80,48},{96,64},{112,80},{1... | collective-permute-start | bytes 786440 | tf_op jit(solution)/shard_map/ppermute | solution.py:35
  71.9 9.2 %collective-permute-start.22 = (bf16[512,256]{1,0:T(8,128)(2,1)S(1)}, bf16[512,256]{1,0:T(8,128)(2,1)S(1)}, u32[]{:S(2)}, u32[]{:S(2)}) collective-permute-start(bf16[512,256]{1,0:T(8,128)(2,1)S(1)} %convolution_convert_fusion), channel_id=1, source_target_pairs={{0,32},{16,48},{32,64},{48,80},{64,96},{80,112},{96,0},{112,16},{1... | collective-permute-start | bytes 786440 | tf_op jit(solution)/shard_map/ppermute | solution.py:35
  71.9 9.2 %collective-permute-start.19 = (bf16[512,256]{1,0:T(8,128)(2,1)S(1)}, bf16[512,256]{1,0:T(8,128)(2,1)S(1)}, u32[]{:S(2)}, u32[]{:S(2)}) collective-permute-start(bf16[512,256]{1,0:T(8,128)(2,1)S(1)} %collective-permute-done.17), channel_id=1, source_target_pairs={{0,96},{16,112},{32,0},{48,16},{64,32},{80,48},{96,64},{112,80},{1... | collective-permute-start | bytes 786440 | tf_op jit(solution)/shard_map/ppermute | solution.py:35
  95.6 10.4 %collective-permute-start.25 = (bf16[512,256]{1,0:T(8,128)(2,1)S(1)}, bf16[512,256]{1,0:T(8,128)(2,1)S(1)}, u32[]{:S(2)}, u32[]{:S(2)}) collective-permute-start(bf16[512,256]{1,0:T(8,128)(2,1)S(1)} %get-tuple-element.13), channel_id=1, source_target_pairs={{0,4},{1,5},{2,6},{3,7},{4,8},{5,9},{6,10},{7,11},{8,12},{9,13},{1... | collective-permute-start | bytes 786440 | tf_op jit(solution)/shard_map/ppermute | solution.py:45
  96.1 9.9 %collective-permute-start.28 = (bf16[512,256]{1,0:T(8,128)(2,1)S(1)}, bf16[512,256]{1,0:T(8,128)(2,1)S(1)}, u32[]{:S(2)}, u32[]{:S(2)}) collective-permute-start(bf16[512,256]{1,0:T(8,128)(2,1)S(1)} %get-tuple-element.15), channel_id=1, source_target_pairs={{0,12},{1,13},{2,14},{3,15},{4,0},{5,1},{6,2},{7,3},{8,4},{9,5},{1... | collective-permute-start | bytes 786440 | tf_op jit(solution)/shard_map/ppermute | solution.py:45
  99.0 12.3 %collective-permute-start.30 = (bf16[512,256]{1,0:T(8,128)(2,1)S(1)}, bf16[512,256]{1,0:T(8,128)(2,1)S(1)}, u32[]{:S(2)}, u32[]{:S(2)}) collective-permute-start(bf16[512,256]{1,0:T(8,128)(2,1)S(1)} %get-tuple-element.14), channel_id=1, source_target_pairs={{0,4},{1,5},{2,6},{3,7},{4,8},{5,9},{6,10},{7,11},{8,12},{9,13},{1... | collective-permute-start | bytes 786440 | tf_op jit(solution)/shard_map/ppermute | solution.py:45
  106.3 9.4 %collective-permute-start.29 = (bf16[512,256]{1,0:T(8,128)(2,1)S(1)}, bf16[512,256]{1,0:T(8,128)(2,1)S(1)}, u32[]{:S(2)}, u32[]{:S(2)}) collective-permute-start(bf16[512,256]{1,0:T(8,128)(2,1)S(1)} %get-tuple-element.12), channel_id=1, source_target_pairs={{0,12},{1,13},{2,14},{3,15},{4,0},{5,1},{6,2},{7,3},{8,4},{9,5},{1... | collective-permute-start | bytes 786440 | tf_op jit(solution)/shard_map/ppermute | solution.py:45
  108.9 10.8 %collective-permute-start.27 = (bf16[512,256]{1,0:T(8,128)(2,1)S(1)}, bf16[512,256]{1,0:T(8,128)(2,1)S(1)}, u32[]{:S(2)}, u32[]{:S(2)}) collective-permute-start(bf16[512,256]{1,0:T(8,128)(2,1)S(1)} %get-tuple-element.16), channel_id=1, source_target_pairs={{0,12},{1,13},{2,14},{3,15},{4,0},{5,1},{6,2},{7,3},{8,4},{9,5},{1... | collective-permute-start | bytes 786440 | tf_op jit(solution)/shard_map/ppermute | solution.py:45
  109.0 10.7 %collective-permute-start.26 = (bf16[512,256]{1,0:T(8,128)(2,1)S(1)}, bf16[512,256]{1,0:T(8,128)(2,1)S(1)}, u32[]{:S(2)}, u32[]{:S(2)}) collective-permute-start(bf16[512,256]{1,0:T(8,128)(2,1)S(1)} %get-tuple-element.11), channel_id=1, source_target_pairs={{0,4},{1,5},{2,6},{3,7},{4,8},{5,9},{6,10},{7,11},{8,12},{9,13},{1... | collective-permute-start | bytes 786440 | tf_op jit(solution)/shard_map/ppermute | solution.py:45
  115.8 9.6 %collective-permute-start.31 = (bf16[512,256]{1,0:T(8,128)(2,1)S(1)}, bf16[512,256]{1,0:T(8,128)(2,1)S(1)}, u32[]{:S(2)}, u32[]{:S(2)}) collective-permute-start(bf16[512,256]{1,0:T(8,128)(2,1)S(1)} %fusion.6), channel_id=1, source_target_pairs={{0,2},{1,3},{2,0},{3,1},{4,6},{5,7},{6,4},{7,5},{8,10},{9,11},{10,... | collective-permute-start | bytes 786440 | tf_op jit(solution)/shard_map/ppermute | solution.py:45
  125.6 9.2 %collective-permute-start.32 = (bf16[512,256]{1,0:T(8,128)(2,1)S(1)}, bf16[512,256]{1,0:T(8,128)(2,1)S(1)}, u32[]{:S(2)}, u32[]{:S(2)}) collective-permute-start(bf16[512,256]{1,0:T(8,128)(2,1)S(1)} %fusion.13.own), channel_id=1, source_target_pairs={{0,16},{16,0},{32,48},{48,32},{64,80},{80,64},{96,112},{112,96},{1... | collective-permute-start | bytes 786440 | tf_op jit(solution)/shard_map/ppermute | solution.py:35
  125.7 11.1 %collective-permute-start.33 = (bf16[512,256]{1,0:T(8,128)(2,1)S(1)}, bf16[512,256]{1,0:T(8,128)(2,1)S(1)}, u32[]{:S(2)}, u32[]{:S(2)}) collective-permute-start(bf16[512,256]{1,0:T(8,128)(2,1)S(1)} %fusion.13.own), channel_id=1, source_target_pairs={{0,96},{16,112},{32,0},{48,16},{64,32},{80,48},{96,64},{112,80},{1... | collective-permute-start | bytes 786440 | tf_op jit(solution)/shard_map/ppermute | solution.py:35
  137.4 9.6 %collective-permute-start.38 = (bf16[512,256]{1,0:T(8,128)(2,1)S(1)}, bf16[512,256]{1,0:T(8,128)(2,1)S(1)}, u32[]{:S(2)}, u32[]{:S(2)}) collective-permute-start(bf16[512,256]{1,0:T(8,128)(2,1)S(1)} %fusion.13.own), channel_id=1, source_target_pairs={{0,32},{16,48},{32,64},{48,80},{64,96},{80,112},{96,0},{112,16},{1... | collective-permute-start | bytes 786440 | tf_op jit(solution)/shard_map/ppermute | solution.py:35
  137.4 9.6 %collective-permute-start.35 = (bf16[512,256]{1,0:T(8,128)(2,1)S(1)}, bf16[512,256]{1,0:T(8,128)(2,1)S(1)}, u32[]{:S(2)}, u32[]{:S(2)}) collective-permute-start(bf16[512,256]{1,0:T(8,128)(2,1)S(1)} %collective-permute-done.33), channel_id=1, source_target_pairs={{0,96},{16,112},{32,0},{48,16},{64,32},{80,48},{96,64},{112,80},{1... | collective-permute-start | bytes 786440 | tf_op jit(solution)/shard_map/ppermute | solution.py:35
  (25 other events, 293.8 us)

commit v3 on v2

v3 whole, which is shorter than its diff:
```python
import functools

import jax
import jax.numpy as jnp
from jax import lax
from jax.experimental import pallas as pl
from jax.experimental.pallas import tpu as pltpu
from jax.sharding import PartitionSpec as P

epsilon = 1e-06
mix_alpha = 0.8

BLK = 128
N_X, N_Y = 4, 4
N_ROW, N_COL = 8, 16
DEV_BLOCKS = 4
DEST = 8
HALF_BLOCKS = DEST * DEV_BLOCKS
HOP = (0, 0, 0, 1, 1, 1, 0, 1)
PLACE = (0, 1, 2, 0, 1, 3, 3, 2)
UNROLL = 8


def row_of(x, z_lo):
    return (x % N_X) * 2 + z_lo


def col_of(y, z_hi, core):
    return ((y % N_Y) * 2 + z_hi) * 2 + core


def shift_row(value, dx, dz):
    perm = [(row_of(x, z), row_of(x + dx, z ^ dz)) for x in range(N_X) for z in range(2)]
    return lax.ppermute(value, "row", perm)


def shift_col(value, dy, dz, dc):
    perm = [
        (col_of(y, z, c), col_of(y + dy, z ^ dz, c ^ dc))
        for y in range(N_Y)
        for z in range(2)
        for c in range(2)
    ]
    return lax.ppermute(value, "col", perm)


def gather_row(own):
    half = own.shape[0] // 2
    from_left = shift_row(own, 1, 0)
    from_right = shift_row(own, -1, 0)
    from_z = shift_row(own, 0, 1)
    far = shift_row(from_right, -1, 0)
    left_z = shift_row(from_z, 1, 0)
    right_z = shift_row(from_right, 0, 1)
    far_z_top = shift_row(from_left[:half], 1, 1)
    far_z_bottom = shift_row(from_right[half:], -1, 1)
    return [own, from_z, from_right, from_left], [right_z, far, left_z, far_z_top, far_z_bottom]


def add(*values):
    total = values[0].astype(jnp.float32)
    for value in values[1:]:
        total = total + value.astype(jnp.float32)
    return total


def scatter_col(send, keep):
    got = shift_col(send, 0, 0, 1)

    def pair(dy, dz, *more):
        at = dy * 2 + dz
        return add(keep[at], got[at], *more)

    def send(value, dy, dz):
        return shift_col(value.astype(jnp.bfloat16), dy, dz, 0)

    far_up = send(pair(2, 0), 1, 0)
    far_down = send(pair(2, 1), -1, 0)
    direct_up = send(pair(1, 1), 1, 1)
    direct_down = send(pair(3, 0), -1, 0)
    other = send(pair(0, 1), 0, 1)
    relay_up = send(pair(1, 0, far_up), 1, 0)
    relay_down = send(pair(3, 1, far_down), -1, 1)
    return pair(0, 0, relay_up, relay_down, direct_up, direct_down, other)


def params(mib):
    return pltpu.CompilerParams(vmem_limit_bytes=mib * 1024 * 1024)


any_spec = pl.BlockSpec(memory_space=pl.ANY)
smem_spec = pl.BlockSpec(memory_space=pltpu.SMEM)
vmem_spec = pl.BlockSpec(memory_space=pltpu.VMEM)


def preload_kernel(source, target, sem):
    copy = pltpu.make_async_copy(source, target, sem)
    copy.start()
    copy.wait()


def preload(vals):
    return pl.pallas_call(
        preload_kernel,
        out_shape=pltpu.VMEM(vals.shape, vals.dtype),
        in_specs=[pl.BlockSpec(memory_space=pltpu.HBM)],
        out_specs=vmem_spec,
        scratch_shapes=[pltpu.SemaphoreType.DMA(())],
        compiler_params=params(16),
        cost_estimate=pl.CostEstimate(flops=0, bytes_accessed=2 * vals.size, transcendentals=0),
        name="load_blocks",
    )(pltpu.with_memory_space_constraint(vals, pltpu.HBM))


def start_panel(pieces, panel, sems):
    copies = []
    start = 0
    for index, piece in enumerate(pieces):
        where = panel.at[pl.ds(start, piece.shape[0]), :, pl.ds(0, piece.shape[2])]
        copies.append(pltpu.make_async_copy(piece, where, sems.at[index]))
        start += piece.shape[0]
    for copy in copies:
        copy.start()
    return copies


def product_kernel(section, n_pieces, count_ref, first_ref, second_ref, vals, *refs):
    pieces = refs[:n_pieces]
    refs = refs[n_pieces:]
    last = section >= 1
    if section > 0:
        refs = refs[1:]
    total = refs[0]
    refs = refs[1:]
    if last:
        out_ref, refs = refs[0], refs[1:]
    panel, sems = refs[:2]
    width = pieces[0].shape[2]
    with_degree = panel.shape[2] > width
    zero_block = panel.shape[0] - 1

    copies = start_panel(pieces, panel, sems)
    panel[zero_block] = jnp.zeros(panel.shape[1:], panel.dtype)
    if with_degree:

        @pl.loop(0, zero_block)
        def _(block):
            panel[block, :, width:] = jnp.ones((BLK, panel.shape[2] - width), panel.dtype)

    if section == 0:

        @pl.loop(0, total.shape[0])
        def _(block):
            total[block] = jnp.zeros(total.shape[1:], jnp.float32)

    for copy in copies:
        copy.wait()

    @pl.loop(0, (count_ref[section] + UNROLL - 1) // UNROLL)
    def _(group):
        for u in range(UNROLL):
            first = first_ref[section, group * UNROLL + u]
            second = second_ref[section, group * UNROLL + u]
            row = lax.shift_right_logical(first, 14)
            col_a = lax.shift_right_logical(first, 9) & 31
            col_b = jnp.minimum(lax.shift_right_logical(second, 9) & 31, zero_block)
            col_a = jnp.minimum(col_a, zero_block)
            left = jnp.concatenate([vals[first & 511], vals[second & 511]], axis=1)
            right = jnp.concatenate([panel[col_a], panel[col_b]], axis=0)
            total[row] += jnp.dot(left, right, preferred_element_type=jnp.float32)

    if not last:
        return
    base = (section - 1) * HALF_BLOCKS
    if with_degree:
        degree = refs[2]
        degree[...] = jnp.zeros(degree.shape, jnp.float32)
        eye = lax.broadcasted_iota(jnp.int32, (BLK, BLK), 0) == lax.broadcasted_iota(
            jnp.int32, (BLK, BLK), 1
        )

    @pl.loop(0, DEST)
    def _(dest):
        for j in range(DEV_BLOCKS):
            block = base + dest * DEV_BLOCKS + j
            out_ref[dest, pl.ds(j * BLK, BLK), :] = total[block, :, :width].astype(out_ref.dtype)
            if with_degree:
                spread = jnp.where(eye, total[block, :, width:], 0.0)
                degree[j : j + 1, :] = jnp.sum(spread, axis=0, keepdims=True)
        if with_degree:
            out_ref[dest, pl.ds(DEV_BLOCKS * BLK, 16), :] = degree[...].astype(out_ref.dtype)


def product(plan, vals, hop, total, section, with_degree):
    pieces = [piece.reshape(-1, BLK, piece.shape[-1]) for piece in hop]
    blocks = sum(piece.shape[0] for piece in pieces)
    width = pieces[0].shape[2]
    wide = width + (BLK if with_degree else 0)
    out_shape = [pltpu.VMEM((2 * HALF_BLOCKS, BLK, wide), jnp.float32)]
    scratch = [
        pltpu.VMEM((blocks + 1, BLK, wide), jnp.bfloat16),
        pltpu.SemaphoreType.DMA((len(pieces),)),
    ]
    operands = [*plan, vals, *pieces]
    in_specs = [smem_spec] * 3 + [vmem_spec] + [any_spec] * len(pieces)
    aliases = {}
    if section > 0:
        aliases = {len(operands): 0}
        operands.append(total)
        in_specs.append(vmem_spec)
    if section >= 1:
        rows = DEV_BLOCKS * BLK + (16 if with_degree else 0)
        out_shape.append(jax.ShapeDtypeStruct((DEST, rows, width), jnp.bfloat16))
        if with_degree:
            scratch.append(pltpu.VMEM((16, BLK), jnp.float32))
    flops = (6_000_000_000, 3_000_000_000, 3_000_000_000)[section]
    return pl.pallas_call(
        functools.partial(product_kernel, section, len(pieces)),
        out_shape=out_shape,
        in_specs=in_specs,
        out_specs=[vmem_spec] * len(out_shape),
        scratch_shapes=scratch,
        input_output_aliases=aliases,
        compiler_params=params(16),
        cost_estimate=pl.CostEstimate(flops=flops, bytes_accessed=1 << 20, transcendentals=0),
        name=("product_near", "product_send", "product_keep")[section],
    )(*operands)


def layer_product(plan, vals, hops, with_degree):
    (total,) = product(plan, vals, hops[0], None, 0, with_degree)
    total, send = product(plan, vals, hops[1], total, 1, with_degree)
    total, keep = product(plan, vals, hops[1], total, 2, with_degree)
    return send, keep


def score_kernel(n_pieces, pair_ref, own, target, attributes, w_attr, attr_bias, *refs):
    pieces = refs[:n_pieces]
    out_ref, panel, sems = refs[n_pieces:]
    copies = start_panel(pieces, panel, sems)
    scale = own.shape[1] ** (-0.5)
    n_pair = pair_ref.shape[1]

    def row_mean(squares, count):
        return jnp.sum(squares.T, axis=0, keepdims=True) / count

    errors = []
    for block in range(DEV_BLOCKS):
        rows = pl.ds(block * BLK, BLK)
        rebuilt = jnp.dot(own[rows, :], w_attr[...], preferred_element_type=jnp.float32)
        gap = rebuilt + attr_bias[...] - attributes[rows, :].astype(jnp.float32)
        errors.append(jnp.sqrt(row_mean(gap * gap, gap.shape[1]) + epsilon))
    for copy in copies:
        copy.wait()
    for block in range(DEV_BLOCKS):
        rows = pl.ds(block * BLK, BLK)
        squares = jnp.zeros((BLK, BLK), jnp.float32)
        for pair in range(n_pair):
            logits = lax.dot_general(
                own[rows, :],
                panel[pair_ref[block, pair]],
                (((1,), (1,)), ((), ())),
                preferred_element_type=jnp.float32,
            )
            gap = jax.nn.sigmoid(logits * scale) - target[rows, pl.ds(pair * BLK, BLK)].astype(
                jnp.float32
            )
            squares = squares + gap * gap
        struct = jnp.sqrt(row_mean(squares, n_pair * BLK) + epsilon)
        out_ref[block : block + 1, :] = mix_alpha * errors[block] + (1.0 - mix_alpha) * struct


def score(hops, pairs, own, target, attributes, w_attr, attr_bias):
    pieces = [piece.reshape(-1, BLK, piece.shape[-1]) for hop in hops for piece in hop]
    out = pl.pallas_call(
        functools.partial(score_kernel, len(pieces)),
        out_shape=jax.ShapeDtypeStruct((DEV_BLOCKS, BLK), jnp.float32),
        in_specs=[smem_spec] + [vmem_spec] * 5 + [any_spec] * len(pieces),
        out_specs=vmem_spec,
        scratch_shapes=[
            pltpu.VMEM((N_ROW * DEV_BLOCKS, BLK, own.shape[1]), jnp.bfloat16),
            pltpu.SemaphoreType.DMA((len(pieces),)),
        ],
        compiler_params=params(16),
        name="score",
    )(pairs, own, target, attributes, w_attr, attr_bias, *pieces)
    return out.reshape(-1)


def make_plan(row_ids, col_ids, live_count, row_at, col_at):
    capacity = row_ids.shape[0]
    sections = 3
    slots = jnp.arange(capacity, dtype=jnp.int32)
    live = slots < live_count
    y, z_hi, core = col_at // 4, (col_at // 2) % 2, col_at % 2
    dest, j = row_ids // DEV_BLOCKS, row_ids % DEV_BLOCKS
    dy = (dest // 4 - y) % N_Y
    dz = (dest // 2 + z_hi) % 2
    keep = 1 - (dest + core) % 2
    row = keep * HALF_BLOCKS + (dy * 2 + dz) * DEV_BLOCKS + j
    hop, col = relative_block(col_ids, row_at)
    section = jnp.where(hop == 1, 1 + keep, 0)
    key = section * (2 * HALF_BLOCKS) + row
    same = (key[:, None] == key[None, :]) & live[None, :]
    within = jnp.sum((same & (slots[None, :] < slots[:, None])).astype(jnp.int32), axis=1)
    opens = live & (within % 2 == 0)
    ahead = (key[None, :] < key[:, None]) & (section[None, :] == section[:, None]) & opens[None, :]
    pair = jnp.sum(ahead.astype(jnp.int32), axis=1) + within // 2
    longest = -(-((capacity + 2 * HALF_BLOCKS) // 2) // UNROLL) * UNROLL
    place = jnp.where(live, (section * longest + pair) * 2 + within % 2, -1)
    places = jnp.arange(sections * longest, dtype=jnp.int32)
    empty = 31 * 512
    word = slots + col * 512 + row * (512 * 32) - empty

    def lay(side):
        hit = place[None, :] == (places * 2 + side)[:, None]
        found = jnp.sum(jnp.where(hit, word[None, :], 0), axis=1)
        return (empty + found).reshape(sections, longest)

    count = jnp.sum(
        (opens[None, :] & (section[None, :] == jnp.arange(sections)[:, None])).astype(jnp.int32),
        axis=1,
    )
    return count, lay(0), lay(1)


def relative_block(ids, row_at):
    owner, j = ids // DEV_BLOCKS, ids % DEV_BLOCKS
    offset = ((owner // 2 - row_at // 2) % N_X) * 2 + (owner + row_at) % 2
    hop = jnp.zeros_like(ids)
    place = jnp.zeros_like(ids)
    for at in range(N_ROW):
        hop = jnp.where(offset == at, HOP[at], hop)
        place = jnp.where(offset == at, PLACE[at], place)
    return hop, place * DEV_BLOCKS + j


def per_device(
    attributes,
    adj_values,
    adj_rows,
    adj_cols,
    adj_count,
    pair_ids,
    struct_target,
    w_first,
    w_rest,
    layer_bias,
    w_attr,
    attr_bias,
):
    vals = preload(adj_values[0, 0])
    hidden_size = w_rest.shape[1]
    row_at = lax.axis_index("row")
    col_at = lax.axis_index("col")
    plan = make_plan(adj_rows[0, 0], adj_cols[0, 0], adj_count[0, 0], row_at, col_at)
    nodes_dev = attributes.shape[0]
    w_near, w_self = w_first[:, :hidden_size], w_first[:, hidden_size:]
    own_part = jnp.dot(attributes, w_self, preferred_element_type=jnp.float32)

    summed = scatter_col(*layer_product(plan, vals, gather_row(attributes), True))
    degree = 1.0 + summed[nodes_dev : nodes_dev + DEV_BLOCKS].reshape(-1)
    row_scale = lax.rsqrt(degree)[:, None]
    aggregate = summed[:nodes_dev]
    coarse = lax.reduce_precision(aggregate, 8, 7)
    fine = (aggregate - coarse).astype(jnp.bfloat16)
    coarse = coarse.astype(jnp.bfloat16)
    mixed = jnp.dot(coarse, w_near, preferred_element_type=jnp.float32) + jnp.dot(
        fine, w_near, preferred_element_type=jnp.float32
    )
    hidden = jnp.tanh(row_scale * mixed + own_part).astype(jnp.bfloat16)

    features = jnp.dot(
        hidden, w_rest[0][:, :hidden_size], preferred_element_type=jnp.float32
    ).astype(jnp.bfloat16)
    hops = gather_row(features)
    own_part = (
        jnp.dot(hidden, w_rest[0][:, hidden_size:], preferred_element_type=jnp.float32)
        + layer_bias[0]
    )
    summed = scatter_col(*layer_product(plan, vals, hops, False))
    hidden = jnp.tanh(row_scale * summed + own_part).astype(jnp.bfloat16)

    hop, place = relative_block(pair_ids, row_at)
    return score(
        gather_row(hidden),
        hop * (N_ROW // 2) * DEV_BLOCKS + place,
        hidden,
        struct_target.reshape(nodes_dev, -1),
        attributes,
        w_attr,
        attr_bias[None, :],
    )


def solution(mesh):
    return jax.shard_map(
        per_device,
        mesh=mesh,
        in_specs=(
            P(("row", "col"), None),
            P("row", "col", None, None, None),
            P("row", "col", None),
            P("row", "col", None),
            P("row", "col"),
            P(("row", "col"), None),
            P(("row", "col"), None, None),
            P(),
            P(),
            P(),
            P(),
            P(),
        ),
        out_specs=P(("row", "col")),
        check_vma=False,
    )
```

time: 154 us -> 144 us (0.935); the launches traced: 152 us -> 145 us
  waiting for transfers between devices: 58.1 us -> 37.2 us
  starting transfers between devices: 57 us -> 74.5 us
  local copies, waits for them, and re-layouts: 4.91 us -> 0.33 us
    ppermute x16, starting transfers between devices: 23.3 us -> 39.1 us  [shift_col(): return lax.ppermute(value, 'col', perm)]
    ppermute x16, waiting for transfers between devices: 28.2 us -> 17.1 us  [shift_col(): return lax.ppermute(value, 'col', perm)]
    ppermute x24, waiting for transfers between devices: 29.9 us -> 20.1 us  [shift_row(): return lax.ppermute(value, 'row', perm)]
    unnamed x19 -> x17, local copies, waits for them, and re-layouts: 4.7 us -> 0.12 us
    pallas_call x1, Pallas kernels: 0.84 us -> 4.62 us  [preload(): pl.pallas_call(preload_kernel, out_shape=pltpu.VMEM(vals.shape, vals.dtyp...]
    pallas_call x7, Pallas kernels: 25.2 us -> 21.4 us  [the longest x6 18.9 us: product(): pl.pallas_call(functools.partial(product_kernel, section, len(pieces)), o...]
    ppermute x24, starting transfers between devices: 33.7 us -> 35.4 us  [shift_row(): return lax.ppermute(value, 'row', perm)]
  transfers between devices with their start and end apart: 40 -> 40, of which waited for: 19 -> 11; matrix products, arithmetic and copies ran while one was open for 2% -> 2% of each run, Pallas kernels for 8% -> 13%
where the time goes in v3:
time: 144 us; the launch traced here: 145 us
  starting transfers between devices  74.5 us (52%)
  waiting for transfers between devices  37.2 us (26%)
  Pallas kernels  26 us (18%)
  other arithmetic  4 us (3%)
    ppermute x16, starting transfers between devices, shift_col(): return lax.ppermute(value, 'col', perm)  39.1 us
    ppermute x24, starting transfers between devices, shift_row(): return lax.ppermute(value, 'row', perm)  35.4 us
    ppermute x24, waiting for transfers between devices, shift_row(): return lax.ppermute(value, 'row', perm)  20.1 us
    pallas_call x6, Pallas kernels, product(): pl.pallas_call(functools.partial(product_kernel, section, len(pieces)), o...  18.9 us
    ppermute x16, waiting for transfers between devices, shift_col(): return lax.ppermute(value, 'col', perm)  17.1 us
    pallas_call x1, Pallas kernels, preload(): pl.pallas_call(preload_kernel, out_shape=pltpu.VMEM(vals.shape, vals.dtyp...  4.62 us
  transfers between devices with their start and end apart: 40, of which 11 were waited for; matrix products, arithmetic and copies ran while one was open for 2% of the time, Pallas kernels for 13%

profile of v3, /device:TPU:0, one launch (start us, length us, event | category | flops | bytes accessed | tf_op | source)
XLA Modules:
  0.0 144.5 jit_solution(11009939317044607036)
XLA Ops:
  0.0 2.8 %collective-permute-start = (bf16[512,128]{1,0:T(8,128)(2,1)}, bf16[512,128]{1,0:T(8,128)(2,1)S(1)}, u32[]{:S(2)}, u32[]{:S(2)}) collective-permute-start(bf16[512,128]{1,0:T(8,128)(2,1)} %attributes.1), channel_id=1, source_target_pairs={{0,96},{16,112},{32,0},{48,16},{64,32},{80,48},{96,64},{112,80},{1... | collective-permute-start | bytes 393224 | tf_op jit(solution)/shard_map/ppermute | solution.py:34
  8.1 4.6 %load_blocks.1.vals = bf16[384,128,128]{2,1,0:T(8,128)(2,1)S(1)} custom-call(bf16[384,128,128]{2,1,0:T(8,128)(2,1)} %bitcast.148), custom_call_target="tpu_custom_call" | custom-call | bytes 12582912 | tf_op jit(solution)/shard_map/load_blocks/pallas_call | solution.py:103
  12.9 2.8 %collective-permute-start.7 = (bf16[256,128]{1,0:T(8,128)(2,1)S(1)}, bf16[256,128]{1,0:T(8,128)(2,1)S(1)}, u32[]{:S(2)}, u32[]{:S(2)}) collective-permute-start(bf16[256,128]{1,0:T(8,128)(2,1)S(1)} %slice.177), channel_id=1, source_target_pairs={{0,112},{16,96},{32,16},{48,0},{64,48},{80,32},{96,80},{112,64},{1... | collective-permute-start | bytes 196616 | tf_op jit(solution)/shard_map/ppermute | solution.py:34
  17.8 2.7 %collective-permute-start.2 = (bf16[512,128]{1,0:T(8,128)(2,1)S(1)}, bf16[512,128]{1,0:T(8,128)(2,1)S(1)}, u32[]{:S(2)}, u32[]{:S(2)}) collective-permute-start(bf16[512,128]{1,0:T(8,128)(2,1)S(1)} %collective-permute-done), channel_id=1, source_target_pairs={{0,96},{16,112},{32,0},{48,16},{64,32},{80,48},{96,64},{112,80},{1... | collective-permute-start | bytes 393224 | tf_op jit(solution)/shard_map/ppermute | solution.py:34
  20.5 4.5 %product_near.2.refs_5_ = f32[64,128,256]{2,1,0:T(8,128)S(1)} custom-call(s32[3]{0:T(128)S(1)} %convert_reduce_fusion.2.count_ref, s32[3,224]{1,0:T(4,128)S(1)} %add.678.first_ref, s32[3,224]{1,0:T(4,128)S(1)} %add.682.second_ref, bf16[384,128,128]{2,1,0:T(8,128)(2,1)S(1)} %load_blocks.1.vals, bf16[4,128,128]{2,1,0:T(8,128)(2,1)S(1)} %bitcast.129, ...), custom_call_target="tpu_custom_call" | custom-call | flops 6000000000 | bytes 1048576 | tf_op jit(solution)/shard_map/product_near/pallas_call | solution.py:217
  26.7 2.6 %product_send.2 = (f32[64,128,256]{2,1,0:T(8,128)S(1)}, bf16[8,528,128]{2,1,0:T(8,128)(2,1)S(1)}) custom-call(s32[3]{0:T(128)S(1)} %convert_reduce_fusion.2.count_ref, s32[3,224]{1,0:T(4,128)S(1)} %add.678.first_ref, s32[3,224]{1,0:T(4,128)S(1)} %add.682.second_ref, bf16[384,128,128]{2,1,0:T(8,128)(2,1)S(1)} %load_blocks.1.vals, ...), custom_call_target="tpu_custom_call", output_to_operand_aliasing={{0}: (9, {})} | custom-call | flops 3000000000 | bytes 1048576 | tf_op jit(solution)/shard_map/product_send/pallas_call | solution.py:217
  32.3 5.1 %collective-permute-start.11 = (bf16[528,128]{1,0:T(8,128)(2,1)S(1)}, bf16[528,128]{1,0:T(8,128)(2,1)S(1)}, u32[]{:S(2)}, u32[]{:S(2)}) collective-permute-start(bf16[528,128]{1,0:T(8,128)(2,1)S(1)} %get-tuple-element.37), channel_id=1, source_target_pairs={{0,12},{1,13},{2,14},{3,15},{4,0},{5,1},{6,2},{7,3},{8,4},{9,5},{1... | collective-permute-start | bytes 405512 | tf_op jit(solution)/shard_map/ppermute | solution.py:44
  37.4 4.2 %collective-permute-start.13 = (bf16[528,128]{1,0:T(8,128)(2,1)S(1)}, bf16[528,128]{1,0:T(8,128)(2,1)S(1)}, u32[]{:S(2)}, u32[]{:S(2)}) collective-permute-start(bf16[528,128]{1,0:T(8,128)(2,1)S(1)} %get-tuple-element.36), channel_id=1, source_target_pairs={{0,6},{1,7},{2,4},{3,5},{4,10},{5,11},{6,8},{7,9},{8,14},{9,15},{1... | collective-permute-start | bytes 405512 | tf_op jit(solution)/shard_map/ppermute | solution.py:44
  41.6 2.7 %collective-permute-start.14 = (bf16[528,128]{1,0:T(8,128)(2,1)S(1)}, bf16[528,128]{1,0:T(8,128)(2,1)S(1)}, u32[]{:S(2)}, u32[]{:S(2)}) collective-permute-start(bf16[528,128]{1,0:T(8,128)(2,1)S(1)} %get-tuple-element.35), channel_id=1, source_target_pairs={{0,12},{1,13},{2,14},{3,15},{4,0},{5,1},{6,2},{7,3},{8,4},{9,5},{1... | collective-permute-start | bytes 405512 | tf_op jit(solution)/shard_map/ppermute | solution.py:44
  45.1 6.5 %collective-permute-start.12 = (bf16[528,128]{1,0:T(8,128)(2,1)S(1)}, bf16[528,128]{1,0:T(8,128)(2,1)S(1)}, u32[]{:S(2)}, u32[]{:S(2)}) collective-permute-start(bf16[528,128]{1,0:T(8,128)(2,1)S(1)} %get-tuple-element.32), channel_id=1, source_target_pairs={{0,14},{1,15},{2,12},{3,13},{4,2},{5,3},{6,0},{7,1},{8,6},{9,7},{1... | collective-permute-start | bytes 405512 | tf_op jit(solution)/shard_map/ppermute | solution.py:44
  51.5 2.8 %collective-permute-done.15 = bf16[528,128]{1,0:T(8,128)(2,1)S(1)} collective-permute-done((bf16[528,128]{1,0:T(8,128)(2,1)S(1)}, bf16[528,128]{1,0:T(8,128)(2,1)S(1)}, u32[]{:S(2)}, u32[]{:S(2)}) %collective-permute-start.15) | collective-permute-done | bytes 135200 | tf_op jit(solution)/shard_map/ppermute | solution.py:44
  55.5 3.2 %collective-permute-start.16 = (bf16[512,256]{1,0:T(8,128)(2,1)S(1)}, bf16[512,256]{1,0:T(8,128)(2,1)S(1)}, u32[]{:S(2)}, u32[]{:S(2)}) collective-permute-start(bf16[512,256]{1,0:T(8,128)(2,1)S(1)} %convolution_convert_fusion), channel_id=1, source_target_pairs={{0,96},{16,112},{32,0},{48,16},{64,32},{80,48},{96,64},{112,80},{1... | collective-permute-start | bytes 786440 | tf_op jit(solution)/shard_map/ppermute | solution.py:34
  59.6 4.2 %collective-permute-done.21 = bf16[512,256]{1,0:T(8,128)(2,1)S(1)} collective-permute-done((bf16[512,256]{1,0:T(8,128)(2,1)S(1)}, bf16[512,256]{1,0:T(8,128)(2,1)S(1)}, u32[]{:S(2)}, u32[]{:S(2)}) %collective-permute-start.21) | collective-permute-done | bytes 262176 | tf_op jit(solution)/shard_map/ppermute | solution.py:34
  65.0 3.1 %collective-permute-start.23 = (bf16[256,256]{1,0:T(8,128)(2,1)S(1)}, bf16[256,256]{1,0:T(8,128)(2,1)S(1)}, u32[]{:S(2)}, u32[]{:S(2)}) collective-permute-start(bf16[256,256]{1,0:T(8,128)(2,1)S(1)} %slice.190), channel_id=1, source_target_pairs={{0,112},{16,96},{32,16},{48,0},{64,48},{80,32},{96,80},{112,64},{1... | collective-permute-start | bytes 393224 | tf_op jit(solution)/shard_map/ppermute | solution.py:34
  71.9 4.4 %product_near.3.refs_5_ = f32[64,128,256]{2,1,0:T(8,128)S(1)} custom-call(s32[3]{0:T(128)S(1)} %convert_reduce_fusion.2.count_ref, s32[3,224]{1,0:T(4,128)S(1)} %add.678.first_ref, s32[3,224]{1,0:T(4,128)S(1)} %add.682.second_ref, bf16[384,128,128]{2,1,0:T(8,128)(2,1)S(1)} %load_blocks.1.vals, bf16[4,128,256]{2,1,0:T(8,128)(2,1)S(1)} %bitcast.138, ...), custom_call_target="tpu_custom_call" | custom-call | flops 6000000000 | bytes 1048576 | tf_op jit(solution)/shard_map/product_near/pallas_call | solution.py:217
  78.3 2.7 %product_send.3 = (f32[64,128,256]{2,1,0:T(8,128)S(1)}, bf16[8,512,256]{2,1,0:T(8,128)(2,1)S(1)}) custom-call(s32[3]{0:T(128)S(1)} %convert_reduce_fusion.2.count_ref, s32[3,224]{1,0:T(4,128)S(1)} %add.678.first_ref, s32[3,224]{1,0:T(4,128)S(1)} %add.682.second_ref, bf16[384,128,128]{2,1,0:T(8,128)(2,1)S(1)} %load_blocks.1.vals, ...), custom_call_target="tpu_custom_call", output_to_operand_aliasing={{0}: (9, {})} | custom-call | flops 3000000000 | bytes 1048576 | tf_op jit(solution)/shard_map/product_send/pallas_call | solution.py:217
  85.7 4.9 %collective-permute-start.27 = (bf16[512,256]{1,0:T(8,128)(2,1)S(1)}, bf16[512,256]{1,0:T(8,128)(2,1)S(1)}, u32[]{:S(2)}, u32[]{:S(2)}) collective-permute-start(bf16[512,256]{1,0:T(8,128)(2,1)S(1)} %get-tuple-element.30), channel_id=1, source_target_pairs={{0,12},{1,13},{2,14},{3,15},{4,0},{5,1},{6,2},{7,3},{8,4},{9,5},{1... | collective-permute-start | bytes 786440 | tf_op jit(solution)/shard_map/ppermute | solution.py:44
  92.2 6.1 %collective-permute-start.30 = (bf16[512,256]{1,0:T(8,128)(2,1)S(1)}, bf16[512,256]{1,0:T(8,128)(2,1)S(1)}, u32[]{:S(2)}, u32[]{:S(2)}) collective-permute-start(bf16[512,256]{1,0:T(8,128)(2,1)S(1)} %get-tuple-element.28), channel_id=1, source_target_pairs={{0,12},{1,13},{2,14},{3,15},{4,0},{5,1},{6,2},{7,3},{8,4},{9,5},{1... | collective-permute-start | bytes 786440 | tf_op jit(solution)/shard_map/ppermute | solution.py:44
  98.6 7.2 %collective-permute-start.28 = (bf16[512,256]{1,0:T(8,128)(2,1)S(1)}, bf16[512,256]{1,0:T(8,128)(2,1)S(1)}, u32[]{:S(2)}, u32[]{:S(2)}) collective-permute-start(bf16[512,256]{1,0:T(8,128)(2,1)S(1)} %get-tuple-element.25), channel_id=1, source_target_pairs={{0,14},{1,15},{2,12},{3,13},{4,2},{5,3},{6,0},{7,1},{8,6},{9,7},{1... | collective-permute-start | bytes 786440 | tf_op jit(solution)/shard_map/ppermute | solution.py:44
  106.1 3.4 %collective-permute-done.29 = bf16[512,256]{1,0:T(8,128)(2,1)S(1)} collective-permute-done((bf16[512,256]{1,0:T(8,128)(2,1)S(1)}, bf16[512,256]{1,0:T(8,128)(2,1)S(1)}, u32[]{:S(2)}, u32[]{:S(2)}) %collective-permute-start.29) | collective-permute-done | bytes 262176 | tf_op jit(solution)/shard_map/ppermute | solution.py:44
  109.5 8.8 %collective-permute-done.31 = bf16[512,256]{1,0:T(8,128)(2,1)S(1)} collective-permute-done((bf16[512,256]{1,0:T(8,128)(2,1)S(1)}, bf16[512,256]{1,0:T(8,128)(2,1)S(1)}, u32[]{:S(2)}, u32[]{:S(2)}) %collective-permute-start.31) | collective-permute-done | bytes 262176 | tf_op jit(solution)/shard_map/ppermute | solution.py:44
  121.4 5.3 %collective-permute-done.33 = bf16[512,256]{1,0:T(8,128)(2,1)S(1)} collective-permute-done((bf16[512,256]{1,0:T(8,128)(2,1)S(1)}, bf16[512,256]{1,0:T(8,128)(2,1)S(1)}, u32[]{:S(2)}, u32[]{:S(2)}) %collective-permute-start.33) | collective-permute-done | bytes 262176 | tf_op jit(solution)/shard_map/ppermute | solution.py:34
  130.4 4.3 %collective-permute-start.39 = (bf16[256,256]{1,0:T(8,128)(2,1)S(1)}, bf16[256,256]{1,0:T(8,128)(2,1)S(1)}, u32[]{:S(2)}, u32[]{:S(2)}) collective-permute-start(bf16[256,256]{1,0:T(8,128)(2,1)S(1)} %slice.201), channel_id=1, source_target_pairs={{0,112},{16,96},{32,16},{48,0},{64,48},{80,32},{96,80},{112,64},{1... | collective-permute-start | bytes 393224 | tf_op jit(solution)/shard_map/ppermute | solution.py:34
  134.7 7.1 %collective-permute-done.38 = bf16[256,256]{1,0:T(8,128)(2,1)S(1)} collective-permute-done((bf16[256,256]{1,0:T(8,128)(2,1)S(1)}, bf16[256,256]{1,0:T(8,128)(2,1)S(1)}, u32[]{:S(2)}, u32[]{:S(2)}) %collective-permute-start.38) | collective-permute-done | bytes 131104 | tf_op jit(solution)/shard_map/ppermute | solution.py:34
  (116 shorter events, 37.4 us)
Async XLA Ops:
  0.0 12.9 %collective-permute-start = (bf16[512,128]{1,0:T(8,128)(2,1)}, bf16[512,128]{1,0:T(8,128)(2,1)S(1)}, u32[]{:S(2)}, u32[]{:S(2)}) collective-permute-start(bf16[512,128]{1,0:T(8,128)(2,1)} %attributes.1), channel_id=1, source_target_pairs={{0,96},{16,112},{32,0},{48,16},{64,32},{80,48},{96,64},{112,80},{1... | collective-permute-start | bytes 393224 | tf_op jit(solution)/shard_map/ppermute | solution.py:34
  2.8 12.9 %collective-permute-start.5 = (bf16[512,128]{1,0:T(8,128)(2,1)}, bf16[512,128]{1,0:T(8,128)(2,1)S(1)}, u32[]{:S(2)}, u32[]{:S(2)}) collective-permute-start(bf16[512,128]{1,0:T(8,128)(2,1)} %attributes.1), channel_id=1, source_target_pairs={{0,32},{16,48},{32,64},{48,80},{64,96},{80,112},{96,0},{112,16},{1... | collective-permute-start | bytes 393224 | tf_op jit(solution)/shard_map/ppermute | solution.py:34
  2.8 17.7 %collective-permute-start.3 = (bf16[512,128]{1,0:T(8,128)(2,1)}, bf16[512,128]{1,0:T(8,128)(2,1)S(1)}, u32[]{:S(2)}, u32[]{:S(2)}) collective-permute-start(bf16[512,128]{1,0:T(8,128)(2,1)} %attributes.1), channel_id=1, source_target_pairs={{0,16},{16,0},{32,48},{48,32},{64,80},{80,64},{96,112},{112,96},{1... | collective-permute-start | bytes 393224 | tf_op jit(solution)/shard_map/ppermute | solution.py:34
  12.9 12.2 %collective-permute-start.7 = (bf16[256,128]{1,0:T(8,128)(2,1)S(1)}, bf16[256,128]{1,0:T(8,128)(2,1)S(1)}, u32[]{:S(2)}, u32[]{:S(2)}) collective-permute-start(bf16[256,128]{1,0:T(8,128)(2,1)S(1)} %slice.177), channel_id=1, source_target_pairs={{0,112},{16,96},{32,16},{48,0},{64,48},{80,32},{96,80},{112,64},{1... | collective-permute-start | bytes 196616 | tf_op jit(solution)/shard_map/ppermute | solution.py:34
  32.3 12.5 %collective-permute-start.11 = (bf16[528,128]{1,0:T(8,128)(2,1)S(1)}, bf16[528,128]{1,0:T(8,128)(2,1)S(1)}, u32[]{:S(2)}, u32[]{:S(2)}) collective-permute-start(bf16[528,128]{1,0:T(8,128)(2,1)S(1)} %get-tuple-element.37), channel_id=1, source_target_pairs={{0,12},{1,13},{2,14},{3,15},{4,0},{5,1},{6,2},{7,3},{8,4},{9,5},{1... | collective-permute-start | bytes 405512 | tf_op jit(solution)/shard_map/ppermute | solution.py:44
  37.4 14.1 %collective-permute-start.13 = (bf16[528,128]{1,0:T(8,128)(2,1)S(1)}, bf16[528,128]{1,0:T(8,128)(2,1)S(1)}, u32[]{:S(2)}, u32[]{:S(2)}) collective-permute-start(bf16[528,128]{1,0:T(8,128)(2,1)S(1)} %get-tuple-element.36), channel_id=1, source_target_pairs={{0,6},{1,7},{2,4},{3,5},{4,10},{5,11},{6,8},{7,9},{8,14},{9,15},{1... | collective-permute-start | bytes 405512 | tf_op jit(solution)/shard_map/ppermute | solution.py:44
  41.6 10.0 %collective-permute-start.14 = (bf16[528,128]{1,0:T(8,128)(2,1)S(1)}, bf16[528,128]{1,0:T(8,128)(2,1)S(1)}, u32[]{:S(2)}, u32[]{:S(2)}) collective-permute-start(bf16[528,128]{1,0:T(8,128)(2,1)S(1)} %get-tuple-element.35), channel_id=1, source_target_pairs={{0,12},{1,13},{2,14},{3,15},{4,0},{5,1},{6,2},{7,3},{8,4},{9,5},{1... | collective-permute-start | bytes 405512 | tf_op jit(solution)/shard_map/ppermute | solution.py:44
  44.3 10.0 %collective-permute-start.15 = (bf16[528,128]{1,0:T(8,128)(2,1)S(1)}, bf16[528,128]{1,0:T(8,128)(2,1)S(1)}, u32[]{:S(2)}, u32[]{:S(2)}) collective-permute-start(bf16[528,128]{1,0:T(8,128)(2,1)S(1)} %get-tuple-element.34), channel_id=1, source_target_pairs={{0,2},{1,3},{2,0},{3,1},{4,6},{5,7},{6,4},{7,5},{8,10},{9,11},{10,... | collective-permute-start | bytes 405512 | tf_op jit(solution)/shard_map/ppermute | solution.py:44
  58.7 12.0 %collective-permute-start.19 = (bf16[512,256]{1,0:T(8,128)(2,1)S(1)}, bf16[512,256]{1,0:T(8,128)(2,1)S(1)}, u32[]{:S(2)}, u32[]{:S(2)}) collective-permute-start(bf16[512,256]{1,0:T(8,128)(2,1)S(1)} %convolution_convert_fusion), channel_id=1, source_target_pairs={{0,16},{16,0},{32,48},{48,32},{64,80},{80,64},{96,112},{112,96},{1... | collective-permute-start | bytes 786440 | tf_op jit(solution)/shard_map/ppermute | solution.py:34
  63.8 12.6 %collective-permute-start.22 = (bf16[256,256]{1,0:T(8,128)(2,1)S(1)}, bf16[256,256]{1,0:T(8,128)(2,1)S(1)}, u32[]{:S(2)}, u32[]{:S(2)}) collective-permute-start(bf16[256,256]{1,0:T(8,128)(2,1)S(1)} %slice.189), channel_id=1, source_target_pairs={{0,48},{16,32},{32,80},{48,64},{64,112},{80,96},{96,16},{112,0},{1... | collective-permute-start | bytes 393224 | tf_op jit(solution)/shard_map/ppermute | solution.py:34
  65.0 11.4 %collective-permute-start.23 = (bf16[256,256]{1,0:T(8,128)(2,1)S(1)}, bf16[256,256]{1,0:T(8,128)(2,1)S(1)}, u32[]{:S(2)}, u32[]{:S(2)}) collective-permute-start(bf16[256,256]{1,0:T(8,128)(2,1)S(1)} %slice.190), channel_id=1, source_target_pairs={{0,112},{16,96},{32,16},{48,0},{64,48},{80,32},{96,80},{112,64},{1... | collective-permute-start | bytes 393224 | tf_op jit(solution)/shard_map/ppermute | solution.py:34
  68.2 10.0 %collective-permute-start.17 = (bf16[512,256]{1,0:T(8,128)(2,1)S(1)}, bf16[512,256]{1,0:T(8,128)(2,1)S(1)}, u32[]{:S(2)}, u32[]{:S(2)}) collective-permute-start(bf16[512,256]{1,0:T(8,128)(2,1)S(1)} %collective-permute-done.16), channel_id=1, source_target_pairs={{0,16},{16,0},{32,48},{48,32},{64,80},{80,64},{96,112},{112,96},{1... | collective-permute-start | bytes 786440 | tf_op jit(solution)/shard_map/ppermute | solution.py:34
  85.6 12.7 %collective-permute-start.25 = (bf16[512,256]{1,0:T(8,128)(2,1)S(1)}, bf16[512,256]{1,0:T(8,128)(2,1)S(1)}, u32[]{:S(2)}, u32[]{:S(2)}) collective-permute-start(bf16[512,256]{1,0:T(8,128)(2,1)S(1)} %get-tuple-element.26), channel_id=1, source_target_pairs={{0,4},{1,5},{2,6},{3,7},{4,8},{5,9},{6,10},{7,11},{8,12},{9,13},{1... | collective-permute-start | bytes 786440 | tf_op jit(solution)/shard_map/ppermute | solution.py:44
  85.7 12.6 %collective-permute-start.27 = (bf16[512,256]{1,0:T(8,128)(2,1)S(1)}, bf16[512,256]{1,0:T(8,128)(2,1)S(1)}, u32[]{:S(2)}, u32[]{:S(2)}) collective-permute-start(bf16[512,256]{1,0:T(8,128)(2,1)S(1)} %get-tuple-element.30), channel_id=1, source_target_pairs={{0,12},{1,13},{2,14},{3,15},{4,0},{5,1},{6,2},{7,3},{8,4},{9,5},{1... | collective-permute-start | bytes 786440 | tf_op jit(solution)/shard_map/ppermute | solution.py:44
  90.6 18.9 %collective-permute-start.29 = (bf16[512,256]{1,0:T(8,128)(2,1)S(1)}, bf16[512,256]{1,0:T(8,128)(2,1)S(1)}, u32[]{:S(2)}, u32[]{:S(2)}) collective-permute-start(bf16[512,256]{1,0:T(8,128)(2,1)S(1)} %get-tuple-element.29), channel_id=1, source_target_pairs={{0,6},{1,7},{2,4},{3,5},{4,10},{5,11},{6,8},{7,9},{8,14},{9,15},{1... | collective-permute-start | bytes 786440 | tf_op jit(solution)/shard_map/ppermute | solution.py:44
  92.2 17.3 %collective-permute-start.30 = (bf16[512,256]{1,0:T(8,128)(2,1)S(1)}, bf16[512,256]{1,0:T(8,128)(2,1)S(1)}, u32[]{:S(2)}, u32[]{:S(2)}) collective-permute-start(bf16[512,256]{1,0:T(8,128)(2,1)S(1)} %get-tuple-element.28), channel_id=1, source_target_pairs={{0,12},{1,13},{2,14},{3,15},{4,0},{5,1},{6,2},{7,3},{8,4},{9,5},{1... | collective-permute-start | bytes 786440 | tf_op jit(solution)/shard_map/ppermute | solution.py:44
  98.3 20.0 %collective-permute-start.31 = (bf16[512,256]{1,0:T(8,128)(2,1)S(1)}, bf16[512,256]{1,0:T(8,128)(2,1)S(1)}, u32[]{:S(2)}, u32[]{:S(2)}) collective-permute-start(bf16[512,256]{1,0:T(8,128)(2,1)S(1)} %get-tuple-element.27), channel_id=1, source_target_pairs={{0,2},{1,3},{2,0},{3,1},{4,6},{5,7},{6,4},{7,5},{8,10},{9,11},{10,... | collective-permute-start | bytes 786440 | tf_op jit(solution)/shard_map/ppermute | solution.py:44
  98.5 19.7 %collective-permute-start.26 = (bf16[512,256]{1,0:T(8,128)(2,1)S(1)}, bf16[512,256]{1,0:T(8,128)(2,1)S(1)}, u32[]{:S(2)}, u32[]{:S(2)}) collective-permute-start(bf16[512,256]{1,0:T(8,128)(2,1)S(1)} %get-tuple-element.24), channel_id=1, source_target_pairs={{0,4},{1,5},{2,6},{3,7},{4,8},{5,9},{6,10},{7,11},{8,12},{9,13},{1... | collective-permute-start | bytes 786440 | tf_op jit(solution)/shard_map/ppermute | solution.py:44
  98.6 19.6 %collective-permute-start.28 = (bf16[512,256]{1,0:T(8,128)(2,1)S(1)}, bf16[512,256]{1,0:T(8,128)(2,1)S(1)}, u32[]{:S(2)}, u32[]{:S(2)}) collective-permute-start(bf16[512,256]{1,0:T(8,128)(2,1)S(1)} %get-tuple-element.25), channel_id=1, source_target_pairs={{0,14},{1,15},{2,12},{3,13},{4,2},{5,3},{6,0},{7,1},{8,6},{9,7},{1... | collective-permute-start | bytes 786440 | tf_op jit(solution)/shard_map/ppermute | solution.py:44
  126.7 15.1 %collective-permute-start.35 = (bf16[512,256]{1,0:T(8,128)(2,1)S(1)}, bf16[512,256]{1,0:T(8,128)(2,1)S(1)}, u32[]{:S(2)}, u32[]{:S(2)}) collective-permute-start(bf16[512,256]{1,0:T(8,128)(2,1)S(1)} %collective-permute-done.33), channel_id=1, source_target_pairs={{0,16},{16,0},{32,48},{48,32},{64,80},{80,64},{96,112},{112,96},{1... | collective-permute-start | bytes 786440 | tf_op jit(solution)/shard_map/ppermute | solution.py:34
  127.4 14.4 %collective-permute-start.36 = (bf16[512,256]{1,0:T(8,128)(2,1)S(1)}, bf16[512,256]{1,0:T(8,128)(2,1)S(1)}, u32[]{:S(2)}, u32[]{:S(2)}) collective-permute-start(bf16[512,256]{1,0:T(8,128)(2,1)S(1)} %collective-permute-done.33), channel_id=1, source_target_pairs={{0,96},{16,112},{32,0},{48,16},{64,32},{80,48},{96,64},{112,80},{1... | collective-permute-start | bytes 786440 | tf_op jit(solution)/shard_map/ppermute | solution.py:34
  129.7 12.1 %collective-permute-start.37 = (bf16[512,256]{1,0:T(8,128)(2,1)S(1)}, bf16[512,256]{1,0:T(8,128)(2,1)S(1)}, u32[]{:S(2)}, u32[]{:S(2)}) collective-permute-start(bf16[512,256]{1,0:T(8,128)(2,1)S(1)} %collective-permute-done.32), channel_id=1, source_target_pairs={{0,32},{16,48},{32,64},{48,80},{64,96},{80,112},{96,0},{112,16},{1... | collective-permute-start | bytes 786440 | tf_op jit(solution)/shard_map/ppermute | solution.py:34
  129.8 12.0 %collective-permute-start.38 = (bf16[256,256]{1,0:T(8,128)(2,1)S(1)}, bf16[256,256]{1,0:T(8,128)(2,1)S(1)}, u32[]{:S(2)}, u32[]{:S(2)}) collective-permute-start(bf16[256,256]{1,0:T(8,128)(2,1)S(1)} %slice.200), channel_id=1, source_target_pairs={{0,48},{16,32},{32,80},{48,64},{64,112},{80,96},{96,16},{112,0},{1... | collective-permute-start | bytes 393224 | tf_op jit(solution)/shard_map/ppermute | solution.py:34
  130.4 11.4 %collective-permute-start.39 = (bf16[256,256]{1,0:T(8,128)(2,1)S(1)}, bf16[256,256]{1,0:T(8,128)(2,1)S(1)}, u32[]{:S(2)}, u32[]{:S(2)}) collective-permute-start(bf16[256,256]{1,0:T(8,128)(2,1)S(1)} %slice.201), channel_id=1, source_target_pairs={{0,112},{16,96},{32,16},{48,0},{64,48},{80,32},{96,80},{112,64},{1... | collective-permute-start | bytes 393224 | tf_op jit(solution)/shard_map/ppermute | solution.py:34
  (24 other events, 322.0 us)

commit v4 on v3

--- a/solution.py
+++ b/solution.py
@@ -17,8 +17,11 @@
 DEST = 8
 HALF_BLOCKS = DEST * DEV_BLOCKS
 HOP = (0, 0, 0, 1, 1, 1, 0, 1)
-PLACE = (0, 1, 2, 0, 1, 3, 3, 2)
+PLACE = (0, 1, 2, 1, 0, 3, 3, 2)
 UNROLL = 8
+TAKEN = 4
+STEPS = 256
+EMPTY = 31 * 512
 
 
 def row_of(x, z_lo):
@@ -44,17 +47,22 @@
     return lax.ppermute(value, "col", perm)
 
 
-def gather_row(own):
-    half = own.shape[0] // 2
+def gather_row(own, joined):
     from_left = shift_row(own, 1, 0)
     from_right = shift_row(own, -1, 0)
     from_z = shift_row(own, 0, 1)
+    near = [own, from_z, from_right, from_left]
+    left_z = shift_row(from_z, 1, 0)
+    if joined:
+        far_right_z = shift_row(jnp.concatenate([from_right, from_z]), -1, 0)
+        far_z = shift_row(from_left, 1, 1)
+        return near, [far_right_z, left_z, far_z]
+    half = own.shape[0] // 2
     far = shift_row(from_right, -1, 0)
-    left_z = shift_row(from_z, 1, 0)
     right_z = shift_row(from_right, 0, 1)
     far_z_top = shift_row(from_left[:half], 1, 1)
     far_z_bottom = shift_row(from_right[half:], -1, 1)
-    return [own, from_z, from_right, from_left], [right_z, far, left_z, far_z_top, far_z_bottom]
+    return near, [far, right_z, left_z, far_z_top, far_z_bottom]
 
 
 def add(*values):
@@ -93,23 +101,108 @@
 vmem_spec = pl.BlockSpec(memory_space=pltpu.VMEM)
 
 
-def preload_kernel(source, target, sem):
-    copy = pltpu.make_async_copy(source, target, sem)
+def down(row):
+    return jnp.broadcast_to(row.astype(jnp.float32), (BLK, row.shape[1])).T
+
+
+def clear(total):
+    @pl.loop(0, total.shape[0])
+    def _(block):
+        total[block] = jnp.zeros(total.shape[1:], jnp.float32)
+
+
+def begin_kernel(place_ref, rows_ref, cols_ref, source, vals, total, plan, sem):
+    copy = pltpu.make_async_copy(source, vals, sem)
     copy.start()
+    count, row_at, col_at = place_ref[0], place_ref[1], place_ref[2]
+    y, z_hi, core = col_at >> 2, (col_at >> 1) & 1, col_at & 1
+    rows = rows_ref[...]
+    capacity = rows.shape[1]
+    slots = lax.broadcasted_iota(jnp.int32, rows.shape, 1)
+    live = slots < count
+    dest, j = rows >> 2, rows & 3
+    dy = ((dest >> 2) - y) & 3
+    dz = ((dest >> 1) + z_hi) & 1
+    keep = 1 - ((dest + core) & 1)
+    row = keep * HALF_BLOCKS + (dy * 2 + dz) * DEV_BLOCKS + j
+    hop, col = relative_block(cols_ref[...], row_at)
+    section = jnp.where(hop == 1, 1 + keep, 0)
+    key = jnp.where(live, section * (2 * HALF_BLOCKS) + row, 1024).astype(jnp.float32)
+    parts = capacity // BLK
+    square = (capacity, capacity)
+    earlier = lax.broadcasted_iota(jnp.int32, square, 0) < lax.broadcasted_iota(jnp.int32, square, 1)
+
+    def wide(column):
+        return jnp.concatenate([column] * parts, axis=1)
+
+    def tally(mask):
+        return jnp.sum(jnp.where(mask, 1.0, 0.0), axis=0, keepdims=True)
+
+    within = tally((wide(down(key)) == key) & earlier).astype(jnp.int32)
+    opens = live & ((within & (TAKEN - 1)) == 0)
+    opener = wide(down(jnp.where(opens, key, 2048.0)))
+    least = (section * (2 * HALF_BLOCKS)).astype(jnp.float32)
+    step = tally((opener >= least) & (opener < key)).astype(jnp.int32) + within // TAKEN
+    lane = lax.broadcasted_iota(jnp.int32, (1, STEPS), 1)
+    ends = jnp.zeros((1, 1), jnp.int32)
+    begin = jnp.zeros(rows.shape, jnp.int32)
+    bounds = jnp.zeros((1, STEPS), jnp.int32)
+    for kind in range(3):
+        begin = jnp.where(section == kind, ends, begin)
+        mine = jnp.where(opens & (section == kind), 1.0, 0.0)
+        number = jnp.sum(mine, axis=1, keepdims=True).astype(jnp.int32)
+        ends = ends + (number + UNROLL - 1) // UNROLL
+        bounds = jnp.where(lane == kind + 1, ends, bounds)
+    spot = (begin * UNROLL + step) * TAKEN + (within & (TAKEN - 1))
+    spot = down(jnp.where(live, spot, -1))
+    word = down(slots + col * 512 + row * (512 * 32) - EMPTY)
+    for side in range(TAKEN):
+        for part in range(STEPS // BLK):
+            here = lax.broadcasted_iota(jnp.int32, (1, BLK), 1) + part * BLK
+            hit = spot == (here * TAKEN + side).astype(jnp.float32)
+            found = jnp.sum(jnp.where(hit, word, 0.0), axis=0, keepdims=True)
+            plan[side : side + 1, part * BLK : (part + 1) * BLK] = found.astype(jnp.int32) + EMPTY
+    plan[TAKEN : TAKEN + 1, :] = bounds
+    clear(total)
     copy.wait()
 
 
-def preload(vals):
+total_shape = (2 * HALF_BLOCKS, BLK, 2 * BLK)
+
+
+def begin(vals, row_ids, col_ids, live_count, row_at, col_at):
+    place = jnp.stack([live_count, row_at, col_at]).astype(jnp.int32)
     return pl.pallas_call(
-        preload_kernel,
-        out_shape=pltpu.VMEM(vals.shape, vals.dtype),
-        in_specs=[pl.BlockSpec(memory_space=pltpu.HBM)],
-        out_specs=vmem_spec,
+        begin_kernel,
+        out_shape=[
+            pltpu.VMEM(vals.shape, vals.dtype),
+            pltpu.VMEM(total_shape, jnp.float32),
+            jax.ShapeDtypeStruct((TAKEN + 1, STEPS), jnp.int32),
+        ],
+        in_specs=[smem_spec, vmem_spec, vmem_spec, pl.BlockSpec(memory_space=pltpu.HBM)],
+        out_specs=[vmem_spec] * 3,
         scratch_shapes=[pltpu.SemaphoreType.DMA(())],
         compiler_params=params(16),
         cost_estimate=pl.CostEstimate(flops=0, bytes_accessed=2 * vals.size, transcendentals=0),
-        name="load_blocks",
-    )(pltpu.with_memory_space_constraint(vals, pltpu.HBM))
+        name="begin",
+    )(
+        place,
+        row_ids[None, :],
+        col_ids[None, :],
+        pltpu.with_memory_space_constraint(vals, pltpu.HBM),
+    )
+
+
+def cleared(after):
+    return pl.pallas_call(
+        lambda after_ref, total: clear(total),
+        out_shape=pltpu.VMEM(total_shape, jnp.float32),
+        in_specs=[any_spec],
+        out_specs=vmem_spec,
+        compiler_params=params(16),
+        cost_estimate=pl.CostEstimate(flops=0, bytes_accessed=1 << 21, transcendentals=0),
+        name="cleared",
+    )(after)
 
 
 def start_panel(pieces, panel, sems):
@@ -124,14 +217,11 @@
     return copies
 
 
-def product_kernel(section, n_pieces, count_ref, first_ref, second_ref, vals, *refs):
+def product_kernel(section, n_pieces, plan, vals, *refs):
     pieces = refs[:n_pieces]
     refs = refs[n_pieces:]
     last = section >= 1
-    if section > 0:
-        refs = refs[1:]
-    total = refs[0]
-    refs = refs[1:]
+    total, refs = refs[1], refs[2:]
     if last:
         out_ref, refs = refs[0], refs[1:]
     panel, sems = refs[:2]
@@ -147,26 +237,17 @@
         def _(block):
             panel[block, :, width:] = jnp.ones((BLK, panel.shape[2] - width), panel.dtype)
 
-    if section == 0:
-
-        @pl.loop(0, total.shape[0])
-        def _(block):
-            total[block] = jnp.zeros(total.shape[1:], jnp.float32)
-
     for copy in copies:
         copy.wait()
 
-    @pl.loop(0, (count_ref[section] + UNROLL - 1) // UNROLL)
+    @pl.loop(plan[TAKEN, section], plan[TAKEN, section + 1])
     def _(group):
         for u in range(UNROLL):
-            first = first_ref[section, group * UNROLL + u]
-            second = second_ref[section, group * UNROLL + u]
-            row = lax.shift_right_logical(first, 14)
-            col_a = lax.shift_right_logical(first, 9) & 31
-            col_b = jnp.minimum(lax.shift_right_logical(second, 9) & 31, zero_block)
-            col_a = jnp.minimum(col_a, zero_block)
-            left = jnp.concatenate([vals[first & 511], vals[second & 511]], axis=1)
-            right = jnp.concatenate([panel[col_a], panel[col_b]], axis=0)
+            words = [plan[side, group * UNROLL + u] for side in range(TAKEN)]
+            cols = [jnp.minimum((word >> 9) & 31, zero_block) for word in words]
+            left = jnp.concatenate([vals[word & 511] for word in words], axis=1)
+            right = jnp.concatenate([panel[col] for col in cols], axis=0)
+            row = words[0] >> 14
             total[row] += jnp.dot(left, right, preferred_element_type=jnp.float32)
 
     if not last:
@@ -196,18 +277,14 @@
     blocks = sum(piece.shape[0] for piece in pieces)
     width = pieces[0].shape[2]
     wide = width + (BLK if with_degree else 0)
-    out_shape = [pltpu.VMEM((2 * HALF_BLOCKS, BLK, wide), jnp.float32)]
+    out_shape = [pltpu.VMEM(total_shape, jnp.float32)]
     scratch = [
         pltpu.VMEM((blocks + 1, BLK, wide), jnp.bfloat16),
         pltpu.SemaphoreType.DMA((len(pieces),)),
     ]
-    operands = [*plan, vals, *pieces]
-    in_specs = [smem_spec] * 3 + [vmem_spec] + [any_spec] * len(pieces)
-    aliases = {}
-    if section > 0:
-        aliases = {len(operands): 0}
-        operands.append(total)
-        in_specs.append(vmem_spec)
+    operands = [plan, vals, *pieces, total]
+    in_specs = [smem_spec, vmem_spec] + [any_spec] * len(pieces) + [vmem_spec]
+    aliases = {len(operands) - 1: 0}
     if section >= 1:
         rows = DEV_BLOCKS * BLK + (16 if with_degree else 0)
         out_shape.append(jax.ShapeDtypeStruct((DEST, rows, width), jnp.bfloat16))
@@ -227,8 +304,8 @@
     )(*operands)
 
 
-def layer_product(plan, vals, hops, with_degree):
-    (total,) = product(plan, vals, hops[0], None, 0, with_degree)
+def layer_product(plan, vals, total, hops, with_degree):
+    (total,) = product(plan, vals, hops[0], total, 0, with_degree)
     total, send = product(plan, vals, hops[1], total, 1, with_degree)
     total, keep = product(plan, vals, hops[1], total, 2, with_degree)
     return send, keep
@@ -287,52 +364,15 @@
     return out.reshape(-1)
 
 
-def make_plan(row_ids, col_ids, live_count, row_at, col_at):
-    capacity = row_ids.shape[0]
-    sections = 3
-    slots = jnp.arange(capacity, dtype=jnp.int32)
-    live = slots < live_count
-    y, z_hi, core = col_at // 4, (col_at // 2) % 2, col_at % 2
-    dest, j = row_ids // DEV_BLOCKS, row_ids % DEV_BLOCKS
-    dy = (dest // 4 - y) % N_Y
-    dz = (dest // 2 + z_hi) % 2
-    keep = 1 - (dest + core) % 2
-    row = keep * HALF_BLOCKS + (dy * 2 + dz) * DEV_BLOCKS + j
-    hop, col = relative_block(col_ids, row_at)
-    section = jnp.where(hop == 1, 1 + keep, 0)
-    key = section * (2 * HALF_BLOCKS) + row
-    same = (key[:, None] == key[None, :]) & live[None, :]
-    within = jnp.sum((same & (slots[None, :] < slots[:, None])).astype(jnp.int32), axis=1)
-    opens = live & (within % 2 == 0)
-    ahead = (key[None, :] < key[:, None]) & (section[None, :] == section[:, None]) & opens[None, :]
-    pair = jnp.sum(ahead.astype(jnp.int32), axis=1) + within // 2
-    longest = -(-((capacity + 2 * HALF_BLOCKS) // 2) // UNROLL) * UNROLL
-    place = jnp.where(live, (section * longest + pair) * 2 + within % 2, -1)
-    places = jnp.arange(sections * longest, dtype=jnp.int32)
-    empty = 31 * 512
-    word = slots + col * 512 + row * (512 * 32) - empty
-
-    def lay(side):
-        hit = place[None, :] == (places * 2 + side)[:, None]
-        found = jnp.sum(jnp.where(hit, word[None, :], 0), axis=1)
-        return (empty + found).reshape(sections, longest)
-
-    count = jnp.sum(
-        (opens[None, :] & (section[None, :] == jnp.arange(sections)[:, None])).astype(jnp.int32),
-        axis=1,
-    )
-    return count, lay(0), lay(1)
-
-
 def relative_block(ids, row_at):
-    owner, j = ids // DEV_BLOCKS, ids % DEV_BLOCKS
-    offset = ((owner // 2 - row_at // 2) % N_X) * 2 + (owner + row_at) % 2
+    owner = ids >> 2
+    offset = (((owner >> 1) - (row_at >> 1)) & 3) * 2 + ((owner + row_at) & 1)
     hop = jnp.zeros_like(ids)
     place = jnp.zeros_like(ids)
     for at in range(N_ROW):
         hop = jnp.where(offset == at, HOP[at], hop)
         place = jnp.where(offset == at, PLACE[at], place)
-    return hop, place * DEV_BLOCKS + j
+    return hop, place * DEV_BLOCKS + (ids & 3)
 
 
 def per_device(
@@ -349,16 +389,18 @@
     w_attr,
     attr_bias,
 ):
-    vals = preload(adj_values[0, 0])
     hidden_size = w_rest.shape[1]
     row_at = lax.axis_index("row")
     col_at = lax.axis_index("col")
-    plan = make_plan(adj_rows[0, 0], adj_cols[0, 0], adj_count[0, 0], row_at, col_at)
+    vals, total, plan = begin(
+        adj_values[0, 0], adj_rows[0, 0], adj_cols[0, 0], adj_count[0, 0], row_at, col_at
+    )
     nodes_dev = attributes.shape[0]
     w_near, w_self = w_first[:, :hidden_size], w_first[:, hidden_size:]
     own_part = jnp.dot(attributes, w_self, preferred_element_type=jnp.float32)
 
-    summed = scatter_col(*layer_product(plan, vals, gather_row(attributes), True))
+    send, keep = layer_product(plan, vals, total, gather_row(attributes, True), True)
+    summed = scatter_col(send, keep)
     degree = 1.0 + summed[nodes_dev : nodes_dev + DEV_BLOCKS].reshape(-1)
     row_scale = lax.rsqrt(degree)[:, None]
     aggregate = summed[:nodes_dev]
@@ -373,17 +415,17 @@
     features = jnp.dot(
         hidden, w_rest[0][:, :hidden_size], preferred_element_type=jnp.float32
     ).astype(jnp.bfloat16)
-    hops = gather_row(features)
+    hops = gather_row(features, True)
     own_part = (
         jnp.dot(hidden, w_rest[0][:, hidden_size:], preferred_element_type=jnp.float32)
         + layer_bias[0]
     )
-    summed = scatter_col(*layer_product(plan, vals, hops, False))
+    summed = scatter_col(*layer_product(plan, vals, cleared(keep), hops, False))
     hidden = jnp.tanh(row_scale * summed + own_part).astype(jnp.bfloat16)
 
     hop, place = relative_block(pair_ids, row_at)
     return score(
-        gather_row(hidden),
+        gather_row(hidden, False),
         hop * (N_ROW // 2) * DEV_BLOCKS + place,
         hidden,
         struct_target.reshape(nodes_dev, -1),

time: 144 us -> 138 us (0.958)
  starting transfers between devices: 74.5 us -> 57.6 us
  waiting for transfers between devices: 37.2 us -> 47.8 us
  other arithmetic: 4 us -> 1.47 us
    ppermute x16, starting transfers between devices: 39.1 us -> 29.7 us  [shift_col(): return lax.ppermute(value, 'col', perm)]
    ppermute x24 -> x20, starting transfers between devices: 35.4 us -> 27.9 us  [shift_row(): return lax.ppermute(value, 'row', perm)]
    ppermute x24 -> x20, waiting for transfers between devices: 20.1 us -> 26 us  [shift_row(): return lax.ppermute(value, 'row', perm)]
    ppermute x16, waiting for transfers between devices: 17.1 us -> 21.8 us  [shift_col(): return lax.ppermute(value, 'col', perm)]
    pallas_call x1 -> x2, Pallas kernels: 4.62 us -> 5.73 us  [the longest x1 5.12 us: begin(): pl.pallas_call(begin_kernel, out_shape=[pltpu.VMEM(vals.shape, vals.dtype...]
  transfers between devices with their start and end apart: 40 -> 36, of which waited for: 11 -> 16; matrix products, arithmetic and copies ran while one was open for 2% -> 1% of each run, Pallas kernels for 13% -> 14%
where the time goes in v4:
time: 138 us; the launch traced here: 137 us
  starting transfers between devices  57.6 us (42%)
  waiting for transfers between devices  47.8 us (35%)
  Pallas kernels  26.8 us (19%)
  local copies, waits for them, and re-layouts  1.5 us (1%)
  other arithmetic  1.47 us (1%)
    ppermute x16, starting transfers between devices, shift_col(): return lax.ppermute(value, 'col', perm)  29.7 us
    ppermute x20, starting transfers between devices, shift_row(): return lax.ppermute(value, 'row', perm)  27.9 us
    ppermute x20, waiting for transfers between devices, shift_row(): return lax.ppermute(value, 'row', perm)  26 us
    ppermute x16, waiting for transfers between devices, shift_col(): return lax.ppermute(value, 'col', perm)  21.8 us
    pallas_call x6, Pallas kernels, product(): pl.pallas_call(functools.partial(product_kernel, section, len(pieces)), o...  18.5 us
    pallas_call x1, Pallas kernels, begin(): pl.pallas_call(begin_kernel, out_shape=[pltpu.VMEM(vals.shape, vals.dtype...  5.12 us
  transfers between devices with their start and end apart: 36, of which 16 were waited for; matrix products, arithmetic and copies ran while one was open for 1% of the time, Pallas kernels for 14%

profile of v4, /device:TPU:0, one launch (start us, length us, event | category | flops | bytes accessed | tf_op | source)
XLA Modules:
  0.0 137.3 jit_solution(1627048439062178877)
XLA Ops:
  2.0 2.8 %collective-permute-start = (bf16[512,128]{1,0:T(8,128)(2,1)}, bf16[512,128]{1,0:T(8,128)(2,1)S(1)}, u32[]{:S(2)}, u32[]{:S(2)}) collective-permute-start(bf16[512,128]{1,0:T(8,128)(2,1)} %attributes.1), channel_id=1, source_target_pairs={{0,96},{16,112},{32,0},{48,16},{64,32},{80,48},{96,64},{112,80},{1... | collective-permute-start | bytes 393224 | tf_op jit(solution)/shard_map/ppermute | solution.py:37
  6.9 5.1 %begin.1 = (bf16[384,128,128]{2,1,0:T(8,128)(2,1)S(1)}, f32[64,128,256]{2,1,0:T(8,128)S(1)}, s32[5,256]{1,0:T(8,128)S(1)}) custom-call(s32[3]{0:T(128)S(1)} %pad_add_fusion.place_ref, s32[1,384]{1,0:T(1,128)S(1)} %bitcast.137, s32[1,384]{1,0:T(1,128)S(1)} %bitcast.138, bf16[384,128,128]{2,1,0:T(8,128)(2,1)} %bitcast.140), custom_call_target="tpu_custom_call" | custom-call | bytes 12582912 | tf_op jit(solution)/shard_map/begin/pallas_call | solution.py:175
  12.0 3.3 %collective-permute-start.2 = (bf16[1024,128]{1,0:T(8,128)(2,1)S(1)}, bf16[1024,128]{1,0:T(8,128)(2,1)S(1)}, u32[]{:S(2)}, u32[]{:S(2)}) collective-permute-start(bf16[1024,128]{1,0:T(8,128)(2,1)S(1)} %pad_maximum_fusion.1), channel_id=1, source_target_pairs={{0,96},{16,112},{32,0},{48,16},{64,32},{80,48},{96,64},{112,80},{1... | collective-permute-start | bytes 786440 | tf_op jit(solution)/shard_map/ppermute | solution.py:37
  15.4 4.2 %product_near.2.refs_3_ = f32[64,128,256]{2,1,0:T(8,128)S(1)} custom-call(s32[5,256]{1,0:T(8,128)S(1)} %get-tuple-element.14.plan, bf16[384,128,128]{2,1,0:T(8,128)(2,1)S(1)} %get-tuple-element.15.vals, bf16[4,128,128]{2,1,0:T(8,128)(2,1)S(1)} %bitcast.111, bf16[4,128,128]{2,1,0:T(8,128)(2,1)S(1)} %bitcast.127, ...), custom_call_target="tpu_custom_call", output_to_operand_aliasing={{}: (6, {})} | custom-call | flops 6000000000 | bytes 1048576 | tf_op jit(solution)/shard_map/product_near/pallas_call | solution.py:294
  19.6 2.5 %collective-permute-done.3 = bf16[512,128]{1,0:T(8,128)(2,1)S(1)} collective-permute-done((bf16[512,128]{1,0:T(8,128)(2,1)S(1)}, bf16[512,128]{1,0:T(8,128)(2,1)S(1)}, u32[]{:S(2)}, u32[]{:S(2)}) %collective-permute-start.3) | collective-permute-done | bytes 131104 | tf_op jit(solution)/shard_map/ppermute | solution.py:37
  25.7 2.9 %product_keep.2 = (f32[64,128,256]{2,1,0:T(8,128)S(1)}, bf16[8,528,128]{2,1,0:T(8,128)(2,1)S(1)}) custom-call(s32[5,256]{1,0:T(8,128)S(1)} %get-tuple-element.14.plan, bf16[384,128,128]{2,1,0:T(8,128)(2,1)S(1)} %get-tuple-element.15.vals, bf16[8,128,128]{2,1,0:T(8,128)(2,1)S(1)} %bitcast.113, ...), custom_call_target="tpu_custom_call", output_to_operand_aliasing={{0}: (5, {})} | custom-call | flops 3000000000 | bytes 1048576 | tf_op jit(solution)/shard_map/product_keep/pallas_call | solution.py:294
  28.9 4.4 %collective-permute-start.7 = (bf16[528,128]{1,0:T(8,128)(2,1)S(1)}, bf16[528,128]{1,0:T(8,128)(2,1)S(1)}, u32[]{:S(2)}, u32[]{:S(2)}) collective-permute-start(bf16[528,128]{1,0:T(8,128)(2,1)S(1)} %get-tuple-element.32), channel_id=1, source_target_pairs={{0,4},{1,5},{2,6},{3,7},{4,8},{5,9},{6,10},{7,11},{8,12},{9,13},{1... | collective-permute-start | bytes 405512 | tf_op jit(solution)/shard_map/ppermute | solution.py:47
  34.8 3.2 %collective-permute-start.11 = (bf16[528,128]{1,0:T(8,128)(2,1)S(1)}, bf16[528,128]{1,0:T(8,128)(2,1)S(1)}, u32[]{:S(2)}, u32[]{:S(2)}) collective-permute-start(bf16[528,128]{1,0:T(8,128)(2,1)S(1)} %get-tuple-element.35), channel_id=1, source_target_pairs={{0,6},{1,7},{2,4},{3,5},{4,10},{5,11},{6,8},{7,9},{8,14},{9,15},{1... | collective-permute-start | bytes 405512 | tf_op jit(solution)/shard_map/ppermute | solution.py:47
  41.1 2.9 %collective-permute-start.10 = (bf16[528,128]{1,0:T(8,128)(2,1)S(1)}, bf16[528,128]{1,0:T(8,128)(2,1)S(1)}, u32[]{:S(2)}, u32[]{:S(2)}) collective-permute-start(bf16[528,128]{1,0:T(8,128)(2,1)S(1)} %get-tuple-element.31), channel_id=1, source_target_pairs={{0,14},{1,15},{2,12},{3,13},{4,2},{5,3},{6,0},{7,1},{8,6},{9,7},{1... | collective-permute-start | bytes 405512 | tf_op jit(solution)/shard_map/ppermute | solution.py:47
  44.7 4.5 %collective-permute-done.13 = bf16[528,128]{1,0:T(8,128)(2,1)S(1)} collective-permute-done((bf16[528,128]{1,0:T(8,128)(2,1)S(1)}, bf16[528,128]{1,0:T(8,128)(2,1)S(1)}, u32[]{:S(2)}, u32[]{:S(2)}) %collective-permute-start.13) | collective-permute-done | bytes 135200 | tf_op jit(solution)/shard_map/ppermute | solution.py:47
  59.8 3.3 %collective-permute-start.16 = (bf16[1024,256]{1,0:T(8,128)(2,1)S(1)}, bf16[1024,256]{1,0:T(8,128)(2,1)S(1)}, u32[]{:S(2)}, u32[]{:S(2)}) collective-permute-start(bf16[1024,256]{1,0:T(8,128)(2,1)S(1)} %pad_maximum_fusion), channel_id=1, source_target_pairs={{0,96},{16,112},{32,0},{48,16},{64,32},{80,48},{96,64},{112,80},{1... | collective-permute-start | bytes 1572872 | tf_op jit(solution)/shard_map/ppermute | solution.py:37
  63.1 4.1 %product_near.3.refs_3_ = f32[64,128,256]{2,1,0:T(8,128)S(1)} custom-call(s32[5,256]{1,0:T(8,128)S(1)} %get-tuple-element.14.plan, bf16[384,128,128]{2,1,0:T(8,128)(2,1)S(1)} %get-tuple-element.15.vals, bf16[4,128,256]{2,1,0:T(8,128)(2,1)S(1)} %bitcast.118, bf16[4,128,256]{2,1,0:T(8,128)(2,1)S(1)} %bitcast.119, ...), custom_call_target="tpu_custom_call", output_to_operand_aliasing={{}: (6, {})} | custom-call | flops 6000000000 | bytes 1048576 | tf_op jit(solution)/shard_map/product_near/pallas_call | solution.py:294
  67.3 6.3 %collective-permute-done.17 = bf16[512,256]{1,0:T(8,128)(2,1)S(1)} collective-permute-done((bf16[512,256]{1,0:T(8,128)(2,1)S(1)}, bf16[512,256]{1,0:T(8,128)(2,1)S(1)}, u32[]{:S(2)}, u32[]{:S(2)}) %collective-permute-start.17) | collective-permute-done | bytes 262176 | tf_op jit(solution)/shard_map/ppermute | solution.py:37
  78.3 2.7 %product_keep.3 = (f32[64,128,256]{2,1,0:T(8,128)S(1)}, bf16[8,512,256]{2,1,0:T(8,128)(2,1)S(1)}) custom-call(s32[5,256]{1,0:T(8,128)S(1)} %get-tuple-element.14.plan, bf16[384,128,128]{2,1,0:T(8,128)(2,1)S(1)} %get-tuple-element.15.vals, bf16[8,128,256]{2,1,0:T(8,128)(2,1)S(1)} %bitcast.109, ...), custom_call_target="tpu_custom_call", output_to_operand_aliasing={{0}: (5, {})} | custom-call | flops 3000000000 | bytes 1048576 | tf_op jit(solution)/shard_map/product_keep/pallas_call | solution.py:294
  82.8 3.7 %collective-permute-start.21 = (bf16[512,256]{1,0:T(8,128)(2,1)S(1)}, bf16[512,256]{1,0:T(8,128)(2,1)S(1)}, u32[]{:S(2)}, u32[]{:S(2)}) collective-permute-start(bf16[512,256]{1,0:T(8,128)(2,1)S(1)} %get-tuple-element.25), channel_id=1, source_target_pairs={{0,4},{1,5},{2,6},{3,7},{4,8},{5,9},{6,10},{7,11},{8,12},{9,13},{1... | collective-permute-start | bytes 786440 | tf_op jit(solution)/shard_map/ppermute | solution.py:47
  88.9 3.2 %collective-permute-start.26 = (bf16[512,256]{1,0:T(8,128)(2,1)S(1)}, bf16[512,256]{1,0:T(8,128)(2,1)S(1)}, u32[]{:S(2)}, u32[]{:S(2)}) collective-permute-start(bf16[512,256]{1,0:T(8,128)(2,1)S(1)} %get-tuple-element.27), channel_id=1, source_target_pairs={{0,12},{1,13},{2,14},{3,15},{4,0},{5,1},{6,2},{7,3},{8,4},{9,5},{1... | collective-permute-start | bytes 786440 | tf_op jit(solution)/shard_map/ppermute | solution.py:47
  93.2 2.5 %collective-permute-done.23 = bf16[512,256]{1,0:T(8,128)(2,1)S(1)} collective-permute-done((bf16[512,256]{1,0:T(8,128)(2,1)S(1)}, bf16[512,256]{1,0:T(8,128)(2,1)S(1)}, u32[]{:S(2)}, u32[]{:S(2)}) %collective-permute-start.23) | collective-permute-done | bytes 262176 | tf_op jit(solution)/shard_map/ppermute | solution.py:47
  96.0 3.6 %collective-permute-start.24 = (bf16[512,256]{1,0:T(8,128)(2,1)S(1)}, bf16[512,256]{1,0:T(8,128)(2,1)S(1)}, u32[]{:S(2)}, u32[]{:S(2)}) collective-permute-start(bf16[512,256]{1,0:T(8,128)(2,1)S(1)} %get-tuple-element.24), channel_id=1, source_target_pairs={{0,14},{1,15},{2,12},{3,13},{4,2},{5,3},{6,0},{7,1},{8,6},{9,7},{1... | collective-permute-start | bytes 786440 | tf_op jit(solution)/shard_map/ppermute | solution.py:47
  102.0 9.7 %collective-permute-done.27 = bf16[512,256]{1,0:T(8,128)(2,1)S(1)} collective-permute-done((bf16[512,256]{1,0:T(8,128)(2,1)S(1)}, bf16[512,256]{1,0:T(8,128)(2,1)S(1)}, u32[]{:S(2)}, u32[]{:S(2)}) %collective-permute-start.27) | collective-permute-done | bytes 262176 | tf_op jit(solution)/shard_map/ppermute | solution.py:47
  116.1 3.8 %collective-permute-done.29 = bf16[512,256]{1,0:T(8,128)(2,1)S(1)} collective-permute-done((bf16[512,256]{1,0:T(8,128)(2,1)S(1)}, bf16[512,256]{1,0:T(8,128)(2,1)S(1)}, u32[]{:S(2)}, u32[]{:S(2)}) %collective-permute-start.29) | collective-permute-done | bytes 262176 | tf_op jit(solution)/shard_map/ppermute | solution.py:37
  119.8 2.6 %collective-permute-start.31 = (bf16[512,256]{1,0:T(8,128)(2,1)S(1)}, bf16[512,256]{1,0:T(8,128)(2,1)S(1)}, u32[]{:S(2)}, u32[]{:S(2)}) collective-permute-start(bf16[512,256]{1,0:T(8,128)(2,1)S(1)} %collective-permute-done.29), channel_id=1, source_target_pairs={{0,96},{16,112},{32,0},{48,16},{64,32},{80,48},{96,64},{112,80},{1... | collective-permute-start | bytes 786440 | tf_op jit(solution)/shard_map/ppermute | solution.py:37
  124.1 4.2 %collective-permute-start.35 = (bf16[256,256]{1,0:T(8,128)(2,1)S(1)}, bf16[256,256]{1,0:T(8,128)(2,1)S(1)}, u32[]{:S(2)}, u32[]{:S(2)}) collective-permute-start(bf16[256,256]{1,0:T(8,128)(2,1)S(1)} %slice.181), channel_id=1, source_target_pairs={{0,112},{16,96},{32,16},{48,0},{64,48},{80,32},{96,80},{112,64},{1... | collective-permute-start | bytes 393224 | tf_op jit(solution)/shard_map/ppermute | solution.py:37
  128.3 6.0 %collective-permute-done.34 = bf16[256,256]{1,0:T(8,128)(2,1)S(1)} collective-permute-done((bf16[256,256]{1,0:T(8,128)(2,1)S(1)}, bf16[256,256]{1,0:T(8,128)(2,1)S(1)}, u32[]{:S(2)}, u32[]{:S(2)}) %collective-permute-start.34) | collective-permute-done | bytes 131104 | tf_op jit(solution)/shard_map/ppermute | solution.py:37
  134.6 2.6 %score.1 = f32[4,128]{1,0:T(4,128)} custom-call(s32[4,4]{1,0:T(4,128)S(1)} %add_add_fusion.pair_ref, bf16[512,256]{1,0:T(8,128)(2,1)S(1)} %fusion.12.own, bf16[512,512]{1,0:T(8,128)(2,1)S(1)} %bitcast.110, bf16[512,128]{1,0:T(8,128)(2,1)S(1)} %copy-done, bf16[256,128]{1,0:T(8,128)(2,1)S(1)} %copy-done.1, f32[1,128]{1,0:T(1,128)S(1)} %bitcast.139, ...), custom_call_target="tpu_custom_call" | custom-call | tf_op jit(solution)/shard_map/score/pallas_call | solution.py:352
  (96 shorter events, 42.2 us)
Async XLA Ops:
  0.0 12.0 %collective-permute-start.1 = (bf16[512,128]{1,0:T(8,128)(2,1)}, bf16[512,128]{1,0:T(8,128)(2,1)S(1)}, u32[]{:S(2)}, u32[]{:S(2)}) collective-permute-start(bf16[512,128]{1,0:T(8,128)(2,1)} %attributes.1), channel_id=1, source_target_pairs={{0,16},{16,0},{32,48},{48,32},{64,80},{80,64},{96,112},{112,96},{1... | collective-permute-start | bytes 393224 | tf_op jit(solution)/shard_map/ppermute | solution.py:37
  2.0 10.0 %collective-permute-start = (bf16[512,128]{1,0:T(8,128)(2,1)}, bf16[512,128]{1,0:T(8,128)(2,1)S(1)}, u32[]{:S(2)}, u32[]{:S(2)}) collective-permute-start(bf16[512,128]{1,0:T(8,128)(2,1)} %attributes.1), channel_id=1, source_target_pairs={{0,96},{16,112},{32,0},{48,16},{64,32},{80,48},{96,64},{112,80},{1... | collective-permute-start | bytes 393224 | tf_op jit(solution)/shard_map/ppermute | solution.py:37
  4.8 10.6 %collective-permute-start.4 = (bf16[512,128]{1,0:T(8,128)(2,1)}, bf16[512,128]{1,0:T(8,128)(2,1)S(1)}, u32[]{:S(2)}, u32[]{:S(2)}) collective-permute-start(bf16[512,128]{1,0:T(8,128)(2,1)} %attributes.1), channel_id=1, source_target_pairs={{0,32},{16,48},{32,64},{48,80},{64,96},{80,112},{96,0},{112,16},{1... | collective-permute-start | bytes 393224 | tf_op jit(solution)/shard_map/ppermute | solution.py:37
  12.0 11.2 %collective-permute-start.2 = (bf16[1024,128]{1,0:T(8,128)(2,1)S(1)}, bf16[1024,128]{1,0:T(8,128)(2,1)S(1)}, u32[]{:S(2)}, u32[]{:S(2)}) collective-permute-start(bf16[1024,128]{1,0:T(8,128)(2,1)S(1)} %pad_maximum_fusion.1), channel_id=1, source_target_pairs={{0,96},{16,112},{32,0},{48,16},{64,32},{80,48},{96,64},{112,80},{1... | collective-permute-start | bytes 786440 | tf_op jit(solution)/shard_map/ppermute | solution.py:37
  28.9 12.1 %collective-permute-start.7 = (bf16[528,128]{1,0:T(8,128)(2,1)S(1)}, bf16[528,128]{1,0:T(8,128)(2,1)S(1)}, u32[]{:S(2)}, u32[]{:S(2)}) collective-permute-start(bf16[528,128]{1,0:T(8,128)(2,1)S(1)} %get-tuple-element.32), channel_id=1, source_target_pairs={{0,4},{1,5},{2,6},{3,7},{4,8},{5,9},{6,10},{7,11},{8,12},{9,13},{1... | collective-permute-start | bytes 405512 | tf_op jit(solution)/shard_map/ppermute | solution.py:47
  34.8 9.9 %collective-permute-start.11 = (bf16[528,128]{1,0:T(8,128)(2,1)S(1)}, bf16[528,128]{1,0:T(8,128)(2,1)S(1)}, u32[]{:S(2)}, u32[]{:S(2)}) collective-permute-start(bf16[528,128]{1,0:T(8,128)(2,1)S(1)} %get-tuple-element.35), channel_id=1, source_target_pairs={{0,6},{1,7},{2,4},{3,5},{4,10},{5,11},{6,8},{7,9},{8,14},{9,15},{1... | collective-permute-start | bytes 405512 | tf_op jit(solution)/shard_map/ppermute | solution.py:47
  39.5 9.7 %collective-permute-start.13 = (bf16[528,128]{1,0:T(8,128)(2,1)S(1)}, bf16[528,128]{1,0:T(8,128)(2,1)S(1)}, u32[]{:S(2)}, u32[]{:S(2)}) collective-permute-start(bf16[528,128]{1,0:T(8,128)(2,1)S(1)} %get-tuple-element.33), channel_id=1, source_target_pairs={{0,2},{1,3},{2,0},{3,1},{4,6},{5,7},{6,4},{7,5},{8,10},{9,11},{10,... | collective-permute-start | bytes 405512 | tf_op jit(solution)/shard_map/ppermute | solution.py:47
  53.8 9.3 %collective-permute-start.18 = (bf16[512,256]{1,0:T(8,128)(2,1)S(1)}, bf16[512,256]{1,0:T(8,128)(2,1)S(1)}, u32[]{:S(2)}, u32[]{:S(2)}) collective-permute-start(bf16[512,256]{1,0:T(8,128)(2,1)S(1)} %convolution_convert_fusion), channel_id=1, source_target_pairs={{0,32},{16,48},{32,64},{48,80},{64,96},{80,112},{96,0},{112,16},{1... | collective-permute-start | bytes 786440 | tf_op jit(solution)/shard_map/ppermute | solution.py:37
  59.8 16.0 %collective-permute-start.16 = (bf16[1024,256]{1,0:T(8,128)(2,1)S(1)}, bf16[1024,256]{1,0:T(8,128)(2,1)S(1)}, u32[]{:S(2)}, u32[]{:S(2)}) collective-permute-start(bf16[1024,256]{1,0:T(8,128)(2,1)S(1)} %pad_maximum_fusion), channel_id=1, source_target_pairs={{0,96},{16,112},{32,0},{48,16},{64,32},{80,48},{96,64},{112,80},{1... | collective-permute-start | bytes 1572872 | tf_op jit(solution)/shard_map/ppermute | solution.py:37
  63.1 10.5 %collective-permute-start.17 = (bf16[512,256]{1,0:T(8,128)(2,1)S(1)}, bf16[512,256]{1,0:T(8,128)(2,1)S(1)}, u32[]{:S(2)}, u32[]{:S(2)}) collective-permute-start(bf16[512,256]{1,0:T(8,128)(2,1)S(1)} %collective-permute-done.15), channel_id=1, source_target_pairs={{0,32},{16,48},{32,64},{48,80},{64,96},{80,112},{96,0},{112,16},{1... | collective-permute-start | bytes 786440 | tf_op jit(solution)/shard_map/ppermute | solution.py:37
  63.1 12.7 %collective-permute-start.19 = (bf16[512,256]{1,0:T(8,128)(2,1)S(1)}, bf16[512,256]{1,0:T(8,128)(2,1)S(1)}, u32[]{:S(2)}, u32[]{:S(2)}) collective-permute-start(bf16[512,256]{1,0:T(8,128)(2,1)S(1)} %collective-permute-done.18), channel_id=1, source_target_pairs={{0,48},{16,32},{32,80},{48,64},{64,112},{80,96},{96,16},{112,0},{1... | collective-permute-start | bytes 786440 | tf_op jit(solution)/shard_map/ppermute | solution.py:37
  82.8 10.3 %collective-permute-start.21 = (bf16[512,256]{1,0:T(8,128)(2,1)S(1)}, bf16[512,256]{1,0:T(8,128)(2,1)S(1)}, u32[]{:S(2)}, u32[]{:S(2)}) collective-permute-start(bf16[512,256]{1,0:T(8,128)(2,1)S(1)} %get-tuple-element.25), channel_id=1, source_target_pairs={{0,4},{1,5},{2,6},{3,7},{4,8},{5,9},{6,10},{7,11},{8,12},{9,13},{1... | collective-permute-start | bytes 786440 | tf_op jit(solution)/shard_map/ppermute | solution.py:47
  86.5 15.5 %collective-permute-start.25 = (bf16[512,256]{1,0:T(8,128)(2,1)S(1)}, bf16[512,256]{1,0:T(8,128)(2,1)S(1)}, u32[]{:S(2)}, u32[]{:S(2)}) collective-permute-start(bf16[512,256]{1,0:T(8,128)(2,1)S(1)} %get-tuple-element.28), channel_id=1, source_target_pairs={{0,6},{1,7},{2,4},{3,5},{4,10},{5,11},{6,8},{7,9},{8,14},{9,15},{1... | collective-permute-start | bytes 786440 | tf_op jit(solution)/shard_map/ppermute | solution.py:47
  88.9 13.1 %collective-permute-start.26 = (bf16[512,256]{1,0:T(8,128)(2,1)S(1)}, bf16[512,256]{1,0:T(8,128)(2,1)S(1)}, u32[]{:S(2)}, u32[]{:S(2)}) collective-permute-start(bf16[512,256]{1,0:T(8,128)(2,1)S(1)} %get-tuple-element.27), channel_id=1, source_target_pairs={{0,12},{1,13},{2,14},{3,15},{4,0},{5,1},{6,2},{7,3},{8,4},{9,5},{1... | collective-permute-start | bytes 786440 | tf_op jit(solution)/shard_map/ppermute | solution.py:47
  92.1 19.6 %collective-permute-start.27 = (bf16[512,256]{1,0:T(8,128)(2,1)S(1)}, bf16[512,256]{1,0:T(8,128)(2,1)S(1)}, u32[]{:S(2)}, u32[]{:S(2)}) collective-permute-start(bf16[512,256]{1,0:T(8,128)(2,1)S(1)} %get-tuple-element.26), channel_id=1, source_target_pairs={{0,2},{1,3},{2,0},{3,1},{4,6},{5,7},{6,4},{7,5},{8,10},{9,11},{10,... | collective-permute-start | bytes 786440 | tf_op jit(solution)/shard_map/ppermute | solution.py:47
  95.9 15.8 %collective-permute-start.22 = (bf16[512,256]{1,0:T(8,128)(2,1)S(1)}, bf16[512,256]{1,0:T(8,128)(2,1)S(1)}, u32[]{:S(2)}, u32[]{:S(2)}) collective-permute-start(bf16[512,256]{1,0:T(8,128)(2,1)S(1)} %get-tuple-element.23), channel_id=1, source_target_pairs={{0,4},{1,5},{2,6},{3,7},{4,8},{5,9},{6,10},{7,11},{8,12},{9,13},{1... | collective-permute-start | bytes 786440 | tf_op jit(solution)/shard_map/ppermute | solution.py:47
  96.0 15.7 %collective-permute-start.24 = (bf16[512,256]{1,0:T(8,128)(2,1)S(1)}, bf16[512,256]{1,0:T(8,128)(2,1)S(1)}, u32[]{:S(2)}, u32[]{:S(2)}) collective-permute-start(bf16[512,256]{1,0:T(8,128)(2,1)S(1)} %get-tuple-element.24), channel_id=1, source_target_pairs={{0,14},{1,15},{2,12},{3,13},{4,2},{5,3},{6,0},{7,1},{8,6},{9,7},{1... | collective-permute-start | bytes 786440 | tf_op jit(solution)/shard_map/ppermute | solution.py:47
  113.4 9.9 %collective-permute-start.28 = (bf16[512,256]{1,0:T(8,128)(2,1)S(1)}, bf16[512,256]{1,0:T(8,128)(2,1)S(1)}, u32[]{:S(2)}, u32[]{:S(2)}) collective-permute-start(bf16[512,256]{1,0:T(8,128)(2,1)S(1)} %fusion.12.own), channel_id=1, source_target_pairs={{0,16},{16,0},{32,48},{48,32},{64,80},{80,64},{96,112},{112,96},{1... | collective-permute-start | bytes 786440 | tf_op jit(solution)/shard_map/ppermute | solution.py:37
  114.2 9.8 %collective-permute-start.30 = (bf16[512,256]{1,0:T(8,128)(2,1)S(1)}, bf16[512,256]{1,0:T(8,128)(2,1)S(1)}, u32[]{:S(2)}, u32[]{:S(2)}) collective-permute-start(bf16[512,256]{1,0:T(8,128)(2,1)S(1)} %fusion.12.own), channel_id=1, source_target_pairs={{0,32},{16,48},{32,64},{48,80},{64,96},{80,112},{96,0},{112,16},{1... | collective-permute-start | bytes 786440 | tf_op jit(solution)/shard_map/ppermute | solution.py:37
  119.8 14.5 %collective-permute-start.31 = (bf16[512,256]{1,0:T(8,128)(2,1)S(1)}, bf16[512,256]{1,0:T(8,128)(2,1)S(1)}, u32[]{:S(2)}, u32[]{:S(2)}) collective-permute-start(bf16[512,256]{1,0:T(8,128)(2,1)S(1)} %collective-permute-done.29), channel_id=1, source_target_pairs={{0,96},{16,112},{32,0},{48,16},{64,32},{80,48},{96,64},{112,80},{1... | collective-permute-start | bytes 786440 | tf_op jit(solution)/shard_map/ppermute | solution.py:37
  122.4 12.2 %collective-permute-start.32 = (bf16[512,256]{1,0:T(8,128)(2,1)S(1)}, bf16[512,256]{1,0:T(8,128)(2,1)S(1)}, u32[]{:S(2)}, u32[]{:S(2)}) collective-permute-start(bf16[512,256]{1,0:T(8,128)(2,1)S(1)} %collective-permute-done.29), channel_id=1, source_target_pairs={{0,16},{16,0},{32,48},{48,32},{64,80},{80,64},{96,112},{112,96},{1... | collective-permute-start | bytes 786440 | tf_op jit(solution)/shard_map/ppermute | solution.py:37
  123.3 11.3 %collective-permute-start.33 = (bf16[512,256]{1,0:T(8,128)(2,1)S(1)}, bf16[512,256]{1,0:T(8,128)(2,1)S(1)}, u32[]{:S(2)}, u32[]{:S(2)}) collective-permute-start(bf16[512,256]{1,0:T(8,128)(2,1)S(1)} %collective-permute-done.28), channel_id=1, source_target_pairs={{0,32},{16,48},{32,64},{48,80},{64,96},{80,112},{96,0},{112,16},{1... | collective-permute-start | bytes 786440 | tf_op jit(solution)/shard_map/ppermute | solution.py:37
  124.0 10.3 %collective-permute-start.34 = (bf16[256,256]{1,0:T(8,128)(2,1)S(1)}, bf16[256,256]{1,0:T(8,128)(2,1)S(1)}, u32[]{:S(2)}, u32[]{:S(2)}) collective-permute-start(bf16[256,256]{1,0:T(8,128)(2,1)S(1)} %slice.180), channel_id=1, source_target_pairs={{0,48},{16,32},{32,80},{48,64},{64,112},{80,96},{96,16},{112,0},{1... | collective-permute-start | bytes 393224 | tf_op jit(solution)/shard_map/ppermute | solution.py:37
  124.1 10.2 %collective-permute-start.35 = (bf16[256,256]{1,0:T(8,128)(2,1)S(1)}, bf16[256,256]{1,0:T(8,128)(2,1)S(1)}, u32[]{:S(2)}, u32[]{:S(2)}) collective-permute-start(bf16[256,256]{1,0:T(8,128)(2,1)S(1)} %slice.181), channel_id=1, source_target_pairs={{0,112},{16,96},{32,16},{48,0},{64,48},{80,32},{96,80},{112,64},{1... | collective-permute-start | bytes 393224 | tf_op jit(solution)/shard_map/ppermute | solution.py:37
  (22 other events, 262.4 us)

commit v5 on v4

--- a/solution.py
+++ b/solution.py
@@ -18,7 +18,7 @@
 HALF_BLOCKS = DEST * DEV_BLOCKS
 HOP = (0, 0, 0, 1, 1, 1, 0, 1)
 PLACE = (0, 1, 2, 1, 0, 3, 3, 2)
-UNROLL = 8
+UNROLL = (16, 8, 8)
 TAKEN = 4
 STEPS = 256
 EMPTY = 31 * 512
@@ -57,12 +57,10 @@
         far_right_z = shift_row(jnp.concatenate([from_right, from_z]), -1, 0)
         far_z = shift_row(from_left, 1, 1)
         return near, [far_right_z, left_z, far_z]
-    half = own.shape[0] // 2
+    far_z = shift_row(from_left, 1, 1)
     far = shift_row(from_right, -1, 0)
     right_z = shift_row(from_right, 0, 1)
-    far_z_top = shift_row(from_left[:half], 1, 1)
-    far_z_bottom = shift_row(from_right[half:], -1, 1)
-    return near, [far, right_z, left_z, far_z_top, far_z_bottom]
+    return near, [far, right_z, left_z, far_z]
 
 
 def add(*values):
@@ -82,14 +80,15 @@
     def send(value, dy, dz):
         return shift_col(value.astype(jnp.bfloat16), dy, dz, 0)
 
+    other = send(pair(0, 1), 0, 1)
+    far_down = send(pair(2, 1), -1, 0)
     far_up = send(pair(2, 0), 1, 0)
-    far_down = send(pair(2, 1), -1, 0)
+    other, far_down, far_up = lax.optimization_barrier((other, far_down, far_up))
     direct_up = send(pair(1, 1), 1, 1)
+    relay_down = send(pair(3, 1, far_down), -1, 1)
+    relay_up = send(pair(1, 0, far_up), 1, 0)
     direct_down = send(pair(3, 0), -1, 0)
-    other = send(pair(0, 1), 0, 1)
-    relay_up = send(pair(1, 0, far_up), 1, 0)
-    relay_down = send(pair(3, 1, far_down), -1, 1)
-    return pair(0, 0, relay_up, relay_down, direct_up, direct_down, other)
+    return pair(0, 0, other, direct_up, relay_down, relay_up, direct_down)
 
 
 def params(mib):
@@ -111,12 +110,20 @@
         total[block] = jnp.zeros(total.shape[1:], jnp.float32)
 
 
-def begin_kernel(place_ref, rows_ref, cols_ref, source, vals, total, plan, sem):
+def begin_kernel(place_ref, rows_in, cols_in, source, vals, total, plan, lists, sem, list_sem):
     copy = pltpu.make_async_copy(source, vals, sem)
+    list_copies = [
+        pltpu.make_async_copy(ids, lists.at[at], list_sem.at[at])
+        for at, ids in enumerate((rows_in, cols_in))
+    ]
+    for list_copy in list_copies:
+        list_copy.start()
     copy.start()
+    for list_copy in list_copies:
+        list_copy.wait()
     count, row_at, col_at = place_ref[0], place_ref[1], place_ref[2]
     y, z_hi, core = col_at >> 2, (col_at >> 1) & 1, col_at & 1
-    rows = rows_ref[...]
+    rows = lists[0]
     capacity = rows.shape[1]
     slots = lax.broadcasted_iota(jnp.int32, rows.shape, 1)
     live = slots < count
@@ -125,7 +132,7 @@
     dz = ((dest >> 1) + z_hi) & 1
     keep = 1 - ((dest + core) & 1)
     row = keep * HALF_BLOCKS + (dy * 2 + dz) * DEV_BLOCKS + j
-    hop, col = relative_block(cols_ref[...], row_at)
+    hop, col = relative_block(lists[1], row_at)
     section = jnp.where(hop == 1, 1 + keep, 0)
     key = jnp.where(live, section * (2 * HALF_BLOCKS) + row, 1024).astype(jnp.float32)
     parts = capacity // BLK
@@ -151,9 +158,10 @@
         begin = jnp.where(section == kind, ends, begin)
         mine = jnp.where(opens & (section == kind), 1.0, 0.0)
         number = jnp.sum(mine, axis=1, keepdims=True).astype(jnp.int32)
-        ends = ends + (number + UNROLL - 1) // UNROLL
+        groups = (number + UNROLL[kind] - 1) // UNROLL[kind]
+        ends = ends + groups * UNROLL[kind]
         bounds = jnp.where(lane == kind + 1, ends, bounds)
-    spot = (begin * UNROLL + step) * TAKEN + (within & (TAKEN - 1))
+    spot = (begin + step) * TAKEN + (within & (TAKEN - 1))
     spot = down(jnp.where(live, spot, -1))
     word = down(slots + col * 512 + row * (512 * 32) - EMPTY)
     for side in range(TAKEN):
@@ -179,16 +187,20 @@
             pltpu.VMEM(total_shape, jnp.float32),
             jax.ShapeDtypeStruct((TAKEN + 1, STEPS), jnp.int32),
         ],
-        in_specs=[smem_spec, vmem_spec, vmem_spec, pl.BlockSpec(memory_space=pltpu.HBM)],
+        in_specs=[smem_spec] + [pl.BlockSpec(memory_space=pltpu.HBM)] * 3,
         out_specs=[vmem_spec] * 3,
-        scratch_shapes=[pltpu.SemaphoreType.DMA(())],
+        scratch_shapes=[
+            pltpu.VMEM((2, 1, row_ids.shape[0]), jnp.int32),
+            pltpu.SemaphoreType.DMA(()),
+            pltpu.SemaphoreType.DMA((2,)),
+        ],
         compiler_params=params(16),
         cost_estimate=pl.CostEstimate(flops=0, bytes_accessed=2 * vals.size, transcendentals=0),
         name="begin",
     )(
         place,
-        row_ids[None, :],
-        col_ids[None, :],
+        pltpu.with_memory_space_constraint(row_ids[None, :], pltpu.HBM),
+        pltpu.with_memory_space_constraint(col_ids[None, :], pltpu.HBM),
         pltpu.with_memory_space_constraint(vals, pltpu.HBM),
     )
 
@@ -240,10 +252,10 @@
     for copy in copies:
         copy.wait()
 
-    @pl.loop(plan[TAKEN, section], plan[TAKEN, section + 1])
+    @pl.loop(plan[TAKEN, section], plan[TAKEN, section + 1], step=UNROLL[section])
     def _(group):
-        for u in range(UNROLL):
-            words = [plan[side, group * UNROLL + u] for side in range(TAKEN)]
+        for u in range(UNROLL[section]):
+            words = [plan[side, group + u] for side in range(TAKEN)]
             cols = [jnp.minimum((word >> 9) & 31, zero_block) for word in words]
             left = jnp.concatenate([vals[word & 511] for word in words], axis=1)
             right = jnp.concatenate([panel[col] for col in cols], axis=0)
@@ -311,22 +323,38 @@
     return send, keep
 
 
-def score_kernel(n_pieces, pair_ref, own, target, attributes, w_attr, attr_bias, *refs):
-    pieces = refs[:n_pieces]
-    out_ref, panel, sems = refs[n_pieces:]
-    copies = start_panel(pieces, panel, sems)
-    scale = own.shape[1] ** (-0.5)
-    n_pair = pair_ref.shape[1]
-
-    def row_mean(squares, count):
-        return jnp.sum(squares.T, axis=0, keepdims=True) / count
-
-    errors = []
+def row_mean(squares, count):
+    return jnp.sum(squares.T, axis=0, keepdims=True) / count
+
+
+def attr_kernel(own, attributes, w_attr, attr_bias, out_ref):
     for block in range(DEV_BLOCKS):
         rows = pl.ds(block * BLK, BLK)
         rebuilt = jnp.dot(own[rows, :], w_attr[...], preferred_element_type=jnp.float32)
         gap = rebuilt + attr_bias[...] - attributes[rows, :].astype(jnp.float32)
-        errors.append(jnp.sqrt(row_mean(gap * gap, gap.shape[1]) + epsilon))
+        out_ref[block : block + 1, :] = jnp.sqrt(row_mean(gap * gap, gap.shape[1]) + epsilon)
+
+
+def attr_error(own, attributes, w_attr, attr_bias):
+    return pl.pallas_call(
+        attr_kernel,
+        out_shape=jax.ShapeDtypeStruct((DEV_BLOCKS, BLK), jnp.float32),
+        in_specs=[vmem_spec] * 4,
+        out_specs=vmem_spec,
+        compiler_params=params(16),
+        cost_estimate=pl.CostEstimate(
+            flops=500_000_000, bytes_accessed=1 << 19, transcendentals=0
+        ),
+        name="attr_error",
+    )(own, attributes, w_attr, attr_bias)
+
+
+def score_kernel(n_pieces, pair_ref, own, target, attr, *refs):
+    pieces = refs[:n_pieces]
+    out_ref, panel, sems = refs[n_pieces:]
+    copies = start_panel(pieces, panel, sems)
+    half_scale = 0.5 * own.shape[1] ** (-0.5)
+    n_pair = pair_ref.shape[1]
     for copy in copies:
         copy.wait()
     for block in range(DEV_BLOCKS):
@@ -339,20 +367,20 @@
                 (((1,), (1,)), ((), ())),
                 preferred_element_type=jnp.float32,
             )
-            gap = jax.nn.sigmoid(logits * scale) - target[rows, pl.ds(pair * BLK, BLK)].astype(
-                jnp.float32
-            )
+            goal = target[rows, pl.ds(pair * BLK, BLK)].astype(jnp.float32)
+            gap = 0.5 * jnp.tanh(logits * half_scale) + (0.5 - goal)
             squares = squares + gap * gap
         struct = jnp.sqrt(row_mean(squares, n_pair * BLK) + epsilon)
-        out_ref[block : block + 1, :] = mix_alpha * errors[block] + (1.0 - mix_alpha) * struct
-
-
-def score(hops, pairs, own, target, attributes, w_attr, attr_bias):
+        mixed = mix_alpha * attr[block : block + 1, :] + (1.0 - mix_alpha) * struct
+        out_ref[block : block + 1, :] = mixed
+
+
+def score(hops, pairs, own, target, attr):
     pieces = [piece.reshape(-1, BLK, piece.shape[-1]) for hop in hops for piece in hop]
     out = pl.pallas_call(
         functools.partial(score_kernel, len(pieces)),
         out_shape=jax.ShapeDtypeStruct((DEV_BLOCKS, BLK), jnp.float32),
-        in_specs=[smem_spec] + [vmem_spec] * 5 + [any_spec] * len(pieces),
+        in_specs=[smem_spec] + [vmem_spec] * 3 + [any_spec] * len(pieces),
         out_specs=vmem_spec,
         scratch_shapes=[
             pltpu.VMEM((N_ROW * DEV_BLOCKS, BLK, own.shape[1]), jnp.bfloat16),
@@ -360,7 +388,7 @@
         ],
         compiler_params=params(16),
         name="score",
-    )(pairs, own, target, attributes, w_attr, attr_bias, *pieces)
+    )(pairs, own, target, attr, *pieces)
     return out.reshape(-1)
 
 
@@ -429,9 +457,7 @@
         hop * (N_ROW // 2) * DEV_BLOCKS + place,
         hidden,
         struct_target.reshape(nodes_dev, -1),
-        attributes,
-        w_attr,
-        attr_bias[None, :],
+        attr_error(hidden, attributes, w_attr, attr_bias[None, :]),
     )
 
 

time: 138 us -> 132 us (0.957)
  starting transfers between devices: 57.6 us -> 47.8 us
  waiting for transfers between devices: 47.8 us -> 53.7 us
  local copies, waits for them, and re-layouts: 1.5 us -> 0.11 us
    ppermute x16, starting transfers between devices: 29.7 us -> 24 us  [shift_col(): return lax.ppermute(value, 'col', perm)]
    ppermute x20 -> x19, waiting for transfers between devices: 26 us -> 30.9 us  [shift_row(): return lax.ppermute(value, 'row', perm)]
    ppermute x20 -> x19, starting transfers between devices: 27.9 us -> 23.7 us  [shift_row(): return lax.ppermute(value, 'row', perm)]
  transfers between devices with their start and end apart: 36 -> 35, of which waited for: 16 -> 20; matrix products, arithmetic and copies ran while one was open for 1% -> 1% of each run, Pallas kernels for 14% -> 15%
where the time goes in v5:
time: 132 us
  waiting for transfers between devices  53.7 us (41%)
  starting transfers between devices  47.8 us (36%)
  Pallas kernels  27 us (20%)
  other arithmetic  1.46 us (1%)
    ppermute x19, waiting for transfers between devices, shift_row(): return lax.ppermute(value, 'row', perm)  30.9 us
    ppermute x16, starting transfers between devices, shift_col(): return lax.ppermute(value, 'col', perm)  24 us
    ppermute x19, starting transfers between devices, shift_row(): return lax.ppermute(value, 'row', perm)  23.7 us
    ppermute x16, waiting for transfers between devices, shift_col(): return lax.ppermute(value, 'col', perm)  22.8 us
    pallas_call x6, Pallas kernels, product(): pl.pallas_call(functools.partial(product_kernel, section, len(pieces)), o...  19 us
    pallas_call x1, Pallas kernels, begin(): pl.pallas_call(begin_kernel, out_shape=[pltpu.VMEM(vals.shape, vals.dtype...  5.18 us
  transfers between devices with their start and end apart: 35, of which 20 were waited for; matrix products, arithmetic and copies ran while one was open for 1% of the time, Pallas kernels for 15%

profile of v5, /device:TPU:0, one launch (start us, length us, event | category | flops | bytes accessed | tf_op | source)
XLA Modules:
  0.0 132.2 jit_solution(5852423029935605138)
XLA Ops:
  2.0 2.8 %collective-permute-start = (bf16[512,128]{1,0:T(8,128)(2,1)}, bf16[512,128]{1,0:T(8,128)(2,1)S(1)}, u32[]{:S(2)}, u32[]{:S(2)}) collective-permute-start(bf16[512,128]{1,0:T(8,128)(2,1)} %attributes.1), channel_id=1, source_target_pairs={{0,96},{16,112},{32,0},{48,16},{64,32},{80,48},{96,64},{112,80},{1... | collective-permute-start | bytes 393224 | tf_op jit(solution)/shard_map/ppermute | solution.py:37
  5.5 5.2 %begin.1 = (bf16[384,128,128]{2,1,0:T(8,128)(2,1)S(1)}, f32[64,128,256]{2,1,0:T(8,128)S(1)}, s32[5,256]{1,0:T(8,128)S(1)}) custom-call(s32[3]{0:T(128)S(1)} %pad_add_fusion.place_ref, s32[1,384]{1,0:T(1,128)} %bitcast.140, s32[1,384]{1,0:T(1,128)} %bitcast.141, bf16[384,128,128]{2,1,0:T(8,128)(2,1)} %bitcast.136), custom_call_target="tpu_custom_call" | custom-call | bytes 12582912 | tf_op jit(solution)/shard_map/begin/pallas_call | solution.py:183
  10.7 3.3 %collective-permute-start.2 = (bf16[1024,128]{1,0:T(8,128)(2,1)S(1)}, bf16[1024,128]{1,0:T(8,128)(2,1)S(1)}, u32[]{:S(2)}, u32[]{:S(2)}) collective-permute-start(bf16[1024,128]{1,0:T(8,128)(2,1)S(1)} %pad_maximum_fusion.1), channel_id=1, source_target_pairs={{0,96},{16,112},{32,0},{48,16},{64,32},{80,48},{96,64},{112,80},{1... | collective-permute-start | bytes 786440 | tf_op jit(solution)/shard_map/ppermute | solution.py:37
  14.1 3.8 %product_near.2.refs_3_ = f32[64,128,256]{2,1,0:T(8,128)S(1)} custom-call(s32[5,256]{1,0:T(8,128)S(1)} %get-tuple-element.20.plan, bf16[384,128,128]{2,1,0:T(8,128)(2,1)S(1)} %get-tuple-element.21.vals, bf16[4,128,128]{2,1,0:T(8,128)(2,1)S(1)} %bitcast.123, bf16[4,128,128]{2,1,0:T(8,128)(2,1)S(1)} %bitcast.124, ...), custom_call_target="tpu_custom_call", output_to_operand_aliasing={{}: (6, {})} | custom-call | flops 6000000000 | bytes 1048576 | tf_op jit(solution)/shard_map/product_near/pallas_call | solution.py:306
  17.9 2.9 %collective-permute-done.3 = bf16[512,128]{1,0:T(8,128)(2,1)S(1)} collective-permute-done((bf16[512,128]{1,0:T(8,128)(2,1)S(1)}, bf16[512,128]{1,0:T(8,128)(2,1)S(1)}, u32[]{:S(2)}, u32[]{:S(2)}) %collective-permute-start.3) | collective-permute-done | bytes 131104 | tf_op jit(solution)/shard_map/ppermute | solution.py:37
  21.9 2.9 %product_send.2 = (f32[64,128,256]{2,1,0:T(8,128)S(1)}, bf16[8,528,128]{2,1,0:T(8,128)(2,1)S(1)}) custom-call(s32[5,256]{1,0:T(8,128)S(1)} %get-tuple-element.20.plan, bf16[384,128,128]{2,1,0:T(8,128)(2,1)S(1)} %get-tuple-element.21.vals, bf16[8,128,128]{2,1,0:T(8,128)(2,1)S(1)} %bitcast.110, ...), custom_call_target="tpu_custom_call", output_to_operand_aliasing={{0}: (5, {})} | custom-call | flops 3000000000 | bytes 1048576 | tf_op jit(solution)/shard_map/product_send/pallas_call | solution.py:306
  24.9 2.9 %product_keep.2 = (f32[64,128,256]{2,1,0:T(8,128)S(1)}, bf16[8,528,128]{2,1,0:T(8,128)(2,1)S(1)}) custom-call(s32[5,256]{1,0:T(8,128)S(1)} %get-tuple-element.20.plan, bf16[384,128,128]{2,1,0:T(8,128)(2,1)S(1)} %get-tuple-element.21.vals, bf16[8,128,128]{2,1,0:T(8,128)(2,1)S(1)} %bitcast.111, ...), custom_call_target="tpu_custom_call", output_to_operand_aliasing={{0}: (5, {})} | custom-call | flops 3000000000 | bytes 1048576 | tf_op jit(solution)/shard_map/product_keep/pallas_call | solution.py:306
  28.1 3.0 %collective-permute-start.7 = (bf16[528,128]{1,0:T(8,128)(2,1)S(1)}, bf16[528,128]{1,0:T(8,128)(2,1)S(1)}, u32[]{:S(2)}, u32[]{:S(2)}) collective-permute-start(bf16[528,128]{1,0:T(8,128)(2,1)S(1)} %get-tuple-element.46), channel_id=1, source_target_pairs={{0,2},{1,3},{2,0},{3,1},{4,6},{5,7},{6,4},{7,5},{8,10},{9,11},{10,... | collective-permute-start | bytes 405512 | tf_op jit(solution)/shard_map/ppermute | solution.py:47
  31.0 3.3 %collective-permute-start.8 = (bf16[528,128]{1,0:T(8,128)(2,1)S(1)}, bf16[528,128]{1,0:T(8,128)(2,1)S(1)}, u32[]{:S(2)}, u32[]{:S(2)}) collective-permute-start(bf16[528,128]{1,0:T(8,128)(2,1)S(1)} %get-tuple-element.45), channel_id=1, source_target_pairs={{0,12},{1,13},{2,14},{3,15},{4,0},{5,1},{6,2},{7,3},{8,4},{9,5},{1... | collective-permute-start | bytes 405512 | tf_op jit(solution)/shard_map/ppermute | solution.py:47
  38.1 3.8 %collective-permute-done.9 = bf16[528,128]{1,0:T(8,128)(2,1)S(1)} collective-permute-done((bf16[528,128]{1,0:T(8,128)(2,1)S(1)}, bf16[528,128]{1,0:T(8,128)(2,1)S(1)}, u32[]{:S(2)}, u32[]{:S(2)}) %collective-permute-start.9) | collective-permute-done | bytes 135200 | tf_op jit(solution)/shard_map/ppermute | solution.py:47
  44.6 4.9 %collective-permute-done.11 = bf16[528,128]{1,0:T(8,128)(2,1)S(1)} collective-permute-done((bf16[528,128]{1,0:T(8,128)(2,1)S(1)}, bf16[528,128]{1,0:T(8,128)(2,1)S(1)}, u32[]{:S(2)}, u32[]{:S(2)}) %collective-permute-start.11) | collective-permute-done | bytes 135200 | tf_op jit(solution)/shard_map/ppermute | solution.py:47
  59.3 3.1 %collective-permute-start.16 = (bf16[1024,256]{1,0:T(8,128)(2,1)S(1)}, bf16[1024,256]{1,0:T(8,128)(2,1)S(1)}, u32[]{:S(2)}, u32[]{:S(2)}) collective-permute-start(bf16[1024,256]{1,0:T(8,128)(2,1)S(1)} %pad_maximum_fusion), channel_id=1, source_target_pairs={{0,96},{16,112},{32,0},{48,16},{64,32},{80,48},{96,64},{112,80},{1... | collective-permute-start | bytes 1572872 | tf_op jit(solution)/shard_map/ppermute | solution.py:37
  62.4 3.7 %product_near.3.refs_3_ = f32[64,128,256]{2,1,0:T(8,128)S(1)} custom-call(s32[5,256]{1,0:T(8,128)S(1)} %get-tuple-element.20.plan, bf16[384,128,128]{2,1,0:T(8,128)(2,1)S(1)} %get-tuple-element.21.vals, bf16[4,128,256]{2,1,0:T(8,128)(2,1)S(1)} %bitcast.116, bf16[4,128,256]{2,1,0:T(8,128)(2,1)S(1)} %bitcast.117, ...), custom_call_target="tpu_custom_call", output_to_operand_aliasing={{}: (6, {})} | custom-call | flops 6000000000 | bytes 1048576 | tf_op jit(solution)/shard_map/product_near/pallas_call | solution.py:306
  66.1 6.6 %collective-permute-done.17 = bf16[512,256]{1,0:T(8,128)(2,1)S(1)} collective-permute-done((bf16[512,256]{1,0:T(8,128)(2,1)S(1)}, bf16[512,256]{1,0:T(8,128)(2,1)S(1)}, u32[]{:S(2)}, u32[]{:S(2)}) %collective-permute-start.17) | collective-permute-done | bytes 262176 | tf_op jit(solution)/shard_map/ppermute | solution.py:37
  72.7 3.6 %collective-permute-done.19 = bf16[512,256]{1,0:T(8,128)(2,1)S(1)} collective-permute-done((bf16[512,256]{1,0:T(8,128)(2,1)S(1)}, bf16[512,256]{1,0:T(8,128)(2,1)S(1)}, u32[]{:S(2)}, u32[]{:S(2)}) %collective-permute-start.19) | collective-permute-done | bytes 262176 | tf_op jit(solution)/shard_map/ppermute | solution.py:37
  76.3 2.9 %product_send.3 = (f32[64,128,256]{2,1,0:T(8,128)S(1)}, bf16[8,512,256]{2,1,0:T(8,128)(2,1)S(1)}) custom-call(s32[5,256]{1,0:T(8,128)S(1)} %get-tuple-element.20.plan, bf16[384,128,128]{2,1,0:T(8,128)(2,1)S(1)} %get-tuple-element.21.vals, bf16[8,128,256]{2,1,0:T(8,128)(2,1)S(1)} %bitcast.107, ...), custom_call_target="tpu_custom_call", output_to_operand_aliasing={{0}: (5, {})} | custom-call | flops 3000000000 | bytes 1048576 | tf_op jit(solution)/shard_map/product_send/pallas_call | solution.py:306
  79.3 2.7 %product_keep.3 = (f32[64,128,256]{2,1,0:T(8,128)S(1)}, bf16[8,512,256]{2,1,0:T(8,128)(2,1)S(1)}) custom-call(s32[5,256]{1,0:T(8,128)S(1)} %get-tuple-element.20.plan, bf16[384,128,128]{2,1,0:T(8,128)(2,1)S(1)} %get-tuple-element.21.vals, bf16[8,128,256]{2,1,0:T(8,128)(2,1)S(1)} %bitcast.108, ...), custom_call_target="tpu_custom_call", output_to_operand_aliasing={{0}: (5, {})} | custom-call | flops 3000000000 | bytes 1048576 | tf_op jit(solution)/shard_map/product_keep/pallas_call | solution.py:306
  86.1 2.8 %collective-permute-start.24 = (bf16[512,256]{1,0:T(8,128)(2,1)S(1)}, bf16[512,256]{1,0:T(8,128)(2,1)S(1)}, u32[]{:S(2)}, u32[]{:S(2)}) collective-permute-start(bf16[512,256]{1,0:T(8,128)(2,1)S(1)} %get-tuple-element.35), channel_id=1, source_target_pairs={{0,6},{1,7},{2,4},{3,5},{4,10},{5,11},{6,8},{7,9},{8,14},{9,15},{1... | collective-permute-start | bytes 786440 | tf_op jit(solution)/shard_map/ppermute | solution.py:47
  88.9 3.2 %collective-permute-start.27 = (bf16[512,256]{1,0:T(8,128)(2,1)S(1)}, bf16[512,256]{1,0:T(8,128)(2,1)S(1)}, u32[]{:S(2)}, u32[]{:S(2)}) collective-permute-start(bf16[512,256]{1,0:T(8,128)(2,1)S(1)} %get-tuple-element.36), channel_id=1, source_target_pairs={{0,12},{1,13},{2,14},{3,15},{4,0},{5,1},{6,2},{7,3},{8,4},{9,5},{1... | collective-permute-start | bytes 786440 | tf_op jit(solution)/shard_map/ppermute | solution.py:47
  100.9 4.1 %collective-permute-done.24 = bf16[512,256]{1,0:T(8,128)(2,1)S(1)} collective-permute-done((bf16[512,256]{1,0:T(8,128)(2,1)S(1)}, bf16[512,256]{1,0:T(8,128)(2,1)S(1)}, u32[]{:S(2)}, u32[]{:S(2)}) %collective-permute-start.24) | collective-permute-done | bytes 262176 | tf_op jit(solution)/shard_map/ppermute | solution.py:47
  105.0 3.2 %collective-permute-done.25 = bf16[512,256]{1,0:T(8,128)(2,1)S(1)} collective-permute-done((bf16[512,256]{1,0:T(8,128)(2,1)S(1)}, bf16[512,256]{1,0:T(8,128)(2,1)S(1)}, u32[]{:S(2)}, u32[]{:S(2)}) %collective-permute-start.25) | collective-permute-done | bytes 262176 | tf_op jit(solution)/shard_map/ppermute | solution.py:47
  112.4 2.6 %collective-permute-done.29 = bf16[512,256]{1,0:T(8,128)(2,1)S(1)} collective-permute-done((bf16[512,256]{1,0:T(8,128)(2,1)S(1)}, bf16[512,256]{1,0:T(8,128)(2,1)S(1)}, u32[]{:S(2)}, u32[]{:S(2)}) %collective-permute-start.29) | collective-permute-done | bytes 262176 | tf_op jit(solution)/shard_map/ppermute | solution.py:37
  121.4 3.8 %collective-permute-done.32 = bf16[512,256]{1,0:T(8,128)(2,1)S(1)} collective-permute-done((bf16[512,256]{1,0:T(8,128)(2,1)S(1)}, bf16[512,256]{1,0:T(8,128)(2,1)S(1)}, u32[]{:S(2)}, u32[]{:S(2)}) %collective-permute-start.32) | collective-permute-done | bytes 262176 | tf_op jit(solution)/shard_map/ppermute | solution.py:37
  126.5 3.7 %collective-permute-done.34 = bf16[512,256]{1,0:T(8,128)(2,1)S(1)} collective-permute-done((bf16[512,256]{1,0:T(8,128)(2,1)S(1)}, bf16[512,256]{1,0:T(8,128)(2,1)S(1)}, u32[]{:S(2)}, u32[]{:S(2)}) %collective-permute-start.34) | collective-permute-done | bytes 262176 | tf_op jit(solution)/shard_map/ppermute | solution.py:37
  (89 shorter events, 46.3 us)
Async XLA Ops:
  0.0 10.7 %collective-permute-start.1 = (bf16[512,128]{1,0:T(8,128)(2,1)}, bf16[512,128]{1,0:T(8,128)(2,1)S(1)}, u32[]{:S(2)}, u32[]{:S(2)}) collective-permute-start(bf16[512,128]{1,0:T(8,128)(2,1)} %attributes.1), channel_id=1, source_target_pairs={{0,16},{16,0},{32,48},{48,32},{64,80},{80,64},{96,112},{112,96},{1... | collective-permute-start | bytes 393224 | tf_op jit(solution)/shard_map/ppermute | solution.py:37
  2.0 8.7 %collective-permute-start = (bf16[512,128]{1,0:T(8,128)(2,1)}, bf16[512,128]{1,0:T(8,128)(2,1)S(1)}, u32[]{:S(2)}, u32[]{:S(2)}) collective-permute-start(bf16[512,128]{1,0:T(8,128)(2,1)} %attributes.1), channel_id=1, source_target_pairs={{0,96},{16,112},{32,0},{48,16},{64,32},{80,48},{96,64},{112,80},{1... | collective-permute-start | bytes 393224 | tf_op jit(solution)/shard_map/ppermute | solution.py:37
  4.8 9.3 %collective-permute-start.4 = (bf16[512,128]{1,0:T(8,128)(2,1)}, bf16[512,128]{1,0:T(8,128)(2,1)S(1)}, u32[]{:S(2)}, u32[]{:S(2)}) collective-permute-start(bf16[512,128]{1,0:T(8,128)(2,1)} %attributes.1), channel_id=1, source_target_pairs={{0,32},{16,48},{32,64},{48,80},{64,96},{80,112},{96,0},{112,16},{1... | collective-permute-start | bytes 393224 | tf_op jit(solution)/shard_map/ppermute | solution.py:37
  10.7 11.2 %collective-permute-start.2 = (bf16[1024,128]{1,0:T(8,128)(2,1)S(1)}, bf16[1024,128]{1,0:T(8,128)(2,1)S(1)}, u32[]{:S(2)}, u32[]{:S(2)}) collective-permute-start(bf16[1024,128]{1,0:T(8,128)(2,1)S(1)} %pad_maximum_fusion.1), channel_id=1, source_target_pairs={{0,96},{16,112},{32,0},{48,16},{64,32},{80,48},{96,64},{112,80},{1... | collective-permute-start | bytes 786440 | tf_op jit(solution)/shard_map/ppermute | solution.py:37
  14.0 7.8 %collective-permute-start.5 = (bf16[512,128]{1,0:T(8,128)(2,1)S(1)}, bf16[512,128]{1,0:T(8,128)(2,1)S(1)}, u32[]{:S(2)}, u32[]{:S(2)}) collective-permute-start(bf16[512,128]{1,0:T(8,128)(2,1)S(1)} %collective-permute-done.4), channel_id=1, source_target_pairs={{0,48},{16,32},{32,80},{48,64},{64,112},{80,96},{96,16},{112,0},{1... | collective-permute-start | bytes 393224 | tf_op jit(solution)/shard_map/ppermute | solution.py:37
  28.1 9.5 %collective-permute-start.7 = (bf16[528,128]{1,0:T(8,128)(2,1)S(1)}, bf16[528,128]{1,0:T(8,128)(2,1)S(1)}, u32[]{:S(2)}, u32[]{:S(2)}) collective-permute-start(bf16[528,128]{1,0:T(8,128)(2,1)S(1)} %get-tuple-element.46), channel_id=1, source_target_pairs={{0,2},{1,3},{2,0},{3,1},{4,6},{5,7},{6,4},{7,5},{8,10},{9,11},{10,... | collective-permute-start | bytes 405512 | tf_op jit(solution)/shard_map/ppermute | solution.py:47
  34.3 10.3 %collective-permute-start.10 = (bf16[528,128]{1,0:T(8,128)(2,1)S(1)}, bf16[528,128]{1,0:T(8,128)(2,1)S(1)}, u32[]{:S(2)}, u32[]{:S(2)}) collective-permute-start(bf16[528,128]{1,0:T(8,128)(2,1)S(1)} %get-tuple-element.42), channel_id=1, source_target_pairs={{0,6},{1,7},{2,4},{3,5},{4,10},{5,11},{6,8},{7,9},{8,14},{9,15},{1... | collective-permute-start | bytes 405512 | tf_op jit(solution)/shard_map/ppermute | solution.py:47
  35.9 8.7 %collective-permute-start.13 = (bf16[528,128]{1,0:T(8,128)(2,1)S(1)}, bf16[528,128]{1,0:T(8,128)(2,1)S(1)}, u32[]{:S(2)}, u32[]{:S(2)}) collective-permute-start(bf16[528,128]{1,0:T(8,128)(2,1)S(1)} %get-tuple-element.43), channel_id=1, source_target_pairs={{0,12},{1,13},{2,14},{3,15},{4,0},{5,1},{6,2},{7,3},{8,4},{9,5},{1... | collective-permute-start | bytes 405512 | tf_op jit(solution)/shard_map/ppermute | solution.py:47
  53.6 8.8 %collective-permute-start.18 = (bf16[512,256]{1,0:T(8,128)(2,1)S(1)}, bf16[512,256]{1,0:T(8,128)(2,1)S(1)}, u32[]{:S(2)}, u32[]{:S(2)}) collective-permute-start(bf16[512,256]{1,0:T(8,128)(2,1)S(1)} %convolution_convert_fusion), channel_id=1, source_target_pairs={{0,32},{16,48},{32,64},{48,80},{64,96},{80,112},{96,0},{112,16},{1... | collective-permute-start | bytes 786440 | tf_op jit(solution)/shard_map/ppermute | solution.py:37
  59.3 17.1 %collective-permute-start.16 = (bf16[1024,256]{1,0:T(8,128)(2,1)S(1)}, bf16[1024,256]{1,0:T(8,128)(2,1)S(1)}, u32[]{:S(2)}, u32[]{:S(2)}) collective-permute-start(bf16[1024,256]{1,0:T(8,128)(2,1)S(1)} %pad_maximum_fusion), channel_id=1, source_target_pairs={{0,96},{16,112},{32,0},{48,16},{64,32},{80,48},{96,64},{112,80},{1... | collective-permute-start | bytes 1572872 | tf_op jit(solution)/shard_map/ppermute | solution.py:37
  62.4 10.3 %collective-permute-start.17 = (bf16[512,256]{1,0:T(8,128)(2,1)S(1)}, bf16[512,256]{1,0:T(8,128)(2,1)S(1)}, u32[]{:S(2)}, u32[]{:S(2)}) collective-permute-start(bf16[512,256]{1,0:T(8,128)(2,1)S(1)} %collective-permute-done.15), channel_id=1, source_target_pairs={{0,32},{16,48},{32,64},{48,80},{64,96},{80,112},{96,0},{112,16},{1... | collective-permute-start | bytes 786440 | tf_op jit(solution)/shard_map/ppermute | solution.py:37
  62.4 13.9 %collective-permute-start.19 = (bf16[512,256]{1,0:T(8,128)(2,1)S(1)}, bf16[512,256]{1,0:T(8,128)(2,1)S(1)}, u32[]{:S(2)}, u32[]{:S(2)}) collective-permute-start(bf16[512,256]{1,0:T(8,128)(2,1)S(1)} %collective-permute-done.18), channel_id=1, source_target_pairs={{0,48},{16,32},{32,80},{48,64},{64,112},{80,96},{96,16},{112,0},{1... | collective-permute-start | bytes 786440 | tf_op jit(solution)/shard_map/ppermute | solution.py:37
  83.8 9.9 %collective-permute-start.21 = (bf16[512,256]{1,0:T(8,128)(2,1)S(1)}, bf16[512,256]{1,0:T(8,128)(2,1)S(1)}, u32[]{:S(2)}, u32[]{:S(2)}) collective-permute-start(bf16[512,256]{1,0:T(8,128)(2,1)S(1)} %get-tuple-element.39), channel_id=1, source_target_pairs={{0,2},{1,3},{2,0},{3,1},{4,6},{5,7},{6,4},{7,5},{8,10},{9,11},{10,... | collective-permute-start | bytes 786440 | tf_op jit(solution)/shard_map/ppermute | solution.py:47
  84.1 9.7 %collective-permute-start.22 = (bf16[512,256]{1,0:T(8,128)(2,1)S(1)}, bf16[512,256]{1,0:T(8,128)(2,1)S(1)}, u32[]{:S(2)}, u32[]{:S(2)}) collective-permute-start(bf16[512,256]{1,0:T(8,128)(2,1)S(1)} %get-tuple-element.38), channel_id=1, source_target_pairs={{0,12},{1,13},{2,14},{3,15},{4,0},{5,1},{6,2},{7,3},{8,4},{9,5},{1... | collective-permute-start | bytes 786440 | tf_op jit(solution)/shard_map/ppermute | solution.py:47
  85.9 10.4 %collective-permute-start.23 = (bf16[512,256]{1,0:T(8,128)(2,1)S(1)}, bf16[512,256]{1,0:T(8,128)(2,1)S(1)}, u32[]{:S(2)}, u32[]{:S(2)}) collective-permute-start(bf16[512,256]{1,0:T(8,128)(2,1)S(1)} %get-tuple-element.37), channel_id=1, source_target_pairs={{0,4},{1,5},{2,6},{3,7},{4,8},{5,9},{6,10},{7,11},{8,12},{9,13},{1... | collective-permute-start | bytes 786440 | tf_op jit(solution)/shard_map/ppermute | solution.py:47
  86.1 18.9 %collective-permute-start.24 = (bf16[512,256]{1,0:T(8,128)(2,1)S(1)}, bf16[512,256]{1,0:T(8,128)(2,1)S(1)}, u32[]{:S(2)}, u32[]{:S(2)}) collective-permute-start(bf16[512,256]{1,0:T(8,128)(2,1)S(1)} %get-tuple-element.35), channel_id=1, source_target_pairs={{0,6},{1,7},{2,4},{3,5},{4,10},{5,11},{6,8},{7,9},{8,14},{9,15},{1... | collective-permute-start | bytes 786440 | tf_op jit(solution)/shard_map/ppermute | solution.py:47
  88.9 16.2 %collective-permute-start.27 = (bf16[512,256]{1,0:T(8,128)(2,1)S(1)}, bf16[512,256]{1,0:T(8,128)(2,1)S(1)}, u32[]{:S(2)}, u32[]{:S(2)}) collective-permute-start(bf16[512,256]{1,0:T(8,128)(2,1)S(1)} %get-tuple-element.36), channel_id=1, source_target_pairs={{0,12},{1,13},{2,14},{3,15},{4,0},{5,1},{6,2},{7,3},{8,4},{9,5},{1... | collective-permute-start | bytes 786440 | tf_op jit(solution)/shard_map/ppermute | solution.py:47
  96.5 11.7 %collective-permute-start.25 = (bf16[512,256]{1,0:T(8,128)(2,1)S(1)}, bf16[512,256]{1,0:T(8,128)(2,1)S(1)}, u32[]{:S(2)}, u32[]{:S(2)}) collective-permute-start(bf16[512,256]{1,0:T(8,128)(2,1)S(1)} %get-tuple-element.40), channel_id=1, source_target_pairs={{0,14},{1,15},{2,12},{3,13},{4,2},{5,3},{6,0},{7,1},{8,6},{9,7},{1... | collective-permute-start | bytes 786440 | tf_op jit(solution)/shard_map/ppermute | solution.py:47
  98.6 9.6 %collective-permute-start.26 = (bf16[512,256]{1,0:T(8,128)(2,1)S(1)}, bf16[512,256]{1,0:T(8,128)(2,1)S(1)}, u32[]{:S(2)}, u32[]{:S(2)}) collective-permute-start(bf16[512,256]{1,0:T(8,128)(2,1)S(1)} %get-tuple-element.41), channel_id=1, source_target_pairs={{0,4},{1,5},{2,6},{3,7},{4,8},{5,9},{6,10},{7,11},{8,12},{9,13},{1... | collective-permute-start | bytes 786440 | tf_op jit(solution)/shard_map/ppermute | solution.py:47
  108.6 9.3 %collective-permute-start.28 = (bf16[512,256]{1,0:T(8,128)(2,1)S(1)}, bf16[512,256]{1,0:T(8,128)(2,1)S(1)}, u32[]{:S(2)}, u32[]{:S(2)}) collective-permute-start(bf16[512,256]{1,0:T(8,128)(2,1)S(1)} %fusion.12.own), channel_id=1, source_target_pairs={{0,16},{16,0},{32,48},{48,32},{64,80},{80,64},{96,112},{112,96},{1... | collective-permute-start | bytes 786440 | tf_op jit(solution)/shard_map/ppermute | solution.py:37
  110.4 9.1 %collective-permute-start.30 = (bf16[512,256]{1,0:T(8,128)(2,1)S(1)}, bf16[512,256]{1,0:T(8,128)(2,1)S(1)}, u32[]{:S(2)}, u32[]{:S(2)}) collective-permute-start(bf16[512,256]{1,0:T(8,128)(2,1)S(1)} %fusion.12.own), channel_id=1, source_target_pairs={{0,32},{16,48},{32,64},{48,80},{64,96},{80,112},{96,0},{112,16},{1... | collective-permute-start | bytes 786440 | tf_op jit(solution)/shard_map/ppermute | solution.py:37
  116.6 8.7 %collective-permute-start.32 = (bf16[512,256]{1,0:T(8,128)(2,1)S(1)}, bf16[512,256]{1,0:T(8,128)(2,1)S(1)}, u32[]{:S(2)}, u32[]{:S(2)}) collective-permute-start(bf16[512,256]{1,0:T(8,128)(2,1)S(1)} %collective-permute-done.29), channel_id=1, source_target_pairs={{0,16},{16,0},{32,48},{48,32},{64,80},{80,64},{96,112},{112,96},{1... | collective-permute-start | bytes 786440 | tf_op jit(solution)/shard_map/ppermute | solution.py:37
  117.9 8.5 %collective-permute-start.33 = (bf16[512,256]{1,0:T(8,128)(2,1)S(1)}, bf16[512,256]{1,0:T(8,128)(2,1)S(1)}, u32[]{:S(2)}, u32[]{:S(2)}) collective-permute-start(bf16[512,256]{1,0:T(8,128)(2,1)S(1)} %collective-permute-done.28), channel_id=1, source_target_pairs={{0,32},{16,48},{32,64},{48,80},{64,96},{80,112},{96,0},{112,16},{1... | collective-permute-start | bytes 786440 | tf_op jit(solution)/shard_map/ppermute | solution.py:37
  119.5 10.7 %collective-permute-start.34 = (bf16[512,256]{1,0:T(8,128)(2,1)S(1)}, bf16[512,256]{1,0:T(8,128)(2,1)S(1)}, u32[]{:S(2)}, u32[]{:S(2)}) collective-permute-start(bf16[512,256]{1,0:T(8,128)(2,1)S(1)} %collective-permute-done.30), channel_id=1, source_target_pairs={{0,48},{16,32},{32,80},{48,64},{64,112},{80,96},{96,16},{112,0},{1... | collective-permute-start | bytes 786440 | tf_op jit(solution)/shard_map/ppermute | solution.py:37
  (19 other events, 196.5 us)

commit v6 on v5

--- a/solution.py
+++ b/solution.py
@@ -18,7 +18,7 @@
 HALF_BLOCKS = DEST * DEV_BLOCKS
 HOP = (0, 0, 0, 1, 1, 1, 0, 1)
 PLACE = (0, 1, 2, 1, 0, 3, 3, 2)
-UNROLL = (16, 8, 8)
+UNROLL = 20
 TAKEN = 4
 STEPS = 256
 EMPTY = 31 * 512
@@ -158,8 +158,7 @@
         begin = jnp.where(section == kind, ends, begin)
         mine = jnp.where(opens & (section == kind), 1.0, 0.0)
         number = jnp.sum(mine, axis=1, keepdims=True).astype(jnp.int32)
-        groups = (number + UNROLL[kind] - 1) // UNROLL[kind]
-        ends = ends + groups * UNROLL[kind]
+        ends = ends + (number + UNROLL - 1) // UNROLL * UNROLL
         bounds = jnp.where(lane == kind + 1, ends, bounds)
     spot = (begin + step) * TAKEN + (within & (TAKEN - 1))
     spot = down(jnp.where(live, spot, -1))
@@ -229,32 +228,36 @@
     return copies
 
 
-def product_kernel(section, n_pieces, plan, vals, *refs):
+def product_kernel(section, with_degree, n_pieces, plan, vals, *refs):
     pieces = refs[:n_pieces]
-    refs = refs[n_pieces:]
+    refs = refs[n_pieces + 1 :]
     last = section >= 1
-    total, refs = refs[1], refs[2:]
+    if section == 2:
+        panel, refs = refs[0], refs[1:]
+    total, refs = refs[0], refs[1:]
     if last:
         out_ref, refs = refs[0], refs[1:]
-    panel, sems = refs[:2]
-    width = pieces[0].shape[2]
-    with_degree = panel.shape[2] > width
+        width = out_ref.shape[2]
+    if section < 2:
+        panel, sems, refs = refs[0], refs[1], refs[2:]
+        width = pieces[0].shape[2]
     zero_block = panel.shape[0] - 1
 
-    copies = start_panel(pieces, panel, sems)
-    panel[zero_block] = jnp.zeros(panel.shape[1:], panel.dtype)
-    if with_degree:
-
-        @pl.loop(0, zero_block)
-        def _(block):
-            panel[block, :, width:] = jnp.ones((BLK, panel.shape[2] - width), panel.dtype)
-
-    for copy in copies:
-        copy.wait()
-
-    @pl.loop(plan[TAKEN, section], plan[TAKEN, section + 1], step=UNROLL[section])
+    if section < 2:
+        copies = start_panel(pieces, panel, sems)
+        panel[zero_block] = jnp.zeros(panel.shape[1:], panel.dtype)
+        if with_degree:
+
+            @pl.loop(0, zero_block)
+            def _(block):
+                panel[block, :, width:] = jnp.ones((BLK, panel.shape[2] - width), panel.dtype)
+
+        for copy in copies:
+            copy.wait()
+
+    @pl.loop(plan[TAKEN, section], plan[TAKEN, section + 1], step=UNROLL)
     def _(group):
-        for u in range(UNROLL[section]):
+        for u in range(UNROLL):
             words = [plan[side, group + u] for side in range(TAKEN)]
             cols = [jnp.minimum((word >> 9) & 31, zero_block) for word in words]
             left = jnp.concatenate([vals[word & 511] for word in words], axis=1)
@@ -266,7 +269,7 @@
         return
     base = (section - 1) * HALF_BLOCKS
     if with_degree:
-        degree = refs[2]
+        degree = refs[0]
         degree[...] = jnp.zeros(degree.shape, jnp.float32)
         eye = lax.broadcasted_iota(jnp.int32, (BLK, BLK), 0) == lax.broadcasted_iota(
             jnp.int32, (BLK, BLK), 1
@@ -284,27 +287,36 @@
             out_ref[dest, pl.ds(DEV_BLOCKS * BLK, 16), :] = degree[...].astype(out_ref.dtype)
 
 
-def product(plan, vals, hop, total, section, with_degree):
+def product(plan, vals, hop, total, section, with_degree, panel=None):
     pieces = [piece.reshape(-1, BLK, piece.shape[-1]) for piece in hop]
     blocks = sum(piece.shape[0] for piece in pieces)
     width = pieces[0].shape[2]
     wide = width + (BLK if with_degree else 0)
+    panel_shape = (blocks + 1, BLK, wide)
+    sems = pltpu.SemaphoreType.DMA((len(pieces),))
     out_shape = [pltpu.VMEM(total_shape, jnp.float32)]
-    scratch = [
-        pltpu.VMEM((blocks + 1, BLK, wide), jnp.bfloat16),
-        pltpu.SemaphoreType.DMA((len(pieces),)),
-    ]
-    operands = [plan, vals, *pieces, total]
-    in_specs = [smem_spec, vmem_spec] + [any_spec] * len(pieces) + [vmem_spec]
-    aliases = {len(operands) - 1: 0}
+    scratch = []
     if section >= 1:
         rows = DEV_BLOCKS * BLK + (16 if with_degree else 0)
         out_shape.append(jax.ShapeDtypeStruct((DEST, rows, width), jnp.bfloat16))
-        if with_degree:
-            scratch.append(pltpu.VMEM((16, BLK), jnp.float32))
+    if section == 0:
+        scratch += [pltpu.VMEM(panel_shape, jnp.bfloat16), sems]
+    elif section == 1:
+        out_shape.append(pltpu.VMEM(panel_shape, jnp.bfloat16))
+        scratch.append(sems)
+    else:
+        pieces = []
+    if section >= 1 and with_degree:
+        scratch.append(pltpu.VMEM((16, BLK), jnp.float32))
+    operands = [plan, vals, *pieces, total]
+    aliases = {len(operands) - 1: 0}
+    in_specs = [smem_spec, vmem_spec] + [any_spec] * len(pieces) + [vmem_spec]
+    if section == 2:
+        operands.append(panel)
+        in_specs.append(vmem_spec)
     flops = (6_000_000_000, 3_000_000_000, 3_000_000_000)[section]
     return pl.pallas_call(
-        functools.partial(product_kernel, section, len(pieces)),
+        functools.partial(product_kernel, section, with_degree, len(pieces)),
         out_shape=out_shape,
         in_specs=in_specs,
         out_specs=[vmem_spec] * len(out_shape),
@@ -318,8 +330,8 @@
 
 def layer_product(plan, vals, total, hops, with_degree):
     (total,) = product(plan, vals, hops[0], total, 0, with_degree)
-    total, send = product(plan, vals, hops[1], total, 1, with_degree)
-    total, keep = product(plan, vals, hops[1], total, 2, with_degree)
+    total, send, panel = product(plan, vals, hops[1], total, 1, with_degree)
+    total, keep = product(plan, vals, hops[1], total, 2, with_degree, panel)
     return send, keep
 
 

time: 132 us -> 129 us (0.977)
  starting transfers between devices: 47.8 us -> 44.2 us
    ppermute x19, waiting for transfers between devices: 30.9 us -> 27.1 us  [shift_row(): return lax.ppermute(value, 'row', perm)]
    ppermute x16, waiting for transfers between devices: 22.8 us -> 25.7 us  [shift_col(): return lax.ppermute(value, 'col', perm)]
    ppermute x19, starting transfers between devices: 23.7 us -> 21.9 us  [shift_row(): return lax.ppermute(value, 'row', perm)]
    ppermute x16, starting transfers between devices: 24 us -> 22.3 us  [shift_col(): return lax.ppermute(value, 'col', perm)]
  transfers between devices with their start and end apart: 35 -> 35, of which waited for: 20 -> 22; matrix products, arithmetic and copies ran while one was open for 1% -> 1% of each run, Pallas kernels for 15% -> 15%
where the time goes in v6:
time: 129 us; the launch traced here: 128 us
  waiting for transfers between devices  52.8 us (41%)
  starting transfers between devices  44.2 us (34%)
  Pallas kernels  27.4 us (21%)
  other arithmetic  1.48 us (1%)
    ppermute x19, waiting for transfers between devices, shift_row(): return lax.ppermute(value, 'row', perm)  27.1 us
    ppermute x16, waiting for transfers between devices, shift_col(): return lax.ppermute(value, 'col', perm)  25.7 us
    ppermute x16, starting transfers between devices, shift_col(): return lax.ppermute(value, 'col', perm)  22.3 us
    ppermute x19, starting transfers between devices, shift_row(): return lax.ppermute(value, 'row', perm)  21.9 us
    pallas_call x6, Pallas kernels, product(): pl.pallas_call(functools.partial(product_kernel, section, with_degree, le...  19.4 us
    pallas_call x1, Pallas kernels, begin(): pl.pallas_call(begin_kernel, out_shape=[pltpu.VMEM(vals.shape, vals.dtype...  5.18 us
  transfers between devices with their start and end apart: 35, of which 22 were waited for; matrix products, arithmetic and copies ran while one was open for 1% of the time, Pallas kernels for 15%

profile of v6, /device:TPU:0, one launch (start us, length us, event | category | flops | bytes accessed | tf_op | source)
XLA Modules:
  0.0 128.2 jit_solution(866712018175800723)
XLA Ops:
  2.0 2.8 %collective-permute-start = (bf16[512,128]{1,0:T(8,128)(2,1)}, bf16[512,128]{1,0:T(8,128)(2,1)S(1)}, u32[]{:S(2)}, u32[]{:S(2)}) collective-permute-start(bf16[512,128]{1,0:T(8,128)(2,1)} %attributes.1), channel_id=1, source_target_pairs={{0,96},{16,112},{32,0},{48,16},{64,32},{80,48},{96,64},{112,80},{1... | collective-permute-start | bytes 393224 | tf_op jit(solution)/shard_map/ppermute | solution.py:37
  5.5 5.2 %begin.1 = (bf16[384,128,128]{2,1,0:T(8,128)(2,1)S(1)}, f32[64,128,256]{2,1,0:T(8,128)S(1)}, s32[5,256]{1,0:T(8,128)S(1)}) custom-call(s32[3]{0:T(128)S(1)} %pad_add_fusion.place_ref, s32[1,384]{1,0:T(1,128)} %bitcast.134, s32[1,384]{1,0:T(1,128)} %bitcast.135, bf16[384,128,128]{2,1,0:T(8,128)(2,1)} %bitcast.130), custom_call_target="tpu_custom_call" | custom-call | bytes 12582912 | tf_op jit(solution)/shard_map/begin/pallas_call | solution.py:182
  10.7 3.3 %collective-permute-start.2 = (bf16[1024,128]{1,0:T(8,128)(2,1)S(1)}, bf16[1024,128]{1,0:T(8,128)(2,1)S(1)}, u32[]{:S(2)}, u32[]{:S(2)}) collective-permute-start(bf16[1024,128]{1,0:T(8,128)(2,1)S(1)} %pad_maximum_fusion.1), channel_id=1, source_target_pairs={{0,96},{16,112},{32,0},{48,16},{64,32},{80,48},{96,64},{112,80},{1... | collective-permute-start | bytes 786440 | tf_op jit(solution)/shard_map/ppermute | solution.py:37
  14.1 4.5 %product_near.2.refs_3_ = f32[64,128,256]{2,1,0:T(8,128)S(1)} custom-call(s32[5,256]{1,0:T(8,128)S(1)} %get-tuple-element.22.plan, bf16[384,128,128]{2,1,0:T(8,128)(2,1)S(1)} %get-tuple-element.23.vals, bf16[4,128,128]{2,1,0:T(8,128)(2,1)S(1)} %bitcast.111, bf16[4,128,128]{2,1,0:T(8,128)(2,1)S(1)} %bitcast.112, ...), custom_call_target="tpu_custom_call", output_to_operand_aliasing={{}: (6, {})} | custom-call | flops 6000000000 | bytes 1048576 | tf_op jit(solution)/shard_map/product_near/pallas_call | solution.py:318
  18.5 2.2 %collective-permute-done.3 = bf16[512,128]{1,0:T(8,128)(2,1)S(1)} collective-permute-done((bf16[512,128]{1,0:T(8,128)(2,1)S(1)}, bf16[512,128]{1,0:T(8,128)(2,1)S(1)}, u32[]{:S(2)}, u32[]{:S(2)}) %collective-permute-start.3) | collective-permute-done | bytes 131104 | tf_op jit(solution)/shard_map/ppermute | solution.py:37
  21.9 3.3 %product_send.2 = (f32[64,128,256]{2,1,0:T(8,128)S(1)}, bf16[8,528,128]{2,1,0:T(8,128)(2,1)S(1)}, bf16[17,128,256]{2,1,0:T(8,128)(2,1)S(1)}) custom-call(s32[5,256]{1,0:T(8,128)S(1)} %get-tuple-element.22.plan, bf16[384,128,128]{2,1,0:T(8,128)(2,1)S(1)} %get-tuple-element.23.vals, ...), custom_call_target="tpu_custom_call", output_to_operand_aliasing={{0}: (5, {})} | custom-call | flops 3000000000 | bytes 1048576 | tf_op jit(solution)/shard_map/product_send/pallas_call | solution.py:318
  28.2 4.2 %collective-permute-start.7 = (bf16[528,128]{1,0:T(8,128)(2,1)S(1)}, bf16[528,128]{1,0:T(8,128)(2,1)S(1)}, u32[]{:S(2)}, u32[]{:S(2)}) collective-permute-start(bf16[528,128]{1,0:T(8,128)(2,1)S(1)} %get-tuple-element.50), channel_id=1, source_target_pairs={{0,2},{1,3},{2,0},{3,1},{4,6},{5,7},{6,4},{7,5},{8,10},{9,11},{10,... | collective-permute-start | bytes 405512 | tf_op jit(solution)/shard_map/ppermute | solution.py:47
  32.4 2.6 %collective-permute-start.8 = (bf16[528,128]{1,0:T(8,128)(2,1)S(1)}, bf16[528,128]{1,0:T(8,128)(2,1)S(1)}, u32[]{:S(2)}, u32[]{:S(2)}) collective-permute-start(bf16[528,128]{1,0:T(8,128)(2,1)S(1)} %get-tuple-element.49), channel_id=1, source_target_pairs={{0,12},{1,13},{2,14},{3,15},{4,0},{5,1},{6,2},{7,3},{8,4},{9,5},{1... | collective-permute-start | bytes 405512 | tf_op jit(solution)/shard_map/ppermute | solution.py:47
  35.6 2.7 %collective-permute-start.13 = (bf16[528,128]{1,0:T(8,128)(2,1)S(1)}, bf16[528,128]{1,0:T(8,128)(2,1)S(1)}, u32[]{:S(2)}, u32[]{:S(2)}) collective-permute-start(bf16[528,128]{1,0:T(8,128)(2,1)S(1)} %get-tuple-element.47), channel_id=1, source_target_pairs={{0,12},{1,13},{2,14},{3,15},{4,0},{5,1},{6,2},{7,3},{8,4},{9,5},{1... | collective-permute-start | bytes 405512 | tf_op jit(solution)/shard_map/ppermute | solution.py:47
  38.3 4.5 %collective-permute-done.9 = bf16[528,128]{1,0:T(8,128)(2,1)S(1)} collective-permute-done((bf16[528,128]{1,0:T(8,128)(2,1)S(1)}, bf16[528,128]{1,0:T(8,128)(2,1)S(1)}, u32[]{:S(2)}, u32[]{:S(2)}) %collective-permute-start.9) | collective-permute-done | bytes 135200 | tf_op jit(solution)/shard_map/ppermute | solution.py:47
  44.0 6.4 %collective-permute-done.11 = bf16[528,128]{1,0:T(8,128)(2,1)S(1)} collective-permute-done((bf16[528,128]{1,0:T(8,128)(2,1)S(1)}, bf16[528,128]{1,0:T(8,128)(2,1)S(1)}, u32[]{:S(2)}, u32[]{:S(2)}) %collective-permute-start.11) | collective-permute-done | bytes 135200 | tf_op jit(solution)/shard_map/ppermute | solution.py:47
  51.5 2.2 %collective-permute-start.14 = (bf16[512,256]{1,0:T(8,128)(2,1)S(1)}, bf16[512,256]{1,0:T(8,128)(2,1)S(1)}, u32[]{:S(2)}, u32[]{:S(2)}) collective-permute-start(bf16[512,256]{1,0:T(8,128)(2,1)S(1)} %convolution_convert_fusion), channel_id=1, source_target_pairs={{0,96},{16,112},{32,0},{48,16},{64,32},{80,48},{96,64},{112,80},{1... | collective-permute-start | bytes 786440 | tf_op jit(solution)/shard_map/ppermute | solution.py:37
  54.3 3.5 %collective-permute-done.15 = bf16[512,256]{1,0:T(8,128)(2,1)S(1)} collective-permute-done((bf16[512,256]{1,0:T(8,128)(2,1)S(1)}, bf16[512,256]{1,0:T(8,128)(2,1)S(1)}, u32[]{:S(2)}, u32[]{:S(2)}) %collective-permute-start.15) | collective-permute-done | bytes 262176 | tf_op jit(solution)/shard_map/ppermute | solution.py:37
  58.9 3.0 %collective-permute-start.16 = (bf16[1024,256]{1,0:T(8,128)(2,1)S(1)}, bf16[1024,256]{1,0:T(8,128)(2,1)S(1)}, u32[]{:S(2)}, u32[]{:S(2)}) collective-permute-start(bf16[1024,256]{1,0:T(8,128)(2,1)S(1)} %pad_maximum_fusion), channel_id=1, source_target_pairs={{0,96},{16,112},{32,0},{48,16},{64,32},{80,48},{96,64},{112,80},{1... | collective-permute-start | bytes 1572872 | tf_op jit(solution)/shard_map/ppermute | solution.py:37
  63.9 4.3 %product_near.3.refs_3_ = f32[64,128,256]{2,1,0:T(8,128)S(1)} custom-call(s32[5,256]{1,0:T(8,128)S(1)} %get-tuple-element.22.plan, bf16[384,128,128]{2,1,0:T(8,128)(2,1)S(1)} %get-tuple-element.23.vals, bf16[4,128,256]{2,1,0:T(8,128)(2,1)S(1)} %bitcast.108, bf16[4,128,256]{2,1,0:T(8,128)(2,1)S(1)} %bitcast.109, ...), custom_call_target="tpu_custom_call", output_to_operand_aliasing={{}: (6, {})} | custom-call | flops 6000000000 | bytes 1048576 | tf_op jit(solution)/shard_map/product_near/pallas_call | solution.py:318
  69.7 3.6 %collective-permute-done.19 = bf16[512,256]{1,0:T(8,128)(2,1)S(1)} collective-permute-done((bf16[512,256]{1,0:T(8,128)(2,1)S(1)}, bf16[512,256]{1,0:T(8,128)(2,1)S(1)}, u32[]{:S(2)}, u32[]{:S(2)}) %collective-permute-start.19) | collective-permute-done | bytes 262176 | tf_op jit(solution)/shard_map/ppermute | solution.py:37
  73.3 3.1 %product_send.3 = (f32[64,128,256]{2,1,0:T(8,128)S(1)}, bf16[8,512,256]{2,1,0:T(8,128)(2,1)S(1)}, bf16[17,128,256]{2,1,0:T(8,128)(2,1)S(1)}) custom-call(s32[5,256]{1,0:T(8,128)S(1)} %get-tuple-element.22.plan, bf16[384,128,128]{2,1,0:T(8,128)(2,1)S(1)} %get-tuple-element.23.vals, ...), custom_call_target="tpu_custom_call", output_to_operand_aliasing={{0}: (5, {})} | custom-call | flops 3000000000 | bytes 1048576 | tf_op jit(solution)/shard_map/product_send/pallas_call | solution.py:318
  86.1 3.2 %collective-permute-start.27 = (bf16[512,256]{1,0:T(8,128)(2,1)S(1)}, bf16[512,256]{1,0:T(8,128)(2,1)S(1)}, u32[]{:S(2)}, u32[]{:S(2)}) collective-permute-start(bf16[512,256]{1,0:T(8,128)(2,1)S(1)} %get-tuple-element.40), channel_id=1, source_target_pairs={{0,12},{1,13},{2,14},{3,15},{4,0},{5,1},{6,2},{7,3},{8,4},{9,5},{1... | collective-permute-start | bytes 786440 | tf_op jit(solution)/shard_map/ppermute | solution.py:47
  94.5 2.4 %collective-permute-start.26 = (bf16[512,256]{1,0:T(8,128)(2,1)S(1)}, bf16[512,256]{1,0:T(8,128)(2,1)S(1)}, u32[]{:S(2)}, u32[]{:S(2)}) collective-permute-start(bf16[512,256]{1,0:T(8,128)(2,1)S(1)} %get-tuple-element.45), channel_id=1, source_target_pairs={{0,4},{1,5},{2,6},{3,7},{4,8},{5,9},{6,10},{7,11},{8,12},{9,13},{1... | collective-permute-start | bytes 786440 | tf_op jit(solution)/shard_map/ppermute | solution.py:47
  97.1 3.9 %collective-permute-done.24 = bf16[512,256]{1,0:T(8,128)(2,1)S(1)} collective-permute-done((bf16[512,256]{1,0:T(8,128)(2,1)S(1)}, bf16[512,256]{1,0:T(8,128)(2,1)S(1)}, u32[]{:S(2)}, u32[]{:S(2)}) %collective-permute-start.24) | collective-permute-done | bytes 262176 | tf_op jit(solution)/shard_map/ppermute | solution.py:47
  100.9 3.7 %collective-permute-done.25 = bf16[512,256]{1,0:T(8,128)(2,1)S(1)} collective-permute-done((bf16[512,256]{1,0:T(8,128)(2,1)S(1)}, bf16[512,256]{1,0:T(8,128)(2,1)S(1)}, u32[]{:S(2)}, u32[]{:S(2)}) %collective-permute-start.25) | collective-permute-done | bytes 262176 | tf_op jit(solution)/shard_map/ppermute | solution.py:47
  107.8 3.6 %collective-permute-done.29 = bf16[512,256]{1,0:T(8,128)(2,1)S(1)} collective-permute-done((bf16[512,256]{1,0:T(8,128)(2,1)S(1)}, bf16[512,256]{1,0:T(8,128)(2,1)S(1)}, u32[]{:S(2)}, u32[]{:S(2)}) %collective-permute-start.29) | collective-permute-done | bytes 262176 | tf_op jit(solution)/shard_map/ppermute | solution.py:37
  117.8 4.5 %collective-permute-done.32 = bf16[512,256]{1,0:T(8,128)(2,1)S(1)} collective-permute-done((bf16[512,256]{1,0:T(8,128)(2,1)S(1)}, bf16[512,256]{1,0:T(8,128)(2,1)S(1)}, u32[]{:S(2)}, u32[]{:S(2)}) %collective-permute-start.32) | collective-permute-done | bytes 262176 | tf_op jit(solution)/shard_map/ppermute | solution.py:37
  122.6 3.5 %collective-permute-done.34 = bf16[512,256]{1,0:T(8,128)(2,1)S(1)} collective-permute-done((bf16[512,256]{1,0:T(8,128)(2,1)S(1)}, bf16[512,256]{1,0:T(8,128)(2,1)S(1)}, u32[]{:S(2)}, u32[]{:S(2)}) %collective-permute-start.34) | collective-permute-done | bytes 262176 | tf_op jit(solution)/shard_map/ppermute | solution.py:37
  (89 shorter events, 40.9 us)
Async XLA Ops:
  0.0 10.7 %collective-permute-start.1 = (bf16[512,128]{1,0:T(8,128)(2,1)}, bf16[512,128]{1,0:T(8,128)(2,1)S(1)}, u32[]{:S(2)}, u32[]{:S(2)}) collective-permute-start(bf16[512,128]{1,0:T(8,128)(2,1)} %attributes.1), channel_id=1, source_target_pairs={{0,16},{16,0},{32,48},{48,32},{64,80},{80,64},{96,112},{112,96},{1... | collective-permute-start | bytes 393224 | tf_op jit(solution)/shard_map/ppermute | solution.py:37
  2.0 8.7 %collective-permute-start = (bf16[512,128]{1,0:T(8,128)(2,1)}, bf16[512,128]{1,0:T(8,128)(2,1)S(1)}, u32[]{:S(2)}, u32[]{:S(2)}) collective-permute-start(bf16[512,128]{1,0:T(8,128)(2,1)} %attributes.1), channel_id=1, source_target_pairs={{0,96},{16,112},{32,0},{48,16},{64,32},{80,48},{96,64},{112,80},{1... | collective-permute-start | bytes 393224 | tf_op jit(solution)/shard_map/ppermute | solution.py:37
  4.8 9.3 %collective-permute-start.4 = (bf16[512,128]{1,0:T(8,128)(2,1)}, bf16[512,128]{1,0:T(8,128)(2,1)S(1)}, u32[]{:S(2)}, u32[]{:S(2)}) collective-permute-start(bf16[512,128]{1,0:T(8,128)(2,1)} %attributes.1), channel_id=1, source_target_pairs={{0,32},{16,48},{32,64},{48,80},{64,96},{80,112},{96,0},{112,16},{1... | collective-permute-start | bytes 393224 | tf_op jit(solution)/shard_map/ppermute | solution.py:37
  10.7 11.2 %collective-permute-start.2 = (bf16[1024,128]{1,0:T(8,128)(2,1)S(1)}, bf16[1024,128]{1,0:T(8,128)(2,1)S(1)}, u32[]{:S(2)}, u32[]{:S(2)}) collective-permute-start(bf16[1024,128]{1,0:T(8,128)(2,1)S(1)} %pad_maximum_fusion.1), channel_id=1, source_target_pairs={{0,96},{16,112},{32,0},{48,16},{64,32},{80,48},{96,64},{112,80},{1... | collective-permute-start | bytes 786440 | tf_op jit(solution)/shard_map/ppermute | solution.py:37
  14.0 7.8 %collective-permute-start.5 = (bf16[512,128]{1,0:T(8,128)(2,1)S(1)}, bf16[512,128]{1,0:T(8,128)(2,1)S(1)}, u32[]{:S(2)}, u32[]{:S(2)}) collective-permute-start(bf16[512,128]{1,0:T(8,128)(2,1)S(1)} %collective-permute-done.4), channel_id=1, source_target_pairs={{0,48},{16,32},{32,80},{48,64},{64,112},{80,96},{96,16},{112,0},{1... | collective-permute-start | bytes 393224 | tf_op jit(solution)/shard_map/ppermute | solution.py:37
  28.2 10.0 %collective-permute-start.7 = (bf16[528,128]{1,0:T(8,128)(2,1)S(1)}, bf16[528,128]{1,0:T(8,128)(2,1)S(1)}, u32[]{:S(2)}, u32[]{:S(2)}) collective-permute-start(bf16[528,128]{1,0:T(8,128)(2,1)S(1)} %get-tuple-element.50), channel_id=1, source_target_pairs={{0,2},{1,3},{2,0},{3,1},{4,6},{5,7},{6,4},{7,5},{8,10},{9,11},{10,... | collective-permute-start | bytes 405512 | tf_op jit(solution)/shard_map/ppermute | solution.py:47
  35.0 9.0 %collective-permute-start.10 = (bf16[528,128]{1,0:T(8,128)(2,1)S(1)}, bf16[528,128]{1,0:T(8,128)(2,1)S(1)}, u32[]{:S(2)}, u32[]{:S(2)}) collective-permute-start(bf16[528,128]{1,0:T(8,128)(2,1)S(1)} %get-tuple-element.46), channel_id=1, source_target_pairs={{0,6},{1,7},{2,4},{3,5},{4,10},{5,11},{6,8},{7,9},{8,14},{9,15},{1... | collective-permute-start | bytes 405512 | tf_op jit(solution)/shard_map/ppermute | solution.py:47
  35.6 8.4 %collective-permute-start.13 = (bf16[528,128]{1,0:T(8,128)(2,1)S(1)}, bf16[528,128]{1,0:T(8,128)(2,1)S(1)}, u32[]{:S(2)}, u32[]{:S(2)}) collective-permute-start(bf16[528,128]{1,0:T(8,128)(2,1)S(1)} %get-tuple-element.47), channel_id=1, source_target_pairs={{0,12},{1,13},{2,14},{3,15},{4,0},{5,1},{6,2},{7,3},{8,4},{9,5},{1... | collective-permute-start | bytes 405512 | tf_op jit(solution)/shard_map/ppermute | solution.py:47
  53.7 8.4 %collective-permute-start.18 = (bf16[512,256]{1,0:T(8,128)(2,1)S(1)}, bf16[512,256]{1,0:T(8,128)(2,1)S(1)}, u32[]{:S(2)}, u32[]{:S(2)}) collective-permute-start(bf16[512,256]{1,0:T(8,128)(2,1)S(1)} %convolution_convert_fusion), channel_id=1, source_target_pairs={{0,32},{16,48},{32,64},{48,80},{64,96},{80,112},{96,0},{112,16},{1... | collective-permute-start | bytes 786440 | tf_op jit(solution)/shard_map/ppermute | solution.py:37
  58.9 14.4 %collective-permute-start.16 = (bf16[1024,256]{1,0:T(8,128)(2,1)S(1)}, bf16[1024,256]{1,0:T(8,128)(2,1)S(1)}, u32[]{:S(2)}, u32[]{:S(2)}) collective-permute-start(bf16[1024,256]{1,0:T(8,128)(2,1)S(1)} %pad_maximum_fusion), channel_id=1, source_target_pairs={{0,96},{16,112},{32,0},{48,16},{64,32},{80,48},{96,64},{112,80},{1... | collective-permute-start | bytes 1572872 | tf_op jit(solution)/shard_map/ppermute | solution.py:37
  62.0 7.8 %collective-permute-start.17 = (bf16[512,256]{1,0:T(8,128)(2,1)S(1)}, bf16[512,256]{1,0:T(8,128)(2,1)S(1)}, u32[]{:S(2)}, u32[]{:S(2)}) collective-permute-start(bf16[512,256]{1,0:T(8,128)(2,1)S(1)} %collective-permute-done.15), channel_id=1, source_target_pairs={{0,32},{16,48},{32,64},{48,80},{64,96},{80,112},{96,0},{112,16},{1... | collective-permute-start | bytes 786440 | tf_op jit(solution)/shard_map/ppermute | solution.py:37
  62.1 11.1 %collective-permute-start.19 = (bf16[512,256]{1,0:T(8,128)(2,1)S(1)}, bf16[512,256]{1,0:T(8,128)(2,1)S(1)}, u32[]{:S(2)}, u32[]{:S(2)}) collective-permute-start(bf16[512,256]{1,0:T(8,128)(2,1)S(1)} %collective-permute-done.18), channel_id=1, source_target_pairs={{0,48},{16,32},{32,80},{48,64},{64,112},{80,96},{96,16},{112,0},{1... | collective-permute-start | bytes 786440 | tf_op jit(solution)/shard_map/ppermute | solution.py:37
  81.1 9.9 %collective-permute-start.21 = (bf16[512,256]{1,0:T(8,128)(2,1)S(1)}, bf16[512,256]{1,0:T(8,128)(2,1)S(1)}, u32[]{:S(2)}, u32[]{:S(2)}) collective-permute-start(bf16[512,256]{1,0:T(8,128)(2,1)S(1)} %get-tuple-element.43), channel_id=1, source_target_pairs={{0,2},{1,3},{2,0},{3,1},{4,6},{5,7},{6,4},{7,5},{8,10},{9,11},{10,... | collective-permute-start | bytes 786440 | tf_op jit(solution)/shard_map/ppermute | solution.py:47
  82.6 9.2 %collective-permute-start.22 = (bf16[512,256]{1,0:T(8,128)(2,1)S(1)}, bf16[512,256]{1,0:T(8,128)(2,1)S(1)}, u32[]{:S(2)}, u32[]{:S(2)}) collective-permute-start(bf16[512,256]{1,0:T(8,128)(2,1)S(1)} %get-tuple-element.42), channel_id=1, source_target_pairs={{0,12},{1,13},{2,14},{3,15},{4,0},{5,1},{6,2},{7,3},{8,4},{9,5},{1... | collective-permute-start | bytes 786440 | tf_op jit(solution)/shard_map/ppermute | solution.py:47
  83.1 10.4 %collective-permute-start.23 = (bf16[512,256]{1,0:T(8,128)(2,1)S(1)}, bf16[512,256]{1,0:T(8,128)(2,1)S(1)}, u32[]{:S(2)}, u32[]{:S(2)}) collective-permute-start(bf16[512,256]{1,0:T(8,128)(2,1)S(1)} %get-tuple-element.41), channel_id=1, source_target_pairs={{0,4},{1,5},{2,6},{3,7},{4,8},{5,9},{6,10},{7,11},{8,12},{9,13},{1... | collective-permute-start | bytes 786440 | tf_op jit(solution)/shard_map/ppermute | solution.py:47
  84.7 16.3 %collective-permute-start.24 = (bf16[512,256]{1,0:T(8,128)(2,1)S(1)}, bf16[512,256]{1,0:T(8,128)(2,1)S(1)}, u32[]{:S(2)}, u32[]{:S(2)}) collective-permute-start(bf16[512,256]{1,0:T(8,128)(2,1)S(1)} %get-tuple-element.39), channel_id=1, source_target_pairs={{0,6},{1,7},{2,4},{3,5},{4,10},{5,11},{6,8},{7,9},{8,14},{9,15},{1... | collective-permute-start | bytes 786440 | tf_op jit(solution)/shard_map/ppermute | solution.py:47
  86.1 14.8 %collective-permute-start.27 = (bf16[512,256]{1,0:T(8,128)(2,1)S(1)}, bf16[512,256]{1,0:T(8,128)(2,1)S(1)}, u32[]{:S(2)}, u32[]{:S(2)}) collective-permute-start(bf16[512,256]{1,0:T(8,128)(2,1)S(1)} %get-tuple-element.40), channel_id=1, source_target_pairs={{0,12},{1,13},{2,14},{3,15},{4,0},{5,1},{6,2},{7,3},{8,4},{9,5},{1... | collective-permute-start | bytes 786440 | tf_op jit(solution)/shard_map/ppermute | solution.py:47
  93.7 10.9 %collective-permute-start.25 = (bf16[512,256]{1,0:T(8,128)(2,1)S(1)}, bf16[512,256]{1,0:T(8,128)(2,1)S(1)}, u32[]{:S(2)}, u32[]{:S(2)}) collective-permute-start(bf16[512,256]{1,0:T(8,128)(2,1)S(1)} %get-tuple-element.44), channel_id=1, source_target_pairs={{0,14},{1,15},{2,12},{3,13},{4,2},{5,3},{6,0},{7,1},{8,6},{9,7},{1... | collective-permute-start | bytes 786440 | tf_op jit(solution)/shard_map/ppermute | solution.py:47
  94.5 10.2 %collective-permute-start.26 = (bf16[512,256]{1,0:T(8,128)(2,1)S(1)}, bf16[512,256]{1,0:T(8,128)(2,1)S(1)}, u32[]{:S(2)}, u32[]{:S(2)}) collective-permute-start(bf16[512,256]{1,0:T(8,128)(2,1)S(1)} %get-tuple-element.45), channel_id=1, source_target_pairs={{0,4},{1,5},{2,6},{3,7},{4,8},{5,9},{6,10},{7,11},{8,12},{9,13},{1... | collective-permute-start | bytes 786440 | tf_op jit(solution)/shard_map/ppermute | solution.py:47
  105.6 8.6 %collective-permute-start.28 = (bf16[512,256]{1,0:T(8,128)(2,1)S(1)}, bf16[512,256]{1,0:T(8,128)(2,1)S(1)}, u32[]{:S(2)}, u32[]{:S(2)}) collective-permute-start(bf16[512,256]{1,0:T(8,128)(2,1)S(1)} %fusion.12.own), channel_id=1, source_target_pairs={{0,16},{16,0},{32,48},{48,32},{64,80},{80,64},{96,112},{112,96},{1... | collective-permute-start | bytes 786440 | tf_op jit(solution)/shard_map/ppermute | solution.py:37
  106.6 7.8 %collective-permute-start.30 = (bf16[512,256]{1,0:T(8,128)(2,1)S(1)}, bf16[512,256]{1,0:T(8,128)(2,1)S(1)}, u32[]{:S(2)}, u32[]{:S(2)}) collective-permute-start(bf16[512,256]{1,0:T(8,128)(2,1)S(1)} %fusion.12.own), channel_id=1, source_target_pairs={{0,32},{16,48},{32,64},{48,80},{64,96},{80,112},{96,0},{112,16},{1... | collective-permute-start | bytes 786440 | tf_op jit(solution)/shard_map/ppermute | solution.py:37
  113.1 9.2 %collective-permute-start.32 = (bf16[512,256]{1,0:T(8,128)(2,1)S(1)}, bf16[512,256]{1,0:T(8,128)(2,1)S(1)}, u32[]{:S(2)}, u32[]{:S(2)}) collective-permute-start(bf16[512,256]{1,0:T(8,128)(2,1)S(1)} %collective-permute-done.29), channel_id=1, source_target_pairs={{0,16},{16,0},{32,48},{48,32},{64,80},{80,64},{96,112},{112,96},{1... | collective-permute-start | bytes 786440 | tf_op jit(solution)/shard_map/ppermute | solution.py:37
  114.2 8.4 %collective-permute-start.33 = (bf16[512,256]{1,0:T(8,128)(2,1)S(1)}, bf16[512,256]{1,0:T(8,128)(2,1)S(1)}, u32[]{:S(2)}, u32[]{:S(2)}) collective-permute-start(bf16[512,256]{1,0:T(8,128)(2,1)S(1)} %collective-permute-done.28), channel_id=1, source_target_pairs={{0,32},{16,48},{32,64},{48,80},{64,96},{80,112},{96,0},{112,16},{1... | collective-permute-start | bytes 786440 | tf_op jit(solution)/shard_map/ppermute | solution.py:37
  114.4 11.6 %collective-permute-start.34 = (bf16[512,256]{1,0:T(8,128)(2,1)S(1)}, bf16[512,256]{1,0:T(8,128)(2,1)S(1)}, u32[]{:S(2)}, u32[]{:S(2)}) collective-permute-start(bf16[512,256]{1,0:T(8,128)(2,1)S(1)} %collective-permute-done.30), channel_id=1, source_target_pairs={{0,48},{16,32},{32,80},{48,64},{64,112},{80,96},{96,16},{112,0},{1... | collective-permute-start | bytes 786440 | tf_op jit(solution)/shard_map/ppermute | solution.py:37
  (19 other events, 194.0 us)

commit v7 on v6

--- a/solution.py
+++ b/solution.py
@@ -18,7 +18,7 @@
 HALF_BLOCKS = DEST * DEV_BLOCKS
 HOP = (0, 0, 0, 1, 1, 1, 0, 1)
 PLACE = (0, 1, 2, 1, 0, 3, 3, 2)
-UNROLL = 20
+UNROLL = (26, 20, 20)
 TAKEN = 4
 STEPS = 256
 EMPTY = 31 * 512
@@ -158,7 +158,8 @@
         begin = jnp.where(section == kind, ends, begin)
         mine = jnp.where(opens & (section == kind), 1.0, 0.0)
         number = jnp.sum(mine, axis=1, keepdims=True).astype(jnp.int32)
-        ends = ends + (number + UNROLL - 1) // UNROLL * UNROLL
+        group = UNROLL[kind]
+        ends = ends + (number + group - 1) // group * group
         bounds = jnp.where(lane == kind + 1, ends, bounds)
     spot = (begin + step) * TAKEN + (within & (TAKEN - 1))
     spot = down(jnp.where(live, spot, -1))
@@ -255,9 +256,9 @@
         for copy in copies:
             copy.wait()
 
-    @pl.loop(plan[TAKEN, section], plan[TAKEN, section + 1], step=UNROLL)
+    @pl.loop(plan[TAKEN, section], plan[TAKEN, section + 1], step=UNROLL[section])
     def _(group):
-        for u in range(UNROLL):
+        for u in range(UNROLL[section]):
             words = [plan[side, group + u] for side in range(TAKEN)]
             cols = [jnp.minimum((word >> 9) & 31, zero_block) for word in words]
             left = jnp.concatenate([vals[word & 511] for word in words], axis=1)

time: 129 us -> 128 us (level); the launches traced: 128 us -> 129 us
  starting transfers between devices: 44.2 us -> 46 us
    ppermute x16, starting transfers between devices: 22.3 us -> 23.7 us  [shift_col(): return lax.ppermute(value, 'col', perm)]
  transfers between devices with their start and end apart: 35 -> 35, of which waited for: 22 -> 20; matrix products, arithmetic and copies ran while one was open for 1% -> 1% of each run, Pallas kernels for 15% -> 15%
where the time goes in v7:
time: 128 us; the launch traced here: 129 us
  waiting for transfers between devices  52.6 us (41%)
  starting transfers between devices  46 us (36%)
  Pallas kernels  26.2 us (20%)
  other arithmetic  1.48 us (1%)
    ppermute x19, waiting for transfers between devices, shift_row(): return lax.ppermute(value, 'row', perm)  26.9 us
    ppermute x16, waiting for transfers between devices, shift_col(): return lax.ppermute(value, 'col', perm)  25.7 us
    ppermute x16, starting transfers between devices, shift_col(): return lax.ppermute(value, 'col', perm)  23.7 us
    ppermute x19, starting transfers between devices, shift_row(): return lax.ppermute(value, 'row', perm)  22.2 us
    pallas_call x6, Pallas kernels, product(): pl.pallas_call(functools.partial(product_kernel, section, with_degree, le...  18.2 us
    pallas_call x1, Pallas kernels, begin(): pl.pallas_call(begin_kernel, out_shape=[pltpu.VMEM(vals.shape, vals.dtype...  5.18 us
  transfers between devices with their start and end apart: 35, of which 20 were waited for; matrix products, arithmetic and copies ran while one was open for 1% of the time, Pallas kernels for 15%

profile of v7, /device:TPU:0, one launch (start us, length us, event | category | flops | bytes accessed | tf_op | source)
XLA Modules:
  0.0 128.6 jit_solution(8800347074795721391)
XLA Ops:
  2.0 2.8 %collective-permute-start = (bf16[512,128]{1,0:T(8,128)(2,1)}, bf16[512,128]{1,0:T(8,128)(2,1)S(1)}, u32[]{:S(2)}, u32[]{:S(2)}) collective-permute-start(bf16[512,128]{1,0:T(8,128)(2,1)} %attributes.1), channel_id=1, source_target_pairs={{0,96},{16,112},{32,0},{48,16},{64,32},{80,48},{96,64},{112,80},{1... | collective-permute-start | bytes 393224 | tf_op jit(solution)/shard_map/ppermute | solution.py:37
  5.5 5.2 %begin.1 = (bf16[384,128,128]{2,1,0:T(8,128)(2,1)S(1)}, f32[64,128,256]{2,1,0:T(8,128)S(1)}, s32[5,256]{1,0:T(8,128)S(1)}) custom-call(s32[3]{0:T(128)S(1)} %pad_add_fusion.place_ref, s32[1,384]{1,0:T(1,128)} %bitcast.134, s32[1,384]{1,0:T(1,128)} %bitcast.135, bf16[384,128,128]{2,1,0:T(8,128)(2,1)} %bitcast.130), custom_call_target="tpu_custom_call" | custom-call | bytes 12582912 | tf_op jit(solution)/shard_map/begin/pallas_call | solution.py:183
  10.7 3.3 %collective-permute-start.2 = (bf16[1024,128]{1,0:T(8,128)(2,1)S(1)}, bf16[1024,128]{1,0:T(8,128)(2,1)S(1)}, u32[]{:S(2)}, u32[]{:S(2)}) collective-permute-start(bf16[1024,128]{1,0:T(8,128)(2,1)S(1)} %pad_maximum_fusion.1), channel_id=1, source_target_pairs={{0,96},{16,112},{32,0},{48,16},{64,32},{80,48},{96,64},{112,80},{1... | collective-permute-start | bytes 786440 | tf_op jit(solution)/shard_map/ppermute | solution.py:37
  14.1 3.9 %product_near.2.refs_3_ = f32[64,128,256]{2,1,0:T(8,128)S(1)} custom-call(s32[5,256]{1,0:T(8,128)S(1)} %get-tuple-element.22.plan, bf16[384,128,128]{2,1,0:T(8,128)(2,1)S(1)} %get-tuple-element.23.vals, bf16[4,128,128]{2,1,0:T(8,128)(2,1)S(1)} %bitcast.111, bf16[4,128,128]{2,1,0:T(8,128)(2,1)S(1)} %bitcast.112, ...), custom_call_target="tpu_custom_call", output_to_operand_aliasing={{}: (6, {})} | custom-call | flops 6000000000 | bytes 1048576 | tf_op jit(solution)/shard_map/product_near/pallas_call | solution.py:319
  18.0 2.8 %collective-permute-done.3 = bf16[512,128]{1,0:T(8,128)(2,1)S(1)} collective-permute-done((bf16[512,128]{1,0:T(8,128)(2,1)S(1)}, bf16[512,128]{1,0:T(8,128)(2,1)S(1)}, u32[]{:S(2)}, u32[]{:S(2)}) %collective-permute-start.3) | collective-permute-done | bytes 131104 | tf_op jit(solution)/shard_map/ppermute | solution.py:37
  24.3 3.1 %product_keep.2 = (f32[64,128,256]{2,1,0:T(8,128)S(1)}, bf16[8,528,128]{2,1,0:T(8,128)(2,1)S(1)}) custom-call(s32[5,256]{1,0:T(8,128)S(1)} %get-tuple-element.22.plan, bf16[384,128,128]{2,1,0:T(8,128)(2,1)S(1)} %get-tuple-element.23.vals, f32[64,128,256]{2,1,0:T(8,128)S(1)} %get-tuple-element.25.refs_0_, ...), custom_call_target="tpu_custom_call", output_to_operand_aliasing={{0}: (2, {})} | custom-call | flops 3000000000 | bytes 1048576 | tf_op jit(solution)/shard_map/product_keep/pallas_call | solution.py:319
  27.6 4.8 %collective-permute-start.7 = (bf16[528,128]{1,0:T(8,128)(2,1)S(1)}, bf16[528,128]{1,0:T(8,128)(2,1)S(1)}, u32[]{:S(2)}, u32[]{:S(2)}) collective-permute-start(bf16[528,128]{1,0:T(8,128)(2,1)S(1)} %get-tuple-element.50), channel_id=1, source_target_pairs={{0,2},{1,3},{2,0},{3,1},{4,6},{5,7},{6,4},{7,5},{8,10},{9,11},{10,... | collective-permute-start | bytes 405512 | tf_op jit(solution)/shard_map/ppermute | solution.py:47
  32.4 3.0 %collective-permute-start.8 = (bf16[528,128]{1,0:T(8,128)(2,1)S(1)}, bf16[528,128]{1,0:T(8,128)(2,1)S(1)}, u32[]{:S(2)}, u32[]{:S(2)}) collective-permute-start(bf16[528,128]{1,0:T(8,128)(2,1)S(1)} %get-tuple-element.49), channel_id=1, source_target_pairs={{0,12},{1,13},{2,14},{3,15},{4,0},{5,1},{6,2},{7,3},{8,4},{9,5},{1... | collective-permute-start | bytes 405512 | tf_op jit(solution)/shard_map/ppermute | solution.py:47
  35.6 3.1 %collective-permute-start.13 = (bf16[528,128]{1,0:T(8,128)(2,1)S(1)}, bf16[528,128]{1,0:T(8,128)(2,1)S(1)}, u32[]{:S(2)}, u32[]{:S(2)}) collective-permute-start(bf16[528,128]{1,0:T(8,128)(2,1)S(1)} %get-tuple-element.47), channel_id=1, source_target_pairs={{0,12},{1,13},{2,14},{3,15},{4,0},{5,1},{6,2},{7,3},{8,4},{9,5},{1... | collective-permute-start | bytes 405512 | tf_op jit(solution)/shard_map/ppermute | solution.py:47
  38.8 4.3 %collective-permute-done.9 = bf16[528,128]{1,0:T(8,128)(2,1)S(1)} collective-permute-done((bf16[528,128]{1,0:T(8,128)(2,1)S(1)}, bf16[528,128]{1,0:T(8,128)(2,1)S(1)}, u32[]{:S(2)}, u32[]{:S(2)}) %collective-permute-start.9) | collective-permute-done | bytes 135200 | tf_op jit(solution)/shard_map/ppermute | solution.py:47
  44.8 6.0 %collective-permute-done.11 = bf16[528,128]{1,0:T(8,128)(2,1)S(1)} collective-permute-done((bf16[528,128]{1,0:T(8,128)(2,1)S(1)}, bf16[528,128]{1,0:T(8,128)(2,1)S(1)}, u32[]{:S(2)}, u32[]{:S(2)}) %collective-permute-start.11) | collective-permute-done | bytes 135200 | tf_op jit(solution)/shard_map/ppermute | solution.py:47
  55.0 3.2 %collective-permute-done.15 = bf16[512,256]{1,0:T(8,128)(2,1)S(1)} collective-permute-done((bf16[512,256]{1,0:T(8,128)(2,1)S(1)}, bf16[512,256]{1,0:T(8,128)(2,1)S(1)}, u32[]{:S(2)}, u32[]{:S(2)}) %collective-permute-start.15) | collective-permute-done | bytes 262176 | tf_op jit(solution)/shard_map/ppermute | solution.py:37
  63.9 3.8 %product_near.3.refs_3_ = f32[64,128,256]{2,1,0:T(8,128)S(1)} custom-call(s32[5,256]{1,0:T(8,128)S(1)} %get-tuple-element.22.plan, bf16[384,128,128]{2,1,0:T(8,128)(2,1)S(1)} %get-tuple-element.23.vals, bf16[4,128,256]{2,1,0:T(8,128)(2,1)S(1)} %bitcast.108, bf16[4,128,256]{2,1,0:T(8,128)(2,1)S(1)} %bitcast.109, ...), custom_call_target="tpu_custom_call", output_to_operand_aliasing={{}: (6, {})} | custom-call | flops 6000000000 | bytes 1048576 | tf_op jit(solution)/shard_map/product_near/pallas_call | solution.py:319
  68.8 3.4 %collective-permute-done.19 = bf16[512,256]{1,0:T(8,128)(2,1)S(1)} collective-permute-done((bf16[512,256]{1,0:T(8,128)(2,1)S(1)}, bf16[512,256]{1,0:T(8,128)(2,1)S(1)}, u32[]{:S(2)}, u32[]{:S(2)}) %collective-permute-start.19) | collective-permute-done | bytes 262176 | tf_op jit(solution)/shard_map/ppermute | solution.py:37
  74.4 3.0 %product_keep.3 = (f32[64,128,256]{2,1,0:T(8,128)S(1)}, bf16[8,512,256]{2,1,0:T(8,128)(2,1)S(1)}) custom-call(s32[5,256]{1,0:T(8,128)S(1)} %get-tuple-element.22.plan, bf16[384,128,128]{2,1,0:T(8,128)(2,1)S(1)} %get-tuple-element.23.vals, f32[64,128,256]{2,1,0:T(8,128)S(1)} %get-tuple-element.32.refs_0_, ...), custom_call_target="tpu_custom_call", output_to_operand_aliasing={{0}: (2, {})} | custom-call | flops 3000000000 | bytes 1048576 | tf_op jit(solution)/shard_map/product_keep/pallas_call | solution.py:319
  78.9 3.6 %collective-permute-start.21 = (bf16[512,256]{1,0:T(8,128)(2,1)S(1)}, bf16[512,256]{1,0:T(8,128)(2,1)S(1)}, u32[]{:S(2)}, u32[]{:S(2)}) collective-permute-start(bf16[512,256]{1,0:T(8,128)(2,1)S(1)} %get-tuple-element.43), channel_id=1, source_target_pairs={{0,2},{1,3},{2,0},{3,1},{4,6},{5,7},{6,4},{7,5},{8,10},{9,11},{10,... | collective-permute-start | bytes 786440 | tf_op jit(solution)/shard_map/ppermute | solution.py:47
  84.5 3.0 %collective-permute-start.27 = (bf16[512,256]{1,0:T(8,128)(2,1)S(1)}, bf16[512,256]{1,0:T(8,128)(2,1)S(1)}, u32[]{:S(2)}, u32[]{:S(2)}) collective-permute-start(bf16[512,256]{1,0:T(8,128)(2,1)S(1)} %get-tuple-element.40), channel_id=1, source_target_pairs={{0,12},{1,13},{2,14},{3,15},{4,0},{5,1},{6,2},{7,3},{8,4},{9,5},{1... | collective-permute-start | bytes 786440 | tf_op jit(solution)/shard_map/ppermute | solution.py:47
  89.1 2.6 %collective-permute-done.22 = bf16[512,256]{1,0:T(8,128)(2,1)S(1)} collective-permute-done((bf16[512,256]{1,0:T(8,128)(2,1)S(1)}, bf16[512,256]{1,0:T(8,128)(2,1)S(1)}, u32[]{:S(2)}, u32[]{:S(2)}) %collective-permute-start.22) | collective-permute-done | bytes 262176 | tf_op jit(solution)/shard_map/ppermute | solution.py:47
  94.6 2.5 %collective-permute-start.26 = (bf16[512,256]{1,0:T(8,128)(2,1)S(1)}, bf16[512,256]{1,0:T(8,128)(2,1)S(1)}, u32[]{:S(2)}, u32[]{:S(2)}) collective-permute-start(bf16[512,256]{1,0:T(8,128)(2,1)S(1)} %get-tuple-element.45), channel_id=1, source_target_pairs={{0,4},{1,5},{2,6},{3,7},{4,8},{5,9},{6,10},{7,11},{8,12},{9,13},{1... | collective-permute-start | bytes 786440 | tf_op jit(solution)/shard_map/ppermute | solution.py:47
  97.3 3.6 %collective-permute-done.24 = bf16[512,256]{1,0:T(8,128)(2,1)S(1)} collective-permute-done((bf16[512,256]{1,0:T(8,128)(2,1)S(1)}, bf16[512,256]{1,0:T(8,128)(2,1)S(1)}, u32[]{:S(2)}, u32[]{:S(2)}) %collective-permute-start.24) | collective-permute-done | bytes 262176 | tf_op jit(solution)/shard_map/ppermute | solution.py:47
  101.0 3.6 %collective-permute-done.25 = bf16[512,256]{1,0:T(8,128)(2,1)S(1)} collective-permute-done((bf16[512,256]{1,0:T(8,128)(2,1)S(1)}, bf16[512,256]{1,0:T(8,128)(2,1)S(1)}, u32[]{:S(2)}, u32[]{:S(2)}) %collective-permute-start.25) | collective-permute-done | bytes 262176 | tf_op jit(solution)/shard_map/ppermute | solution.py:47
  108.5 3.4 %collective-permute-done.29 = bf16[512,256]{1,0:T(8,128)(2,1)S(1)} collective-permute-done((bf16[512,256]{1,0:T(8,128)(2,1)S(1)}, bf16[512,256]{1,0:T(8,128)(2,1)S(1)}, u32[]{:S(2)}, u32[]{:S(2)}) %collective-permute-start.29) | collective-permute-done | bytes 262176 | tf_op jit(solution)/shard_map/ppermute | solution.py:37
  118.2 4.8 %collective-permute-done.32 = bf16[512,256]{1,0:T(8,128)(2,1)S(1)} collective-permute-done((bf16[512,256]{1,0:T(8,128)(2,1)S(1)}, bf16[512,256]{1,0:T(8,128)(2,1)S(1)}, u32[]{:S(2)}, u32[]{:S(2)}) %collective-permute-start.32) | collective-permute-done | bytes 262176 | tf_op jit(solution)/shard_map/ppermute | solution.py:37
  123.0 3.5 %collective-permute-done.34 = bf16[512,256]{1,0:T(8,128)(2,1)S(1)} collective-permute-done((bf16[512,256]{1,0:T(8,128)(2,1)S(1)}, bf16[512,256]{1,0:T(8,128)(2,1)S(1)}, u32[]{:S(2)}, u32[]{:S(2)}) %collective-permute-start.34) | collective-permute-done | bytes 262176 | tf_op jit(solution)/shard_map/ppermute | solution.py:37
  (89 shorter events, 41.2 us)
Async XLA Ops:
  0.0 10.7 %collective-permute-start.1 = (bf16[512,128]{1,0:T(8,128)(2,1)}, bf16[512,128]{1,0:T(8,128)(2,1)S(1)}, u32[]{:S(2)}, u32[]{:S(2)}) collective-permute-start(bf16[512,128]{1,0:T(8,128)(2,1)} %attributes.1), channel_id=1, source_target_pairs={{0,16},{16,0},{32,48},{48,32},{64,80},{80,64},{96,112},{112,96},{1... | collective-permute-start | bytes 393224 | tf_op jit(solution)/shard_map/ppermute | solution.py:37
  2.0 8.7 %collective-permute-start = (bf16[512,128]{1,0:T(8,128)(2,1)}, bf16[512,128]{1,0:T(8,128)(2,1)S(1)}, u32[]{:S(2)}, u32[]{:S(2)}) collective-permute-start(bf16[512,128]{1,0:T(8,128)(2,1)} %attributes.1), channel_id=1, source_target_pairs={{0,96},{16,112},{32,0},{48,16},{64,32},{80,48},{96,64},{112,80},{1... | collective-permute-start | bytes 393224 | tf_op jit(solution)/shard_map/ppermute | solution.py:37
  4.8 9.3 %collective-permute-start.4 = (bf16[512,128]{1,0:T(8,128)(2,1)}, bf16[512,128]{1,0:T(8,128)(2,1)S(1)}, u32[]{:S(2)}, u32[]{:S(2)}) collective-permute-start(bf16[512,128]{1,0:T(8,128)(2,1)} %attributes.1), channel_id=1, source_target_pairs={{0,32},{16,48},{32,64},{48,80},{64,96},{80,112},{96,0},{112,16},{1... | collective-permute-start | bytes 393224 | tf_op jit(solution)/shard_map/ppermute | solution.py:37
  10.7 11.2 %collective-permute-start.2 = (bf16[1024,128]{1,0:T(8,128)(2,1)S(1)}, bf16[1024,128]{1,0:T(8,128)(2,1)S(1)}, u32[]{:S(2)}, u32[]{:S(2)}) collective-permute-start(bf16[1024,128]{1,0:T(8,128)(2,1)S(1)} %pad_maximum_fusion.1), channel_id=1, source_target_pairs={{0,96},{16,112},{32,0},{48,16},{64,32},{80,48},{96,64},{112,80},{1... | collective-permute-start | bytes 786440 | tf_op jit(solution)/shard_map/ppermute | solution.py:37
  14.0 7.8 %collective-permute-start.5 = (bf16[512,128]{1,0:T(8,128)(2,1)S(1)}, bf16[512,128]{1,0:T(8,128)(2,1)S(1)}, u32[]{:S(2)}, u32[]{:S(2)}) collective-permute-start(bf16[512,128]{1,0:T(8,128)(2,1)S(1)} %collective-permute-done.4), channel_id=1, source_target_pairs={{0,48},{16,32},{32,80},{48,64},{64,112},{80,96},{96,16},{112,0},{1... | collective-permute-start | bytes 393224 | tf_op jit(solution)/shard_map/ppermute | solution.py:37
  27.6 11.1 %collective-permute-start.7 = (bf16[528,128]{1,0:T(8,128)(2,1)S(1)}, bf16[528,128]{1,0:T(8,128)(2,1)S(1)}, u32[]{:S(2)}, u32[]{:S(2)}) collective-permute-start(bf16[528,128]{1,0:T(8,128)(2,1)S(1)} %get-tuple-element.50), channel_id=1, source_target_pairs={{0,2},{1,3},{2,0},{3,1},{4,6},{5,7},{6,4},{7,5},{8,10},{9,11},{10,... | collective-permute-start | bytes 405512 | tf_op jit(solution)/shard_map/ppermute | solution.py:47
  35.5 9.3 %collective-permute-start.10 = (bf16[528,128]{1,0:T(8,128)(2,1)S(1)}, bf16[528,128]{1,0:T(8,128)(2,1)S(1)}, u32[]{:S(2)}, u32[]{:S(2)}) collective-permute-start(bf16[528,128]{1,0:T(8,128)(2,1)S(1)} %get-tuple-element.46), channel_id=1, source_target_pairs={{0,6},{1,7},{2,4},{3,5},{4,10},{5,11},{6,8},{7,9},{8,14},{9,15},{1... | collective-permute-start | bytes 405512 | tf_op jit(solution)/shard_map/ppermute | solution.py:47
  35.6 9.2 %collective-permute-start.13 = (bf16[528,128]{1,0:T(8,128)(2,1)S(1)}, bf16[528,128]{1,0:T(8,128)(2,1)S(1)}, u32[]{:S(2)}, u32[]{:S(2)}) collective-permute-start(bf16[528,128]{1,0:T(8,128)(2,1)S(1)} %get-tuple-element.47), channel_id=1, source_target_pairs={{0,12},{1,13},{2,14},{3,15},{4,0},{5,1},{6,2},{7,3},{8,4},{9,5},{1... | collective-permute-start | bytes 405512 | tf_op jit(solution)/shard_map/ppermute | solution.py:47
  52.4 9.3 %collective-permute-start.18 = (bf16[512,256]{1,0:T(8,128)(2,1)S(1)}, bf16[512,256]{1,0:T(8,128)(2,1)S(1)}, u32[]{:S(2)}, u32[]{:S(2)}) collective-permute-start(bf16[512,256]{1,0:T(8,128)(2,1)S(1)} %convolution_convert_fusion), channel_id=1, source_target_pairs={{0,32},{16,48},{32,64},{48,80},{64,96},{80,112},{96,0},{112,16},{1... | collective-permute-start | bytes 786440 | tf_op jit(solution)/shard_map/ppermute | solution.py:37
  59.6 12.6 %collective-permute-start.16 = (bf16[1024,256]{1,0:T(8,128)(2,1)S(1)}, bf16[1024,256]{1,0:T(8,128)(2,1)S(1)}, u32[]{:S(2)}, u32[]{:S(2)}) collective-permute-start(bf16[1024,256]{1,0:T(8,128)(2,1)S(1)} %pad_maximum_fusion), channel_id=1, source_target_pairs={{0,96},{16,112},{32,0},{48,16},{64,32},{80,48},{96,64},{112,80},{1... | collective-permute-start | bytes 1572872 | tf_op jit(solution)/shard_map/ppermute | solution.py:37
  61.0 7.8 %collective-permute-start.17 = (bf16[512,256]{1,0:T(8,128)(2,1)S(1)}, bf16[512,256]{1,0:T(8,128)(2,1)S(1)}, u32[]{:S(2)}, u32[]{:S(2)}) collective-permute-start(bf16[512,256]{1,0:T(8,128)(2,1)S(1)} %collective-permute-done.15), channel_id=1, source_target_pairs={{0,32},{16,48},{32,64},{48,80},{64,96},{80,112},{96,0},{112,16},{1... | collective-permute-start | bytes 786440 | tf_op jit(solution)/shard_map/ppermute | solution.py:37
  61.7 10.5 %collective-permute-start.19 = (bf16[512,256]{1,0:T(8,128)(2,1)S(1)}, bf16[512,256]{1,0:T(8,128)(2,1)S(1)}, u32[]{:S(2)}, u32[]{:S(2)}) collective-permute-start(bf16[512,256]{1,0:T(8,128)(2,1)S(1)} %collective-permute-done.18), channel_id=1, source_target_pairs={{0,48},{16,32},{32,80},{48,64},{64,112},{80,96},{96,16},{112,0},{1... | collective-permute-start | bytes 786440 | tf_op jit(solution)/shard_map/ppermute | solution.py:37
  78.9 10.2 %collective-permute-start.21 = (bf16[512,256]{1,0:T(8,128)(2,1)S(1)}, bf16[512,256]{1,0:T(8,128)(2,1)S(1)}, u32[]{:S(2)}, u32[]{:S(2)}) collective-permute-start(bf16[512,256]{1,0:T(8,128)(2,1)S(1)} %get-tuple-element.43), channel_id=1, source_target_pairs={{0,2},{1,3},{2,0},{3,1},{4,6},{5,7},{6,4},{7,5},{8,10},{9,11},{10,... | collective-permute-start | bytes 786440 | tf_op jit(solution)/shard_map/ppermute | solution.py:47
  82.5 9.2 %collective-permute-start.22 = (bf16[512,256]{1,0:T(8,128)(2,1)S(1)}, bf16[512,256]{1,0:T(8,128)(2,1)S(1)}, u32[]{:S(2)}, u32[]{:S(2)}) collective-permute-start(bf16[512,256]{1,0:T(8,128)(2,1)S(1)} %get-tuple-element.42), channel_id=1, source_target_pairs={{0,12},{1,13},{2,14},{3,15},{4,0},{5,1},{6,2},{7,3},{8,4},{9,5},{1... | collective-permute-start | bytes 786440 | tf_op jit(solution)/shard_map/ppermute | solution.py:47
  83.6 10.4 %collective-permute-start.23 = (bf16[512,256]{1,0:T(8,128)(2,1)S(1)}, bf16[512,256]{1,0:T(8,128)(2,1)S(1)}, u32[]{:S(2)}, u32[]{:S(2)}) collective-permute-start(bf16[512,256]{1,0:T(8,128)(2,1)S(1)} %get-tuple-element.41), channel_id=1, source_target_pairs={{0,4},{1,5},{2,6},{3,7},{4,8},{5,9},{6,10},{7,11},{8,12},{9,13},{1... | collective-permute-start | bytes 786440 | tf_op jit(solution)/shard_map/ppermute | solution.py:47
  84.5 16.4 %collective-permute-start.24 = (bf16[512,256]{1,0:T(8,128)(2,1)S(1)}, bf16[512,256]{1,0:T(8,128)(2,1)S(1)}, u32[]{:S(2)}, u32[]{:S(2)}) collective-permute-start(bf16[512,256]{1,0:T(8,128)(2,1)S(1)} %get-tuple-element.39), channel_id=1, source_target_pairs={{0,6},{1,7},{2,4},{3,5},{4,10},{5,11},{6,8},{7,9},{8,14},{9,15},{1... | collective-permute-start | bytes 786440 | tf_op jit(solution)/shard_map/ppermute | solution.py:47
  84.5 16.4 %collective-permute-start.27 = (bf16[512,256]{1,0:T(8,128)(2,1)S(1)}, bf16[512,256]{1,0:T(8,128)(2,1)S(1)}, u32[]{:S(2)}, u32[]{:S(2)}) collective-permute-start(bf16[512,256]{1,0:T(8,128)(2,1)S(1)} %get-tuple-element.40), channel_id=1, source_target_pairs={{0,12},{1,13},{2,14},{3,15},{4,0},{5,1},{6,2},{7,3},{8,4},{9,5},{1... | collective-permute-start | bytes 786440 | tf_op jit(solution)/shard_map/ppermute | solution.py:47
  94.3 10.3 %collective-permute-start.25 = (bf16[512,256]{1,0:T(8,128)(2,1)S(1)}, bf16[512,256]{1,0:T(8,128)(2,1)S(1)}, u32[]{:S(2)}, u32[]{:S(2)}) collective-permute-start(bf16[512,256]{1,0:T(8,128)(2,1)S(1)} %get-tuple-element.44), channel_id=1, source_target_pairs={{0,14},{1,15},{2,12},{3,13},{4,2},{5,3},{6,0},{7,1},{8,6},{9,7},{1... | collective-permute-start | bytes 786440 | tf_op jit(solution)/shard_map/ppermute | solution.py:47
  94.6 9.9 %collective-permute-start.26 = (bf16[512,256]{1,0:T(8,128)(2,1)S(1)}, bf16[512,256]{1,0:T(8,128)(2,1)S(1)}, u32[]{:S(2)}, u32[]{:S(2)}) collective-permute-start(bf16[512,256]{1,0:T(8,128)(2,1)S(1)} %get-tuple-element.45), channel_id=1, source_target_pairs={{0,4},{1,5},{2,6},{3,7},{4,8},{5,9},{6,10},{7,11},{8,12},{9,13},{1... | collective-permute-start | bytes 786440 | tf_op jit(solution)/shard_map/ppermute | solution.py:47
  106.2 7.7 %collective-permute-start.28 = (bf16[512,256]{1,0:T(8,128)(2,1)S(1)}, bf16[512,256]{1,0:T(8,128)(2,1)S(1)}, u32[]{:S(2)}, u32[]{:S(2)}) collective-permute-start(bf16[512,256]{1,0:T(8,128)(2,1)S(1)} %fusion.12.own), channel_id=1, source_target_pairs={{0,16},{16,0},{32,48},{48,32},{64,80},{80,64},{96,112},{112,96},{1... | collective-permute-start | bytes 786440 | tf_op jit(solution)/shard_map/ppermute | solution.py:37
  106.4 9.0 %collective-permute-start.30 = (bf16[512,256]{1,0:T(8,128)(2,1)S(1)}, bf16[512,256]{1,0:T(8,128)(2,1)S(1)}, u32[]{:S(2)}, u32[]{:S(2)}) collective-permute-start(bf16[512,256]{1,0:T(8,128)(2,1)S(1)} %fusion.12.own), channel_id=1, source_target_pairs={{0,32},{16,48},{32,64},{48,80},{64,96},{80,112},{96,0},{112,16},{1... | collective-permute-start | bytes 786440 | tf_op jit(solution)/shard_map/ppermute | solution.py:37
  113.8 9.2 %collective-permute-start.32 = (bf16[512,256]{1,0:T(8,128)(2,1)S(1)}, bf16[512,256]{1,0:T(8,128)(2,1)S(1)}, u32[]{:S(2)}, u32[]{:S(2)}) collective-permute-start(bf16[512,256]{1,0:T(8,128)(2,1)S(1)} %collective-permute-done.29), channel_id=1, source_target_pairs={{0,16},{16,0},{32,48},{48,32},{64,80},{80,64},{96,112},{112,96},{1... | collective-permute-start | bytes 786440 | tf_op jit(solution)/shard_map/ppermute | solution.py:37
  113.9 9.0 %collective-permute-start.33 = (bf16[512,256]{1,0:T(8,128)(2,1)S(1)}, bf16[512,256]{1,0:T(8,128)(2,1)S(1)}, u32[]{:S(2)}, u32[]{:S(2)}) collective-permute-start(bf16[512,256]{1,0:T(8,128)(2,1)S(1)} %collective-permute-done.28), channel_id=1, source_target_pairs={{0,32},{16,48},{32,64},{48,80},{64,96},{80,112},{96,0},{112,16},{1... | collective-permute-start | bytes 786440 | tf_op jit(solution)/shard_map/ppermute | solution.py:37
  115.4 11.1 %collective-permute-start.34 = (bf16[512,256]{1,0:T(8,128)(2,1)S(1)}, bf16[512,256]{1,0:T(8,128)(2,1)S(1)}, u32[]{:S(2)}, u32[]{:S(2)}) collective-permute-start(bf16[512,256]{1,0:T(8,128)(2,1)S(1)} %collective-permute-done.30), channel_id=1, source_target_pairs={{0,48},{16,32},{32,80},{48,64},{64,112},{80,96},{96,16},{112,0},{1... | collective-permute-start | bytes 786440 | tf_op jit(solution)/shard_map/ppermute | solution.py:37
  (19 other events, 198.4 us)
